TPU v7x, 256 devices: a whole 4x4x8 slice. The times are simulated.
256 devices in a mesh: dp: 16 (over y, x), tensor: 16 (over z, core).
Axes of the slice: x: 4, y: 4, z: 8, core: 2. Of those that a mesh axis runs over, the one named last changes fastest.
Arguments:
- inputs: bfloat16 [2048, 7168], P('dp', 'tensor'), may hold values from -6 to 6
- out_grad: bfloat16 [2048, 7168], P('dp', 'tensor'), may hold values from -6 to 6
- w_in: bfloat16 [112, 8, 128, 128], P('tensor'), may hold values from -0.21875 to 0.21875
- w_out: bfloat16 [112, 8, 128, 128], P('tensor'), may hold values from -0.25 to 0.25
- columns: int32 [112, 8], P('tensor'), may hold values from 0 to 55, as said below
- counts: int32 [112], P('tensor'), may hold values from 4 to 8, as said below
Outputs:
- outputs: bfloat16 [2048, 7168], P('dp', 'tensor')
- input_grad: bfloat16 [2048, 7168], P('dp', 'tensor')
- grad_win: float32 [112, 8, 128, 128], P('tensor', None, 'dp')
- grad_wout: float32 [112, 8, 128, 128], P('tensor', None, 'dp')
Inputs may be any that keep to these rules, and one draw needn't show every extreme that they name: Within each hidden block-row the 8 listed block-columns are distinct. `counts`: some hidden block-row has all 8 slots live; slots at or past a row's count are ignored.
All inputs are finite; a program needn't handle non-finite values.
Results may differ from a plain program's by a relative error of at most 0.018.
Values may be sent and summed in bfloat16 or wider, within the bound.
A program may use at most 64 MiB of HBM per device.

v0:
```python
import jax
import jax.numpy as jnp
from jax import lax
from jax.sharding import PartitionSpec as P

BLK = 128


def gelu_tanh(value):
    return jax.nn.gelu(value, approximate=True)


def select_blocks(field, flat, nrows, slots):
    tokens = field.shape[0]
    shaped = field.reshape(tokens, field.shape[1] // BLK, BLK)
    picked = jnp.take(shaped, flat, axis=1)
    return picked.reshape(tokens, nrows, slots, BLK)


def place_blocks(contrib, flat, blocks_wide):
    tokens = contrib.shape[0]
    flat_contrib = contrib.reshape(tokens, -1, BLK)
    placed = jnp.zeros((tokens, blocks_wide, BLK), jnp.float32).at[:, flat].add(flat_contrib)
    return placed.reshape(tokens, -1)


def on_device(inputs, out_grad, w_in, w_out, columns, counts):
    nrows, slots = columns.shape
    flat = columns.reshape(-1)
    live = lax.broadcasted_iota(jnp.int32, (nrows, slots), 1) < counts[:, None]
    live_b = live.astype(jnp.bfloat16)[:, :, None, None]
    live_f = live.astype(jnp.float32)[:, :, None, None]
    w_in_live = w_in * live_b
    w_out_live = w_out * live_b
    gathered = lax.all_gather(inputs, "tensor", axis=1, tiled=True)
    blocks_wide = gathered.shape[1] // BLK
    x_blocks = select_blocks(gathered, flat, nrows, slots)
    pre = jnp.einsum("tnki,nkib->tnb", x_blocks, w_in_live, preferred_element_type=jnp.float32)
    hidden = gelu_tanh(pre).astype(jnp.bfloat16)
    contrib = jnp.einsum("tnb,nkbc->tnkc", hidden, w_out_live, preferred_element_type=jnp.float32)
    partial_out = place_blocks(contrib, flat, blocks_wide)
    outputs = lax.psum_scatter(
        partial_out.astype(jnp.bfloat16), "tensor", scatter_dimension=1, tiled=True
    )
    grads_all = lax.all_gather(out_grad, "tensor", axis=1, tiled=True)
    g_blocks = select_blocks(grads_all, flat, nrows, slots)
    grad_hidden = jnp.einsum(
        "tnkc,nkbc->tnb", g_blocks, w_out_live, preferred_element_type=jnp.float32
    )
    grad_wout = (
        jnp.einsum("tnb,tnkc->nkbc", hidden, g_blocks, preferred_element_type=jnp.float32) * live_f
    )
    grad_pre = jax.vjp(gelu_tanh, pre)[1](grad_hidden)[0].astype(jnp.bfloat16)
    grad_win = (
        jnp.einsum("tnki,tnb->nkib", x_blocks, grad_pre, preferred_element_type=jnp.float32)
        * live_f
    )
    back = jnp.einsum("tnb,nkib->tnki", grad_pre, w_in_live, preferred_element_type=jnp.float32)
    partial_in = place_blocks(back, flat, blocks_wide)
    input_grad = lax.psum_scatter(
        partial_in.astype(jnp.bfloat16), "tensor", scatter_dimension=1, tiled=True
    )
    summed_win, summed_wout = (
        lax.psum_scatter(
            grad_win.astype(jnp.bfloat16), "dp", scatter_dimension=2, tiled=True
        ).astype(jnp.float32),
        lax.psum_scatter(
            grad_wout.astype(jnp.bfloat16), "dp", scatter_dimension=2, tiled=True
        ).astype(jnp.float32),
    )
    return (outputs, input_grad, summed_win, summed_wout)


def solution(mesh):
    return jax.shard_map(
        on_device,
        mesh=mesh,
        in_specs=(
            P("dp", "tensor"),
            P("dp", "tensor"),
            P("tensor", None, None, None),
            P("tensor", None, None, None),
            P("tensor", None),
            P("tensor"),
        ),
        out_specs=(
            P("dp", "tensor"),
            P("dp", "tensor"),
            P("tensor", None, "dp", None),
            P("tensor", None, "dp", None),
        ),
        check_vma=False,
    )
```

profile of v0, /device:TPU:32, one launch (start us, length us, event | category | flops | bytes accessed | tf_op | source)
XLA Modules:
  0.0 407.4 jit_solution(16567690389738569273)
XLA Ops:
  7.2 0.0 all-gather.3.cloned.1.call-start
  7.2 0.7 all-gather.3.cloned.1.call-update
  7.9 0.0 all-gather.5.cloned.1.call-start
  7.9 0.7 all-gather.5.cloned.1.call-update
  8.6 0.0 all-reduce.3.cloned.1.call-start
  8.7 0.8 reshape.106
  9.5 0.7 fusion.33
  10.2 41.2 %all-gather.3.cloned.1.call-done = bf16[128,7168]{0,1:T(8,128)(2,1)} async-done(((bf16[128,448]{0,1:T(8,128)(2,1)}), bf16[128,7168]{0,1:T(8,128)(2,1)}) %all-gather.3.cloned.1.call-update) | async-done | bytes 1835024 | tf_op jit(solution)/shard_map/all_gather | solution.py:35
  51.5 2.4 gather_fusion
  53.9 37.4 %all-gather.5.cloned.1.call-done = bf16[128,7168]{0,1:T(8,128)(2,1)} async-done(((bf16[128,448]{0,1:T(8,128)(2,1)}), bf16[128,7168]{0,1:T(8,128)(2,1)}) %all-gather.5.cloned.1.call-update) | async-done | bytes 1835024 | tf_op jit(solution)/shard_map/all_gather | solution.py:45
  91.3 3.5 gather_fusion.1
  94.9 2.0 broadcast_select_fusion
  96.9 0.8 fusion.12
  97.7 0.4 copy-done.4
  98.1 0.9 copy-done.2
  99.1 0.8 fusion.28
  99.9 1.9 multiply_convert_fusion.1
  101.8 0.0 reduce-scatter.9.cloned.1.call-start
  101.8 2.2 fusion.8
  104.0 2.8 copy.46
  106.8 0.0 reduce-scatter.9.cloned.1.call-update
  106.8 0.0 reduce-scatter.7.cloned.1.call-start
  106.9 0.1 reshape.104
  106.9 1.3 copy-done.1
  108.3 2.5 fusion
  110.8 5.5 %copy.42 = f32[128,56,128]{2,0,1:T(8,128)} copy(f32[128,56,128]{0,2,1:T(8,128)} %bitcast.61) | data formatting | bytes 7340032 | tf_op jit(solution)/shard_map/reshape | solution.py:22
  116.3 2.3 broadcast.63.clone.1
  118.6 13.3 %scatter_fusion.1 = f32[128,56,128]{2,0,1:T(8,128)} fusion(f32[128,56,128]{2,0,1:T(8,128)} %broadcast.63.clone.1, s32[56]{0:T(128)S(1)} %fusion.35, f32[56,128,128]{2,1,0:T(8,128)} %bitcast.59), kind=kCustom, calls=%fused_computation.3 | custom fusion | flops 917504 | bytes 11010272 | tf_op jit(solution)/shard_map/scatter-add | solution.py:23
  131.9 2.3 convert_element_type.52
  134.3 2.9 copy.43
  137.2 0.0 reduce-scatter.7.cloned.1.call-update
  137.2 0.0 reduce-scatter.5.cloned.1.call-start
  137.3 1.4 copy-done.3
  138.7 2.7 fusion.6
  141.4 5.3 %copy.38 = f32[128,56,128]{2,0,1:T(8,128)} copy(f32[128,56,128]{0,2,1:T(8,128)} %bitcast.60) | data formatting | bytes 7340032 | tf_op jit(solution)/shard_map/reshape | solution.py:22
  146.7 2.3 broadcast.63.clone
  149.0 13.3 %scatter_fusion = f32[128,56,128]{2,0,1:T(8,128)} fusion(f32[128,56,128]{2,0,1:T(8,128)} %broadcast.63.clone, s32[56]{0:T(128)S(1)} %fusion.35, f32[56,128,128]{2,1,0:T(8,128)} %bitcast.58), kind=kCustom, calls=%fused_computation.2 | custom fusion | flops 917504 | bytes 11010272 | tf_op jit(solution)/shard_map/scatter-add | solution.py:23
  162.2 2.3 convert_element_type.49
  164.6 2.9 copy.39
  167.5 0.0 reduce-scatter.5.cloned.1.call-update
  167.5 0.6 copy-done.6
  168.2 0.6 dynamic-slice
  169.4 31.1 %all-reduce.3.cloned.1.call-done = bf16[7,8,128,128]{3,2,1,0:T(8,128)(2,1)} async-done(((bf16[7,8,128,128]{3,2,1,0:T(8,128)(2,1)}), bf16[7,8,128,128]{3,2,1,0:T(8,128)(2,1)}) %all-reduce.3.cloned.1.call-update) | async-done | bytes 1835024
  200.5 1.6 dynamic-slice_convert_fusion
  202.1 80.3 %reduce-scatter.9.cloned.1.call-done = bf16[7,8,8,128]{3,1,0,2:T(8,128)(2,1)} async-done(((bf16[7,8,128,128]{3,1,0,2:T(8,128)(2,1)}), bf16[7,8,8,128]{3,1,0,2:T(8,128)(2,1)}) %reduce-scatter.9.cloned.1.call-update) | async-done | bytes 114704 | tf_op jit(solution)/shard_map/reduce_scatter | solution.py:67
  282.4 1.6 copy.47
  284.0 56.2 %reduce-scatter.7.cloned.1.call-done = bf16[128,448]{0,1:T(8,128)(2,1)} async-done(((bf16[128,7168]{0,1:T(8,128)(2,1)}), bf16[128,448]{0,1:T(8,128)(2,1)}) %reduce-scatter.7.cloned.1.call-update) | async-done | bytes 114704 | tf_op jit(solution)/shard_map/reduce_scatter | solution.py:60
  340.3 60.3 %reduce-scatter.5.cloned.1.call-done = bf16[128,448]{0,1:T(8,128)(2,1)} async-done(((bf16[128,7168]{0,1:T(8,128)(2,1)}), bf16[128,448]{0,1:T(8,128)(2,1)}) %reduce-scatter.5.cloned.1.call-update) | async-done | bytes 114704 | tf_op jit(solution)/shard_map/reduce_scatter | solution.py:42
  (14 shorter events, 0.1 us)
Async XLA Ops:
  7.2 44.3 %all-gather.3.cloned.1.call-start = ((), (), s32[]{:S(2)}) async-start(), calls=%async_computation.3 | async-start | bytes 1949696 | tf_op jit(solution)/shard_map/all_gather | solution.py:35
  7.9 83.4 %all-gather.5.cloned.1.call-start = ((), (), s32[]{:S(2)}) async-start(), calls=%async_computation.5 | async-start | bytes 1949696 | tf_op jit(solution)/shard_map/all_gather | solution.py:45
  8.6 191.9 %all-reduce.3.cloned.1.call-start = ((), (), s32[]{:S(2)}) async-start(), calls=%async_computation.8 | async-start | bytes 3670016
  94.9 2.1 copy-start
  96.9 1.2 copy-start.4
  96.9 2.2 copy-start.2
  101.8 180.6 %reduce-scatter.9.cloned.1.call-start = ((), (), s32[]{:S(2)}) async-start(), calls=%async_computation.7 | async-start | bytes 1949696 | tf_op jit(solution)/shard_map/reduce_scatter | solution.py:67
  104.0 2.8 copy-start.5
  106.8 1.5 copy-start.1
  106.8 233.5 %reduce-scatter.7.cloned.1.call-start = ((), (), s32[]{:S(2)}) async-start(), calls=%async_computation.6 | async-start | bytes 1949696 | tf_op jit(solution)/shard_map/reduce_scatter | solution.py:60
  137.2 1.5 copy-start.3
  137.2 263.3 %reduce-scatter.5.cloned.1.call-start = ((), (), s32[]{:S(2)}) async-start(), calls=%async_computation.4 | async-start | bytes 1949696 | tf_op jit(solution)/shard_map/reduce_scatter | solution.py:42
  167.5 0.7 copy-start.6
Sparse Core Ops, SparseCore 0:
  9.8 41.5 all-gather.2
  53.3 37.9 all-gather.4
  101.9 98.5 all-reduce.2
  203.9 78.4 reduce-scatter.8
  285.4 54.8 reduce-scatter.6
  343.4 57.0 reduce-scatter.4
where the time goes:
time: 412 us; the launch traced here: 407 us
  waiting for transfers between devices  308 us (75%)
  local copies, waits for them, and re-layouts  37.7 us (9%)
  other arithmetic  35.7 us (9%)
  between operations  14.9 us (4%)
  matrix products  10.9 us (3%)
    reduce_scatter x1, waiting for transfers between devices, on_device(): lax.psum_scatter(grad_wout.astype(jnp.bfloat16), 'dp', scatter_dimension=...  80.3 us
    reduce_scatter x1, waiting for transfers between devices, on_device(): lax.psum_scatter(partial_out.astype(jnp.bfloat16), 'tensor', scatter_dime...  60.3 us
    reduce_scatter x1, waiting for transfers between devices, on_device(): lax.psum_scatter(partial_in.astype(jnp.bfloat16), 'tensor', scatter_dimen...  56.2 us
    all_gather x1, waiting for transfers between devices, on_device(): gathered = lax.all_gather(inputs, 'tensor', axis=1, tiled=True)  41.2 us
    all_gather x1, waiting for transfers between devices, on_device(): grads_all = lax.all_gather(out_grad, 'tensor', axis=1, tiled=True)  37.4 us
    unnamed x7, waiting for transfers between devices  32.5 us
    scatter-add x2, other arithmetic, place_blocks(): jnp.zeros((tokens, blocks_wide, BLK), jnp.float32).at[:, flat]  26.6 us
    reshape x2, local copies, waits for them, and re-layouts, place_blocks(): flat_contrib = contrib.reshape(tokens, -1, BLK)  10.8 us
  transfers between devices with their start and end apart: 6, of which 6 were waited for; matrix products, arithmetic and copies ran while one was open for 17% of the time, Pallas kernels for 0%

commit v1 on v0

v1 whole, which is shorter than its diff:
```python
import functools

import jax
import jax.numpy as jnp
from jax import lax
from jax.experimental import pallas as pl
from jax.experimental.pallas import tpu as pltpu
from jax.sharding import PartitionSpec as P

BLK = 128
SLOTS = 8
ROWS = 7
NB = ROWS * SLOTS
DB = 56
NZ = 8
NQ = 4
CH = 448
BF = jnp.bfloat16
F32 = jnp.float32
MESH = pl.DeviceIdType.MESH
C0 = 0.7978845608028654
C1 = 0.044715


def cat(parts, axis):
    return jnp.concatenate(parts, axis=axis)


def kernel(
    pick_ref, tab_ref, x_ref, g_ref, win_hbm, wout_hbm,
    out_ref, ing_ref, gwin_ref, gwout_ref,
    xg, gg, xb, gb, win, wout, dgelu, hid, gpre, cbuf, part, sib, rp, rm, wgt, wp, red, w2,
    lsem, ag_s, ag_r, sb_s, sb_r, ss_s, ss_r, zs, zr, xs, xr,
):
    dp = lax.axis_index("dp")
    tn = lax.axis_index("tensor")
    yy, xx = dp // NQ, dp % NQ
    z, core = tn // 2, tn % 2

    def zdev(step):
        return {"dp": dp, "tensor": ((z + step + NZ) % NZ) * 2 + core}

    sdev = {"dp": dp, "tensor": z * 2 + (1 - core)}

    def ydev(step):
        return {"dp": ((yy + step + NQ) % NQ) * NQ + xx, "tensor": tn}

    def xdev(step):
        return {"dp": yy * NQ + (xx + step + NQ) % NQ, "tensor": tn}

    sends = []

    def rcopy(src, dst, ssem, rsem, dev):
        return pltpu.make_async_remote_copy(
            src_ref=src, dst_ref=dst, send_sem=ssem, recv_sem=rsem,
            device_id=dev, device_id_type=MESH,
        )

    def go(copy):
        copy.start()
        sends.append(copy)

    wcopies = [
        pltpu.make_async_copy(win_hbm, win, lsem.at[0]),
        pltpu.make_async_copy(wout_hbm, wout, lsem.at[1]),
    ]
    for c in wcopies:
        c.start()

    barrier = pltpu.get_barrier_semaphore()
    for dev in (sdev, zdev(1), zdev(-1), xdev(1), xdev(-1), ydev(1), ydev(-1)):
        pl.semaphore_signal(barrier, inc=1, device_id=dev, device_id_type=MESH)

    def fold(src, dst):
        base = pl.multiple_of(tn * CH, 64)

        @pl.when(core == 0)
        def _():
            v = src[...]
            for k in range(3):
                dst[pl.ds(base + 128 * k, 128), :] = v[:, 128 * k:128 * k + 128]
            h = v[:, 384:448].astype(F32)
            dst[pl.ds(base + 384, 64), :] = cat([h[:64], h[64:]], 1).astype(BF)

        @pl.when(core == 1)
        def _():
            v = src[...].astype(F32)
            for k in range(3):
                dst[pl.ds(base + 128 * k, 128), :] = v[:, 64 + 128 * k:192 + 128 * k].astype(BF)
            h = v[:, 0:64]
            dst[pl.ds(base + 384, 64), :] = cat([h[64:], h[:64]], 1).astype(BF)

    fields = (xg, gg)
    fold(x_ref, xg)
    fold(g_ref, gg)
    pl.semaphore_wait(barrier, 7)

    def rows(ref, t, lo=0, n=CH):
        return ref.at[pl.ds(pl.multiple_of(t * CH + lo, 32), n), :]

    def zchunk(step):
        return ((z + step + 2 * NZ) % NZ) * 2 + core

    def ag_span(way, k):
        if k < 3:
            return 0, CH
        return (0, CH // 2) if way == 0 else (CH // 2, CH // 2)

    def ag_copy(a, way, k, t):
        lo, n = ag_span(way, k)
        i = (a * 2 + way) * 4 + k
        v = rows(fields[a], t, lo, n)
        return rcopy(v, v, ag_s.at[i], ag_r.at[i], zdev(1 if way == 0 else -1))

    def sb_copy(a, j, t, lo=0, n=CH):
        v = rows(fields[a], t, lo, n)
        return rcopy(v, v, sb_s.at[a * 9 + j], sb_r.at[a * 9 + j], sdev)

    def sb_span(j):
        if j == 0:
            return 0, 0, CH
        way, k = (j - 1) // 4, (j - 1) % 4
        lo, n = ag_span(way, k)
        return (-(k + 1) if way == 0 else k + 1), lo, n

    for a in range(2):
        for way in range(2):
            go(ag_copy(a, way, 0, tn))
    for a in range(2):
        go(sb_copy(a, 0, tn))
    for k in range(4):
        for a in range(2):
            for way in range(2):
                step = -(k + 1) if way == 0 else k + 1
                t = zchunk(step)
                ag_copy(a, way, k, t).wait_recv()
                if k < 3:
                    go(ag_copy(a, way, k + 1, t))
                lo, n = ag_span(way, k)
                go(sb_copy(a, 1 + way * 4 + k, t, lo, n))
                if k == 0 and way == 1 and a == 1:
                    xb[DB] = jnp.zeros((BLK, BLK), BF)
                    gb[DB] = jnp.zeros((BLK, BLK), BF)
                    cbuf[NB] = jnp.zeros((BLK, BLK), F32)
                    for c in wcopies:
                        c.wait()

    lane = lax.broadcasted_iota(jnp.int32, (64, 128), 1)

    def gathered(a):
        for j in range(9):
            step, lo, n = sb_span(j)
            t = ((z + step + 2 * NZ) % NZ) * 2 + (1 - core)
            sb_copy(a, j, t, lo, n).wait_recv()
        ref, out = fields[a], (xb, gb)[a]

        def whole(zz, carry):
            one = pl.multiple_of(zz * 2 * CH, 128)
            two = pl.multiple_of(zz * 2 * CH + CH, 64)
            for k in range(3):
                out[zz * 7 + k] = ref[pl.ds(one + 128 * k, 128), :]
                out[zz * 7 + 4 + k] = ref[pl.ds(two + 128 * k, 128), :]
            h0 = ref[pl.ds(one + 384, 64), :].astype(F32)
            h1 = ref[pl.ds(two + 384, 64), :].astype(F32)
            top = jnp.where(lane < 64, h0, h1)
            low = pltpu.roll(jnp.where(lane < 64, h1, h0), 64, 1)
            out[zz * 7 + 3] = cat([top, low], 0).astype(BF)
            return carry

        lax.fori_loop(0, NZ, whole, 0)

    def listed(ref, n):
        return cat([ref[pick_ref[n * SLOTS + s]] for s in range(SLOTS)], 1)

    def wide(ref, n):
        return cat([ref[n * SLOTS + s] for s in range(SLOTS)], 1)

    def tall(ref, n):
        return ref[pl.ds(n * SLOTS, SLOTS)].reshape(SLOTS * BLK, BLK)

    def keep(n, prod):
        for s in range(SLOTS):
            cbuf[n * SLOTS + s] = prod[:, s * BLK:(s + 1) * BLK]

    gathered(0)

    def forward(n, carry):
        pre = jnp.dot(listed(xb, n), tall(win, n), preferred_element_type=F32)
        sq = pre * pre
        th = jnp.tanh(C0 * pre * (1.0 + C1 * sq))
        half = 0.5 * (1.0 + th)
        dgelu[n] = half + 0.5 * pre * (1.0 - th * th) * (C0 * (1.0 + 3.0 * C1 * sq))
        h = (pre * half).astype(BF)
        hid[n] = h
        keep(n, jnp.dot(h, wide(wout, n), preferred_element_type=F32))
        return carry

    lax.fori_loop(0, ROWS, forward, 0)

    def sib_copy(a, zz):
        return rcopy(
            part.at[a, 1 - core, zz], sib.at[a, zz], ss_s.at[a * NZ + zz], ss_r.at[a * NZ + zz], sdev
        )

    ORDER = (4, 3, -3, 2, -2, 1, -1, 0)

    def place(a):
        for step in ORDER:
            zz = (z + step + NZ) % NZ

            def column(k):
                c = zz * 7 + k
                acc = cbuf[tab_ref[c * ROWS]]
                for n in range(1, ROWS):
                    acc = acc + cbuf[tab_ref[c * ROWS + n]]
                return acc

            for k in range(3):
                part[a, 0, zz, 128 * k:128 * k + 128, :] = column(k).astype(BF)
                part[a, 1, zz, 128 * k:128 * k + 128, :] = column(k + 4).astype(BF)
            mid = column(3)
            top = mid[:64]
            low = pltpu.roll(mid[64:], 64, 1)
            part[a, 0, zz, 384:448, :] = jnp.where(lane < 64, top, low).astype(BF)
            part[a, 1, zz, 384:448, :] = jnp.where(lane < 64, low, top).astype(BF)
            go(sib_copy(a, zz))

    def chip_sum(a, step):
        zz = (z + step + 2 * NZ) % NZ
        sib_copy(a, zz).wait_recv()
        return zz, part[a, core, zz].astype(F32) + sib[a, zz].astype(F32)

    def z_copy(src, a, way, r):
        i = (a * 2 + way) * 4 + r
        dst = (rp if way == 0 else rm).at[a, r]
        return rcopy(src, dst, zs.at[i], zr.at[i], zdev(1 if way == 0 else -1))

    def z_first(a, way):
        r = 3 if a == way else 2
        step = r + 1 if way == 0 else -(r + 1)
        zz, total = chip_sum(a, step)
        part[a, core, zz] = total.astype(BF)
        go(z_copy(part.at[a, core, zz], a, way, r))

    def z_next(a, way, r):
        buf = rp if way == 0 else rm
        z_copy(buf.at[a, r], a, way, r).wait_recv()
        zz, total = chip_sum(a, r if way == 0 else -r)
        buf[a, r] = (buf[a, r].astype(F32) + total).astype(BF)
        go(z_copy(buf.at[a, r], a, way, r - 1))

    def unfold(total, dst):
        @pl.when(core == 0)
        def _():
            for k in range(3):
                dst[:, 128 * k:128 * k + 128] = total[128 * k:128 * k + 128].astype(BF)
            h = total[384:448]
            dst[:, 384:448] = cat([h[:, :64], h[:, 64:]], 0).astype(BF)

        @pl.when(core == 1)
        def _():
            h = total[384:448]
            parts = [cat([h[:, 64:], h[:, :64]], 0)]
            for k in range(3):
                parts.append(total[128 * k:128 * k + 128])
            dst[...] = cat(parts, 1).astype(BF)

    def z_last(a, dst):
        for way in range(2):
            buf = rp if way == 0 else rm
            z_copy(buf.at[a, 0], a, way, 0).wait_recv()
        _, total = chip_sum(a, 0)
        unfold(total + rp[a, 0].astype(F32) + rm[a, 0].astype(F32), dst)

    coords = ((yy, xx), (xx, yy))
    devs = ((ydev, xdev), (xdev, ydev))

    def w_copy(src, a, m):
        i = a * 6 + m
        return rcopy(src, wp.at[a, m], xs.at[i], xr.at[i], devs[a][0](1 if m < 3 else -1))

    def at4(i):
        return (i + 2 * NQ) % NQ

    def w_first(a):
        p = coords[a][0]
        go(w_copy(wgt.at[a, at4(p + 2), pl.ds(0, 2)], a, 0))
        go(w_copy(wgt.at[a, at4(p - 2), pl.ds(2, 2)], a, 3))
        go(w_copy(wgt.at[a, at4(p + 1), pl.ds(2, 2)], a, 1))
        go(w_copy(wgt.at[a, at4(p - 1), pl.ds(0, 2)], a, 4))

    def w_second(a):
        p = coords[a][0]
        w_copy(wp.at[a, 0], a, 0).wait_recv()
        for q in range(2):
            wp[a, 0, q] = (wp[a, 0, q].astype(F32) + wgt[a, at4(p + 1), q].astype(F32)).astype(BF)
        go(w_copy(wp.at[a, 0], a, 2))
        w_copy(wp.at[a, 3], a, 3).wait_recv()
        for q in range(2):
            wp[a, 3, q] = (wp[a, 3, q].astype(F32) + wgt[a, at4(p - 1), 2 + q].astype(F32)).astype(BF)
        go(w_copy(wp.at[a, 3], a, 5))

    def w_third(a):
        p = coords[a][0]
        for m in (1, 4, 2, 5):
            w_copy(wp.at[a, m], a, m).wait_recv()
        for q in range(2):
            red[a, q] = (
                wgt[a, p, q].astype(F32) + wp[a, 2, q].astype(F32) + wp[a, 4, q].astype(F32)
            ).astype(BF)
            red[a, 2 + q] = (
                wgt[a, p, 2 + q].astype(F32) + wp[a, 5, q].astype(F32) + wp[a, 1, q].astype(F32)
            ).astype(BF)

    H = CH // 2

    def v_copy(src, a, m):
        i = 12 + a * 6 + m
        return rcopy(src, w2.at[a, m], xs.at[i], xr.at[i], devs[a][1](1 if m < 3 else -1))

    def v_first(a):
        q = coords[a][1]
        go(v_copy(red.at[a, at4(q + 2), pl.ds(0, H)], a, 0))
        go(v_copy(red.at[a, at4(q - 2), pl.ds(H, H)], a, 3))
        go(v_copy(red.at[a, at4(q + 1), pl.ds(H, H)], a, 1))
        go(v_copy(red.at[a, at4(q - 1), pl.ds(0, H)], a, 4))

    def v_second(a):
        q = coords[a][1]
        v_copy(w2.at[a, 0], a, 0).wait_recv()
        w2[a, 0] = (w2[a, 0].astype(F32) + red[a, at4(q + 1), 0:H].astype(F32)).astype(BF)
        go(v_copy(w2.at[a, 0], a, 2))
        v_copy(w2.at[a, 3], a, 3).wait_recv()
        w2[a, 3] = (w2[a, 3].astype(F32) + red[a, at4(q - 1), H:CH].astype(F32)).astype(BF)
        go(v_copy(w2.at[a, 3], a, 5))

    def v_third(a, dst):
        q = coords[a][1]
        for m in (1, 4, 2, 5):
            v_copy(w2.at[a, m], a, m).wait_recv()
        dst[0:H, :] = red[a, q, 0:H].astype(F32) + w2[a, 2].astype(F32) + w2[a, 4].astype(F32)
        dst[H:CH, :] = red[a, q, H:CH].astype(F32) + w2[a, 5].astype(F32) + w2[a, 1].astype(F32)

    place(0)
    gathered(1)
    z_first(0, 0)
    z_first(0, 1)

    def backward_out(n, carry):
        picked = listed(gb, n)
        gh = lax.dot_general(picked, wide(wout, n), (((1,), (1,)), ((), ())), preferred_element_type=F32)
        gpre[n] = (gh * dgelu[n]).astype(BF)
        gw = lax.dot_general(hid[n], picked, (((0,), (0,)), ((), ())), preferred_element_type=F32)
        for s in range(0, SLOTS, 2):
            one = gw[:, s * BLK:(s + 1) * BLK].reshape(16, 8, BLK)
            two = gw[:, (s + 1) * BLK:(s + 2) * BLK].reshape(16, 8, BLK)
            row = pl.multiple_of((n * SLOTS + s) * 8, 16)
            wgt[0, :, :, pl.ds(row, 16), :] = cat([one, two], 1).astype(BF).reshape(4, 4, 16, BLK)
        return carry

    lax.fori_loop(0, ROWS, backward_out, 0)
    w_first(0)

    def backward_in(n, carry):
        picked = listed(xb, n)
        gw = lax.dot_general(picked, gpre[n], (((0,), (0,)), ((), ())), preferred_element_type=F32)
        gw = gw.reshape(SLOTS, 16, 8, BLK)
        for s in range(0, SLOTS, 2):
            both = cat([gw[s], gw[s + 1]], 1).astype(BF).reshape(4, 4, 16, BLK)
            row = pl.multiple_of((n * SLOTS + s) * 8, 16)
            for p in range(4):
                for q in range(4):
                    wgt[1, p, q, pl.ds(row, 16), :] = both[q, p]
        return carry

    lax.fori_loop(0, ROWS, backward_in, 0)
    w_first(1)
    z_next(0, 0, 3)
    z_next(0, 1, 2)

    def backward_x(n, carry):
        keep(n, lax.dot_general(gpre[n], tall(win, n), (((1,), (1,)), ((), ())), preferred_element_type=F32))
        return carry

    lax.fori_loop(0, ROWS, backward_x, 0)
    place(1)
    z_next(0, 0, 2)
    z_next(0, 1, 1)
    z_first(1, 0)
    z_first(1, 1)
    z_next(0, 0, 1)
    w_second(0)
    z_next(1, 0, 2)
    z_next(1, 1, 3)
    w_second(1)
    z_next(1, 0, 1)
    z_next(1, 1, 2)
    z_last(0, out_ref)
    z_next(1, 1, 1)
    w_third(0)
    v_first(0)
    w_third(1)
    v_first(1)
    v_second(0)
    v_second(1)
    z_last(1, ing_ref)
    v_third(0, gwout_ref)
    v_third(1, gwin_ref)
    for c in sends:
        c.wait_send()


def on_device(inputs, out_grad, w_in, w_out, columns, counts):
    nrows, slots = columns.shape
    live = lax.broadcasted_iota(jnp.int32, (nrows, slots), 1) < counts[:, None]
    pick = jnp.where(live, columns, DB).reshape(-1)
    slot = lax.broadcasted_iota(jnp.int32, (nrows, slots), 0) * slots + lax.broadcasted_iota(
        jnp.int32, (nrows, slots), 1
    )
    same = (jnp.where(live, columns, -1)[None] == jnp.arange(DB, dtype=jnp.int32)[:, None, None])
    tab = jnp.min(jnp.where(same, slot[None], NB), axis=2).reshape(-1)

    vm = pl.BlockSpec(memory_space=pltpu.VMEM)
    sm = pl.BlockSpec(memory_space=pltpu.SMEM)
    anyw = pl.BlockSpec(memory_space=pl.ANY)
    dma = pltpu.SemaphoreType.DMA
    out, ing, gwin, gwout = pl.pallas_call(
        kernel,
        out_shape=(
            jax.ShapeDtypeStruct((128, CH), BF),
            jax.ShapeDtypeStruct((128, CH), BF),
            jax.ShapeDtypeStruct((CH, BLK), F32),
            jax.ShapeDtypeStruct((CH, BLK), F32),
        ),
        in_specs=[sm, sm, vm, vm, anyw, anyw],
        out_specs=(vm, vm, vm, vm),
        scratch_shapes=[
            pltpu.VMEM((16 * CH, BLK), BF),
            pltpu.VMEM((16 * CH, BLK), BF),
            pltpu.VMEM((DB + 1, BLK, BLK), BF),
            pltpu.VMEM((DB + 1, BLK, BLK), BF),
            pltpu.VMEM((NB, BLK, BLK), BF),
            pltpu.VMEM((NB, BLK, BLK), BF),
            pltpu.VMEM((ROWS, 128, BLK), F32),
            pltpu.VMEM((ROWS, 128, BLK), BF),
            pltpu.VMEM((ROWS, 128, BLK), BF),
            pltpu.VMEM((NB + 1, 128, BLK), F32),
            pltpu.VMEM((2, 2, NZ, CH, BLK), BF),
            pltpu.VMEM((2, NZ, CH, BLK), BF),
            pltpu.VMEM((2, 4, CH, BLK), BF),
            pltpu.VMEM((2, 4, CH, BLK), BF),
            pltpu.VMEM((2, 4, 4, CH, BLK), BF),
            pltpu.VMEM((2, 6, 2, CH, BLK), BF),
            pltpu.VMEM((2, 4, CH, BLK), BF),
            pltpu.VMEM((2, 6, CH // 2, BLK), BF),
            dma((2,)),
            dma((16,)), dma((16,)),
            dma((18,)), dma((18,)),
            dma((16,)), dma((16,)),
            dma((16,)), dma((16,)),
            dma((24,)), dma((24,)),
        ],
        compiler_params=pltpu.CompilerParams(
            collective_id=0, has_side_effects=True, vmem_limit_bytes=50 * 1024 * 1024
        ),
        cost_estimate=pl.CostEstimate(flops=1_409_286_144, bytes_accessed=8_000_000, transcendentals=114_688),
    )(pick, tab, inputs, out_grad, w_in.reshape(NB, BLK, BLK), w_out.reshape(NB, BLK, BLK))
    return (out, ing, gwin.reshape(ROWS, SLOTS, 8, BLK), gwout.reshape(ROWS, SLOTS, 8, BLK))


def solution(mesh):
    return jax.shard_map(
        on_device,
        mesh=mesh,
        in_specs=(
            P("dp", "tensor"),
            P("dp", "tensor"),
            P("tensor", None, None, None),
            P("tensor", None, None, None),
            P("tensor", None),
            P("tensor"),
        ),
        out_specs=(
            P("dp", "tensor"),
            P("dp", "tensor"),
            P("tensor", None, "dp", None),
            P("tensor", None, "dp", None),
        ),
        check_vma=False,
    )
```

time: 412 us -> 78.6 us (0.19); the launches traced: 407 us -> 78.4 us
  waiting for transfers between devices: 308 us -> 0 us
  Pallas kernels: 0 us -> 70.2 us
  other arithmetic: 35.7 us -> 0.86 us
  local copies, waits for them, and re-layouts: 37.7 us -> 6.71 us
  between operations: 14.9 us -> 0.68 us
  matrix products: 10.9 us -> 0 us
    reduce_scatter x3 -> x0, waiting for transfers between devices: 197 us -> none  [the longest x1 80.3 us: on_device(): lax.psum_scatter(grad_wout.astype(jnp.bfloat16), 'dp', scatter_dimension=...]
    all_gather x2 -> x0, waiting for transfers between devices: 78.7 us -> none  [the longest x1 41.2 us: on_device(): gathered = lax.all_gather(inputs, 'tensor', axis=1, tiled=True)]
    pallas_call x0 -> x1, Pallas kernels: none -> 70.2 us  [on_device(): pl.pallas_call(kernel, out_shape=(jax.ShapeDtypeStruct((128, CH), BF), ja...]
    unnamed x7 -> x0, waiting for transfers between devices: 32.5 us -> none
    scatter-add x2 -> x0, other arithmetic: 26.6 us -> none  [place_blocks(): jnp.zeros((tokens, blocks_wide, BLK), jnp.float32).at[:, flat]]
    reshape x4 -> x2, local copies, waits for them, and re-layouts: 11.6 us -> 0.21 us  [the longest x1 0.13 us: on_device(): tab = jnp.min(jnp.where(same, slot[None], NB), axis=2).reshape(-1)]
    dot_general x6 -> x0, matrix products: 10.9 us -> none  [the longest x1 2.72 us: on_device(): jnp.einsum('tnb,nkbc->tnkc', hidden, w_out_live, preferred_element_type=j...]
    convert_element_type x3 -> x0, local copies, waits for them, and re-layouts: 8.6 us -> none  [the longest x1 2.94 us: on_device(): partial_in.astype(jnp.bfloat16)]
  transfers between devices with their start and end apart: 6 -> 0, of which waited for: 6 -> 0; matrix products, arithmetic and copies ran while one was open for 17% -> 0% of each run, Pallas kernels for 0% -> 0%
where the time goes in v1:
time: 78.6 us; the launch traced here: 78.4 us
  Pallas kernels  70.2 us (89%)
  local copies, waits for them, and re-layouts  6.71 us (9%)
  other arithmetic  0.86 us (1%)
    pallas_call x1, Pallas kernels, on_device(): pl.pallas_call(kernel, out_shape=(jax.ShapeDtypeStruct((128, CH), BF), ja...  70.2 us
    unnamed x8, local copies, waits for them, and re-layouts  6.41 us

profile of v1, /device:TPU:32, one launch (start us, length us, event | category | flops | bytes accessed | tf_op | source)
XLA Modules:
  0.0 78.4 jit_solution(1404601399168939739)
XLA Ops:
  0.6 0.8 fusion
  1.4 0.1 select_reduce_fusion
  1.5 0.1 reshape.41.pick_ref
  1.6 0.1 copy.18
  1.7 0.1 reshape.42.tab_ref
  1.8 1.0 %copy.19.x_ref = bf16[128,448]{1,0:T(8,128)(2,1)S(1)} copy(bf16[128,448]{0,1:T(8,128)(2,1)} %param.6) | data formatting | bytes 229376 | tf_op args[0]
  2.8 1.0 %copy.20.g_ref = bf16[128,448]{1,0:T(8,128)(2,1)S(1)} copy(bf16[128,448]{0,1:T(8,128)(2,1)} %param.7) | data formatting | bytes 229376 | tf_op args[1]
  3.8 0.0 copy-start
  3.8 1.5 %copy-done = bf16[7,8,128,128]{3,2,1,0:T(8,128)(2,1)S(1)} copy-done((bf16[7,8,128,128]{3,2,1,0:T(8,128)(2,1)S(1)}, bf16[7,8,128,128]{3,2,1,0:T(8,128)(2,1)}, u32[]{:S(2)}) %copy-start) | copy-done | bytes 1835032
  5.3 70.2 %shard_map.93 = (bf16[128,448]{1,0:T(8,128)(2,1)S(1)}, bf16[128,448]{1,0:T(8,128)(2,1)S(1)}, f32[448,128]{1,0:T(8,128)S(1)}, f32[448,128]{1,0:T(8,128)S(1)}) custom-call(s32[56]{0:T(128)S(1)} %reshape.41.pick_ref, s32[392]{0:T(512)S(1)} %reshape.42.tab_ref, bf16[128,448]{1,0:T(8,128)(2,1)S(1)} %copy.19.x_ref, bf16[128,448]{1,0:T(8,128)(2,1)S(1)} %copy.20.g_ref, ...), custom_call_target="tpu_custom_call" | custom-call | flops 1409286144 | bytes 8000000 | tf_op jit(solution)/shard_map/pallas_call | solution.py:427
  75.5 0.8 copy.21
  76.3 0.8 copy.22
  77.0 0.7 copy.25
  77.7 0.7 copy.26
  (1 shorter events, 0.0 us)
Async XLA Ops:
  3.8 1.5 %copy-start = (bf16[7,8,128,128]{3,2,1,0:T(8,128)(2,1)S(1)}, bf16[7,8,128,128]{3,2,1,0:T(8,128)(2,1)}, u32[]{:S(2)}) copy-start(bf16[7,8,128,128]{3,2,1,0:T(8,128)(2,1)} %param.8) | copy-start | bytes 5505028

commit v2 on v0

v2 whole, which is shorter than its diff:
```python
import jax
import jax.numpy as jnp
from jax import lax
from jax.experimental import pallas as pl
from jax.experimental.pallas import tpu as pltpu
from jax.sharding import PartitionSpec as P

BLK = 128
SLOTS = 8
ROWS = 7
NB = ROWS * SLOTS
DB = 56
NZ = 8
NQ = 4
CH = 448
U = 7
SPAN = ((0, 4), (4, 3))
BF = jnp.bfloat16
F32 = jnp.float32
MESH = pl.DeviceIdType.MESH
C0 = 0.7978845608028654
C1 = 0.044715
ORDER = (4, 3, -3, 2, -2, 1, -1, 0)
NT = (((1,), (1,)), ((), ()))


def cat(parts, axis):
    return jnp.concatenate(parts, axis=axis)


def dot(a, b):
    return jnp.dot(a, b, preferred_element_type=F32)


def kernel(
    col_ref, cnt_ref, x_hbm, g_hbm, win_hbm, wout_hbm,
    out_ref, ing_ref, gwin_ref, gwout_ref,
    xg, gg, win, wout, wint, woutt, dgelu, hid, gpre, cbuf, part, sib, rp, rm,
    wgt, wpa, wpb, red, w2a, w2b, tabv, tab,
    lsem, ag_s, ag_r, sb_s, sb_r, ss_s, ss_r, zs, zr, xs, xr,
):
    dp = lax.axis_index("dp")
    tn = lax.axis_index("tensor")
    yy, xx = dp // NQ, dp % NQ
    z, core = tn // 2, tn % 2

    def zdev(step):
        return {"dp": dp, "tensor": ((z + step + NZ) % NZ) * 2 + core}

    sdev = {"dp": dp, "tensor": z * 2 + (1 - core)}

    def ydev(step):
        return {"dp": ((yy + step + NQ) % NQ) * NQ + xx, "tensor": tn}

    def xdev(step):
        return {"dp": yy * NQ + (xx + step + NQ) % NQ, "tensor": tn}

    sends = []

    def rcopy(src, dst, ssem, rsem, dev):
        return pltpu.make_async_remote_copy(
            src_ref=src, dst_ref=dst, send_sem=ssem, recv_sem=rsem,
            device_id=dev, device_id_type=MESH,
        )

    def go(copy):
        copy.start()
        sends.append(copy)

    barrier = pltpu.get_barrier_semaphore()
    for dev in (sdev, zdev(1), zdev(-1), xdev(1), xdev(-1), ydev(1), ydev(-1)):
        pl.semaphore_signal(barrier, inc=1, device_id=dev, device_id_type=MESH)

    fields = (xg, gg)
    own = pl.ds(tn * U, U)
    local = [
        pltpu.make_async_copy(x_hbm, xg.at[own], lsem.at[0]),
        pltpu.make_async_copy(g_hbm, gg.at[own], lsem.at[1]),
        pltpu.make_async_copy(win_hbm, win, lsem.at[2]),
        pltpu.make_async_copy(wout_hbm, wout, lsem.at[3]),
    ]
    for c in local:
        c.start()

    def live_col(n, s):
        return jnp.where(s < cnt_ref[n], col_ref[n, s], DB)

    sub = lax.broadcasted_iota(jnp.int32, (8, 128), 0)
    lan = lax.broadcasted_iota(jnp.int32, (8, 128), 1)
    table = jnp.full((8, 128), NB, jnp.int32)
    for n in range(ROWS):
        for s in range(SLOTS):
            table = jnp.where((sub == n) & (lan == live_col(n, s)), n * SLOTS + s, table)
    table = jnp.where(lan < DB, table, NB)
    tabv[...] = table
    tcopy = pltpu.make_async_copy(tabv, tab, lsem.at[4])
    tcopy.start()
    xg[2 * DB] = jnp.zeros((64, BLK), BF)
    xg[2 * DB + 1] = jnp.zeros((64, BLK), BF)
    gg[2 * DB] = jnp.zeros((64, BLK), BF)
    gg[2 * DB + 1] = jnp.zeros((64, BLK), BF)
    cbuf[NB] = jnp.zeros((BLK, BLK), F32)

    def piece(ref, t, lo=0, n=U):
        return ref.at[pl.ds(t * U + lo, n)]

    def wrap(step):
        return (z + step + 2 * NZ) % NZ

    def ag_copy(a, way, k, h):
        step = -(k + 1) if way == 0 else k + 1
        v = piece(fields[a], wrap(step) * 2 + core, *SPAN[h])
        i = ((a * 2 + way) * 4 + k) * 2 + h
        return rcopy(v, v, ag_s.at[i], ag_r.at[i], zdev(1 if way == 0 else -1))

    def ag_send(a, way, k, h):
        step = -k if way == 0 else k
        v = piece(fields[a], wrap(step) * 2 + core, *SPAN[h])
        i = ((a * 2 + way) * 4 + k) * 2 + h
        return rcopy(v, v, ag_s.at[i], ag_r.at[i], zdev(1 if way == 0 else -1))

    def sb_place(j):
        if j == 0:
            return 0, (0, U)
        if j < 7:
            way, k = (j - 1) // 3, (j - 1) % 3
            return (-(k + 1) if way == 0 else k + 1), (0, U)
        return 4, SPAN[j - 7]

    def sb_copy(a, j, mine):
        step, span = sb_place(j)
        v = piece(fields[a], wrap(step) * 2 + (core if mine else 1 - core), *span)
        return rcopy(v, v, sb_s.at[a * 9 + j], sb_r.at[a * 9 + j], sdev)

    def ag_start(a):
        for h in range(2):
            for way in range(2):
                go(ag_send(a, way, 0, h))
        go(sb_copy(a, 0, True))

    def ag_event(a, k, h):
        for way in range(2):
            if k == 3 and h != way:
                continue
            ag_copy(a, way, k, h).wait_recv()
            if k < 2 or (k == 2 and h == way):
                go(ag_send(a, way, k + 1, h))
        if k < 3 and h == 1:
            go(sb_copy(a, 1 + k, True))
            go(sb_copy(a, 4 + k, True))
        if k == 3:
            go(sb_copy(a, 7 + h, True))

    def gathered(a):
        for j in range(9):
            sb_copy(a, j, False).wait_recv()

    def turn(lo, hi):
        def body(n, carry):
            for s in range(SLOTS):
                i = n * SLOTS + s
                wint[n, :, s * BLK:(s + 1) * BLK] = win[i].T
                woutt[i] = wout[i].T
            return carry

        lax.fori_loop(lo, hi, body, 0)

    def listed(ref, n):
        parts = []
        for s in range(SLOTS):
            i = live_col(n, s) * 2
            parts += [ref[i], ref[i + 1]]
        return cat(parts, 0)

    def tall(ref, n):
        return ref[pl.ds(n * SLOTS, SLOTS)].reshape(SLOTS * BLK, BLK)

    def keep(n, prod):
        cbuf[pl.ds(n * SLOTS, SLOTS)] = prod.reshape(SLOTS, BLK, BLK)

    def forward(lo, hi):
        def body(n, carry):
            pre = dot(wint[n], listed(xg, n))
            sq = pre * pre
            th = jnp.tanh(C0 * pre * (1.0 + C1 * sq))
            half = 0.5 * (1.0 + th)
            dgelu[n] = half + 0.5 * pre * (1.0 - th * th) * (C0 * (1.0 + 3.0 * C1 * sq))
            h = (pre * half).astype(BF)
            hid[n] = h
            keep(n, dot(tall(woutt, n), h))
            return carry

        lax.fori_loop(lo, hi, body, 0)

    def half_of(ref, c):
        return ref.at[pl.ds(pl.multiple_of(c * CH, 64), CH)]

    def sib_copy(a, zz):
        i = a * NZ + zz
        return rcopy(half_of(part.at[a, zz], 1 - core), sib.at[a, zz], ss_s.at[i], ss_r.at[i], sdev)

    def place(a, steps):
        for step in steps:
            zz = wrap(step)
            for k in range(7):
                acc = cbuf[tab[0, zz * 7 + k]]
                for n in range(1, ROWS):
                    acc = acc + cbuf[tab[n, zz * 7 + k]]
                part[a, zz, 128 * k:128 * k + 128, :] = acc.astype(BF)
            go(sib_copy(a, zz))

    def chip_sum(a, step):
        zz = wrap(step)
        sib_copy(a, zz).wait_recv()
        return zz, half_of(part.at[a, zz], core)[...].astype(F32) + sib[a, zz].astype(F32)

    def z_copy(src, a, way, r):
        i = (a * 2 + way) * 4 + r
        dst = (rp if way == 0 else rm).at[a, r]
        return rcopy(src, dst, zs.at[i], zr.at[i], zdev(1 if way == 0 else -1))

    def z_first(a, way):
        r = 3 if a == way else 2
        zz, total = chip_sum(a, r + 1 if way == 0 else -(r + 1))
        src = half_of(part.at[a, zz], core)
        src[...] = total.astype(BF)
        go(z_copy(src, a, way, r))

    def z_next(a, way, r):
        buf = rp if way == 0 else rm
        z_copy(buf.at[a, r], a, way, r).wait_recv()
        zz, total = chip_sum(a, r if way == 0 else -r)
        buf[a, r] = (buf[a, r].astype(F32) + total).astype(BF)
        go(z_copy(buf.at[a, r], a, way, r - 1))

    def z_last(a, dst):
        zz, total = chip_sum(a, 0)
        for way in range(2):
            buf = rp if way == 0 else rm
            z_copy(buf.at[a, 0], a, way, 0).wait_recv()
            total = total + buf[a, 0].astype(F32)
        dst[...] = total.astype(BF)

    coords = ((yy, xx), (xx, yy))
    devs = ((ydev, xdev), (xdev, ydev))
    bufs = ((wpa, w2a), (wpb, w2b))

    def at4(i):
        return (i + 2 * NQ) % NQ

    def lines(h):
        return pl.ds(SPAN[h][0] * 64, SPAN[h][1] * 64)

    def w_copy(src, a, ph, h, m):
        sign = 1 if h == 0 else -1
        i = ((a * 2 + ph) * 2 + h) * 3 + m
        return rcopy(
            src, bufs[h][ph].at[a, m], xs.at[i], xr.at[i], devs[a][ph](sign if m < 2 else -sign)
        )

    def w_src(a, ph, h, step):
        c = at4(coords[a][ph] + step * (1 if h == 0 else -1))
        if ph == 0:
            return wgt.at[a, c, :, lines(h)]
        return red.at[a, c, lines(h)]

    def w_start(a, ph, h):
        go(w_copy(w_src(a, ph, h, 2), a, ph, h, 0))
        go(w_copy(w_src(a, ph, h, -1), a, ph, h, 2))

    def w_pass(a, ph, h):
        buf = bufs[h][ph]
        w_copy(buf.at[a, 0], a, ph, h, 0).wait_recv()
        mine = w_src(a, ph, h, 1)
        if ph == 0:
            for q in range(NQ):
                buf[a, 0, q] = (buf[a, 0, q].astype(F32) + mine[q].astype(F32)).astype(BF)
        else:
            buf[a, 0] = (buf[a, 0].astype(F32) + mine[...].astype(F32)).astype(BF)
        go(w_copy(buf.at[a, 0], a, ph, h, 1))

    def w_done(a, ph, h, dst):
        buf = bufs[h][ph]
        for m in (2, 1):
            w_copy(buf.at[a, m], a, ph, h, m).wait_recv()
        mine = w_src(a, ph, h, 0)
        if ph == 0:
            for q in range(NQ):
                total = mine[q].astype(F32) + buf[a, 1, q].astype(F32) + buf[a, 2, q].astype(F32)
                red[a, q, lines(h)] = total.astype(BF)
        else:
            dst[lines(h), :] = mine[...].astype(F32) + buf[a, 1].astype(F32) + buf[a, 2].astype(F32)

    def backward_out(lo, hi):
        def body(n, carry):
            picked = listed(gg, n)
            gh = dot(cat([wout[n * SLOTS + s] for s in range(SLOTS)], 1), picked)
            gpre[n] = (gh * dgelu[n]).astype(BF)
            gw = lax.dot_general(hid[n], picked, NT, preferred_element_type=F32)
            for s in range(0, SLOTS, 2):
                one = gw[:, s * BLK:(s + 1) * BLK].reshape(16, 8, BLK)
                two = gw[:, (s + 1) * BLK:(s + 2) * BLK].reshape(16, 8, BLK)
                row = pl.multiple_of((n * SLOTS + s) * 8, 16)
                wgt[0, :, :, pl.ds(row, 16), :] = cat([one, two], 1).astype(BF).reshape(4, 4, 16, BLK)
            return carry

        lax.fori_loop(lo, hi, body, 0)

    def backward_in(lo, hi):
        def body(n, carry):
            gw = lax.dot_general(listed(xg, n), gpre[n], NT, preferred_element_type=F32)
            gw = gw.reshape(SLOTS, 16, 8, BLK)
            for s in range(0, SLOTS, 2):
                both = cat([gw[s], gw[s + 1]], 1).astype(BF).reshape(4, 4, 16, BLK)
                row = pl.multiple_of((n * SLOTS + s) * 8, 16)
                for p in range(4):
                    for q in range(4):
                        wgt[1, p, q, pl.ds(row, 16), :] = both[q, p]
            return carry

        lax.fori_loop(lo, hi, body, 0)

    def backward_x(lo, hi):
        def body(n, carry):
            keep(n, dot(tall(win, n), gpre[n]))
            return carry

        lax.fori_loop(lo, hi, body, 0)

    local[0].wait()
    local[1].wait()
    pl.semaphore_wait(barrier, 7)
    ag_start(0)
    local[2].wait()
    local[3].wait()
    tcopy.wait()
    turn(0, 2)
    ag_event(0, 0, 0)
    turn(2, 3)
    ag_event(0, 0, 1)
    turn(3, 4)
    ag_event(0, 1, 0)
    turn(4, 5)
    ag_event(0, 1, 1)
    turn(5, 6)
    ag_event(0, 2, 0)
    turn(6, 7)
    ag_event(0, 2, 1)
    ag_start(1)
    ag_event(0, 3, 0)
    ag_event(0, 3, 1)
    gathered(0)
    forward(0, 3)
    ag_event(1, 0, 0)
    ag_event(1, 0, 1)
    forward(3, 5)
    ag_event(1, 1, 0)
    ag_event(1, 1, 1)
    forward(5, 7)
    place(0, ORDER[:3])
    ag_event(1, 2, 0)
    ag_event(1, 2, 1)
    place(0, ORDER[3:])
    ag_event(1, 3, 0)
    ag_event(1, 3, 1)
    z_first(0, 0)
    z_first(0, 1)
    gathered(1)
    backward_out(0, 4)
    w_start(0, 0, 0)
    backward_out(4, 7)
    w_start(0, 0, 1)
    z_next(0, 0, 3)
    z_next(0, 1, 2)
    backward_in(0, 4)
    w_start(1, 0, 0)
    backward_in(4, 7)
    w_start(1, 0, 1)
    backward_x(0, 7)
    w_pass(0, 0, 0)
    w_pass(0, 0, 1)
    z_next(0, 0, 2)
    z_next(0, 1, 1)
    place(1, ORDER)
    z_first(1, 1)
    z_first(1, 0)
    w_pass(1, 0, 0)
    w_pass(1, 0, 1)
    z_next(0, 0, 1)
    z_next(1, 1, 3)
    z_next(1, 0, 2)
    z_last(0, out_ref)
    w_done(0, 0, 0, None)
    w_start(0, 1, 0)
    w_done(0, 0, 1, None)
    w_start(0, 1, 1)
    z_next(1, 1, 2)
    z_next(1, 0, 1)
    w_done(1, 0, 0, None)
    w_start(1, 1, 0)
    w_done(1, 0, 1, None)
    w_start(1, 1, 1)
    w_pass(0, 1, 0)
    w_pass(0, 1, 1)
    z_next(1, 1, 1)
    w_pass(1, 1, 0)
    w_pass(1, 1, 1)
    z_last(1, ing_ref)
    for a, dst in ((0, gwout_ref), (1, gwin_ref)):
        for h in range(2):
            w_done(a, 1, h, dst)
    for c in sends:
        c.wait_send()


def copy_out(*refs):
    copies = [pltpu.make_async_copy(refs[i], refs[4 + i], refs[8].at[i]) for i in range(4)]
    for c in copies:
        c.start()
    for c in copies:
        c.wait()


def on_device(inputs, out_grad, w_in, w_out, columns, counts):
    vm = pl.BlockSpec(memory_space=pltpu.VMEM)
    sm = pl.BlockSpec(memory_space=pltpu.SMEM)
    hbm = pl.BlockSpec(memory_space=pltpu.HBM)
    anyw = pl.BlockSpec(memory_space=pl.ANY)
    dma = pltpu.SemaphoreType.DMA
    shapes = (
        jax.ShapeDtypeStruct((CH, BLK), BF),
        jax.ShapeDtypeStruct((CH, BLK), BF),
        jax.ShapeDtypeStruct((CH, BLK), F32),
        jax.ShapeDtypeStruct((CH, BLK), F32),
    )
    res = pl.pallas_call(
        kernel,
        out_shape=shapes,
        in_specs=[sm, sm, hbm, hbm, hbm, hbm],
        out_specs=(vm, vm, vm, vm),
        scratch_shapes=[
            pltpu.VMEM((2 * DB + 2, 64, BLK), BF),
            pltpu.VMEM((2 * DB + 2, 64, BLK), BF),
            pltpu.VMEM((NB, BLK, BLK), BF),
            pltpu.VMEM((NB, BLK, BLK), BF),
            pltpu.VMEM((ROWS, BLK, SLOTS * BLK), BF),
            pltpu.VMEM((NB, BLK, BLK), BF),
            pltpu.VMEM((ROWS, BLK, 128), F32),
            pltpu.VMEM((ROWS, BLK, 128), BF),
            pltpu.VMEM((ROWS, BLK, 128), BF),
            pltpu.VMEM((NB + 1, BLK, 128), F32),
            pltpu.VMEM((2, NZ, 2 * CH, BLK), BF),
            pltpu.VMEM((2, NZ, CH, BLK), BF),
            pltpu.VMEM((2, 4, CH, BLK), BF),
            pltpu.VMEM((2, 4, CH, BLK), BF),
            pltpu.VMEM((2, 4, 4, CH, BLK), BF),
            pltpu.VMEM((2, 3, 4, 256, BLK), BF),
            pltpu.VMEM((2, 3, 4, 192, BLK), BF),
            pltpu.VMEM((2, 4, CH, BLK), BF),
            pltpu.VMEM((2, 3, 256, BLK), BF),
            pltpu.VMEM((2, 3, 192, BLK), BF),
            pltpu.VMEM((8, 128), jnp.int32),
            pltpu.SMEM((8, 128), jnp.int32),
            dma((5,)),
            dma((32,)), dma((32,)),
            dma((18,)), dma((18,)),
            dma((16,)), dma((16,)),
            dma((16,)), dma((16,)),
            dma((24,)), dma((24,)),
        ],
        compiler_params=pltpu.CompilerParams(
            collective_id=0, has_side_effects=True, vmem_limit_bytes=52 * 1024 * 1024
        ),
        cost_estimate=pl.CostEstimate(flops=1_409_286_144, bytes_accessed=8_000_000, transcendentals=114_688),
    )(
        columns, counts,
        inputs.T.reshape(U, 64, BLK), out_grad.T.reshape(U, 64, BLK),
        w_in.reshape(NB, BLK, BLK), w_out.reshape(NB, BLK, BLK),
    )
    out, ing, gwin, gwout = pl.pallas_call(
        copy_out,
        out_shape=shapes,
        in_specs=[anyw] * 4,
        out_specs=(anyw,) * 4,
        scratch_shapes=[dma((4,))],
        cost_estimate=pl.CostEstimate(flops=0, bytes_accessed=1_400_000, transcendentals=0),
    )(*res)
    return (out.T, ing.T, gwin.reshape(ROWS, SLOTS, 8, BLK), gwout.reshape(ROWS, SLOTS, 8, BLK))


def solution(mesh):
    return jax.shard_map(
        on_device,
        mesh=mesh,
        in_specs=(
            P("dp", "tensor"),
            P("dp", "tensor"),
            P("tensor", None, None, None),
            P("tensor", None, None, None),
            P("tensor", None),
            P("tensor"),
        ),
        out_specs=(
            P("dp", "tensor"),
            P("dp", "tensor"),
            P("tensor", None, "dp", None),
            P("tensor", None, "dp", None),
        ),
        check_vma=False,
    )
```

time: 412 us -> 103 us (0.25)
  waiting for transfers between devices: 308 us -> 0 us
  Pallas kernels: 0 us -> 94.8 us
  other arithmetic: 35.7 us -> 0 us
  local copies, waits for them, and re-layouts: 37.7 us -> 5.77 us
  between operations: 14.9 us -> 0.66 us
  matrix products: 10.9 us -> 0 us
    reduce_scatter x3 -> x0, waiting for transfers between devices: 197 us -> none  [the longest x1 80.3 us: on_device(): lax.psum_scatter(grad_wout.astype(jnp.bfloat16), 'dp', scatter_dimension=...]
    pallas_call x0 -> x2, Pallas kernels: none -> 94.8 us  [the longest x1 72.9 us: on_device(): pl.pallas_call(kernel, out_shape=shapes, in_specs=[sm, sm, hbm, hbm, hbm,...]
    all_gather x2 -> x0, waiting for transfers between devices: 78.7 us -> none  [the longest x1 41.2 us: on_device(): gathered = lax.all_gather(inputs, 'tensor', axis=1, tiled=True)]
    unnamed x7 -> x0, waiting for transfers between devices: 32.5 us -> none
    scatter-add x2 -> x0, other arithmetic: 26.6 us -> none  [place_blocks(): jnp.zeros((tokens, blocks_wide, BLK), jnp.float32).at[:, flat]]
    reshape x4 -> x0, local copies, waits for them, and re-layouts: 11.6 us -> none  [the longest x2 10.8 us: place_blocks(): flat_contrib = contrib.reshape(tokens, -1, BLK)]
    dot_general x6 -> x0, matrix products: 10.9 us -> none  [the longest x1 2.72 us: on_device(): jnp.einsum('tnb,nkbc->tnkc', hidden, w_out_live, preferred_element_type=j...]
    convert_element_type x3 -> x0, local copies, waits for them, and re-layouts: 8.6 us -> none  [the longest x1 2.94 us: on_device(): partial_in.astype(jnp.bfloat16)]
  transfers between devices with their start and end apart: 6 -> 0, of which waited for: 6 -> 0; matrix products, arithmetic and copies ran while one was open for 17% -> 0% of each run, Pallas kernels for 0% -> 0%
where the time goes in v2:
time: 103 us; the launch traced here: 101 us
  Pallas kernels  94.8 us (92%)
  local copies, waits for them, and re-layouts  5.77 us (6%)
    pallas_call x1, Pallas kernels, on_device(): pl.pallas_call(kernel, out_shape=shapes, in_specs=[sm, sm, hbm, hbm, hbm,...  72.9 us
    pallas_call x1, Pallas kernels, on_device(): pl.pallas_call(copy_out, out_shape=shapes, in_specs=[anyw] * 4, out_specs...  22 us
    unnamed x16, local copies, waits for them, and re-layouts  5.77 us

profile of v2, /device:TPU:32, one launch (start us, length us, event | category | flops | bytes accessed | tf_op | source)
XLA Modules:
  0.0 101.3 jit_solution(14318408025990519820)
XLA Ops:
  0.6 0.0 copy-start.4
  0.6 0.9 copy-done.4
  1.5 0.0 copy-start.5
  1.5 0.9 copy-done.5
  2.4 0.0 copy-start.6
  2.4 0.7 copy-done.6
  3.1 0.0 copy-start.7
  3.1 0.7 copy-done.7
  3.8 72.9 %shard_map.93 = (bf16[448,128]{1,0:T(8,128)(2,1)S(1)}, bf16[448,128]{1,0:T(8,128)(2,1)S(1)}, f32[448,128]{1,0:T(8,128)S(1)}, f32[448,128]{1,0:T(8,128)S(1)}) custom-call(s32[7,8]{1,0:T(8,128)S(1)} %copy-done.6, s32[7]{0:T(128)S(1)} %copy-done.7, bf16[7,64,128]{2,1,0:T(8,128)(2,1)S(1)} %bitcast.12, bf16[7,64,128]{2,1,0:T(8,128)(2,1)S(1)} %bitcast.13, ...), custom_call_target="tpu_custom_call" | custom-call | flops 1409286144 | bytes 8000000 | tf_op jit(solution)/shard_map/pallas_call | solution.py:436
  76.6 0.0 copy-start
  76.6 0.7 copy-done
  77.3 0.0 copy-start.1
  77.3 0.7 copy-done.1
  78.0 0.0 copy-start.2
  78.0 0.6 copy-done.2
  78.6 0.0 copy-start.3
  78.6 0.6 copy-done.3
  79.3 22.0 %shard_map.94 = (bf16[448,128]{1,0:T(8,128)(2,1)}, bf16[448,128]{1,0:T(8,128)(2,1)}, f32[448,128]{1,0:T(8,128)}, f32[448,128]{1,0:T(8,128)}) custom-call(bf16[448,128]{1,0:T(8,128)(2,1)} %copy-done.2, bf16[448,128]{1,0:T(8,128)(2,1)} %copy-done.3, f32[448,128]{1,0:T(8,128)} %copy-done, f32[448,128]{1,0:T(8,128)} %copy-done.1), custom_call_target="tpu_custom_call" | custom-call | bytes 1400000 | tf_op jit(solution)/shard_map/pallas_call | solution.py:480
Async XLA Ops:
  0.6 0.9 copy-start.4
  1.5 0.9 copy-start.5
  2.4 0.7 copy-start.6
  3.1 0.7 copy-start.7
  76.6 0.7 copy-start
  77.3 0.7 copy-start.1
  78.0 0.6 copy-start.2
  78.6 0.6 copy-start.3

commit v3 on v2

v3 whole, which is shorter than its diff:
```python
import jax
import jax.numpy as jnp
from jax import lax
from jax.experimental import pallas as pl
from jax.experimental.pallas import tpu as pltpu
from jax.sharding import PartitionSpec as P

BLK = 128
SLOTS = 8
ROWS = 7
NB = ROWS * SLOTS
DB = 56
NZ = 8
NQ = 4
CH = 448
U = 7
SPAN = ((0, 4), (4, 3))
H = 224
W = 112
BF = jnp.bfloat16
F32 = jnp.float32
MESH = pl.DeviceIdType.MESH
C0 = 0.7978845608028654
C1 = 0.044715
ORDER = (4, 3, -3, 2, -2, 1, -1, 0)
NT = (((1,), (1,)), ((), ()))


def cat(parts, axis):
    return jnp.concatenate(parts, axis=axis)


def dot(a, b):
    return jnp.dot(a, b, preferred_element_type=F32)


def kernel(
    col_ref, cnt_ref, x_hbm, g_hbm, win_hbm, wout_hbm,
    out_ref, ing_ref, gwin_ref, gwout_ref,
    xg, gg, win, wout, wint, woutt, dgelu, hid, gpre, cbuf, run, part, sib, zb,
    wgt, wp, red, w2, tabv, tab,
    lsem, ag_s, ag_r, sb_s, sb_r, ss_s, ss_r, zs, zr, xs, xr,
):
    dp = lax.axis_index("dp")
    tn = lax.axis_index("tensor")
    yy, xx = dp // NQ, dp % NQ
    z, core = tn // 2, tn % 2

    def zdev(step):
        return {"dp": dp, "tensor": ((z + step + NZ) % NZ) * 2 + core}

    sdev = {"dp": dp, "tensor": z * 2 + (1 - core)}

    def ydev(step):
        return {"dp": ((yy + step + NQ) % NQ) * NQ + xx, "tensor": tn}

    def xdev(step):
        return {"dp": yy * NQ + (xx + step + NQ) % NQ, "tensor": tn}

    sends = []

    def rcopy(src, dst, ssem, rsem, dev):
        return pltpu.make_async_remote_copy(
            src_ref=src, dst_ref=dst, send_sem=ssem, recv_sem=rsem,
            device_id=dev, device_id_type=MESH,
        )

    def go(copy):
        copy.start()
        sends.append(copy)

    barrier = pltpu.get_barrier_semaphore()
    for dev in (sdev, zdev(1), zdev(-1), xdev(1), xdev(-1), ydev(1), ydev(-1)):
        pl.semaphore_signal(barrier, inc=1, device_id=dev, device_id_type=MESH)

    fields = (xg, gg)
    own = pl.ds(tn * U, U)
    local = [
        pltpu.make_async_copy(x_hbm, xg.at[own], lsem.at[0]),
        pltpu.make_async_copy(g_hbm, gg.at[own], lsem.at[1]),
        pltpu.make_async_copy(win_hbm, win, lsem.at[2]),
        pltpu.make_async_copy(wout_hbm, wout, lsem.at[3]),
    ]
    for c in local:
        c.start()

    def live_col(n, s):
        return jnp.where(s < cnt_ref[n], col_ref[n, s], DB)

    def make_table():
        sub = lax.broadcasted_iota(jnp.int32, (8, 128), 0)
        lan = lax.broadcasted_iota(jnp.int32, (8, 128), 1)
        down = []
        across = jnp.full((8, 128), 1000, jnp.int32)
        for n in range(ROWS):
            v = jnp.zeros((8, 128), jnp.int32)
            for s in range(SLOTS):
                c = live_col(n, s)
                v = jnp.where(sub == s, c, v)
                across = jnp.where(lan == n * SLOTS + s, c, across)
            down.append(v)
        across = across * 64 + lan

        def add_rows(parts):
            t = parts[0]
            for v in parts[1:]:
                t = t + v
            for sh in (4, 2, 1):
                t = t + pltpu.roll(t, sh, 0)
            return t

        def count(v):
            return jnp.where(v, 1, 0)

        spots = [jnp.full((8, 128), n * SLOTS, jnp.int32) + sub for n in range(ROWS)]
        ranks = []
        for n in range(ROWS):
            t = count(across < down[n] * 64 + spots[n])
            for sh in (64, 32, 16, 8, 4, 2, 1):
                t = t + pltpu.roll(t, sh, 1)
            ranks.append(t)
        perm = add_rows([jnp.where(ranks[n] == lan, spots[n], 0) for n in range(ROWS)])
        cols = add_rows([jnp.where(ranks[n] == lan, down[n], 0) for n in range(ROWS)])
        same = count((cols == pltpu.roll(cols, 1, 1)) & (lan > 0))
        upto = add_rows([count(down[n] <= lan) for n in range(ROWS)])
        here = add_rows([count(down[n] == lan) for n in range(ROWS)])
        last = jnp.where(here > 0, upto - 1, NB)
        tabv[...] = jnp.where(sub == 0, perm, jnp.where(sub == 1, same, last))

    for ref in fields:
        ref[2 * DB] = jnp.zeros((64, BLK), BF)
        ref[2 * DB + 1] = jnp.zeros((64, BLK), BF)
    run[NB] = jnp.zeros((BLK, BLK), BF)

    def piece(ref, t, lo=0, n=U):
        return ref.at[pl.ds(t * U + lo, n)]

    def wrap(step):
        return (z + step + 2 * NZ) % NZ

    def ag_copy(a, way, k, h):
        step = -(k + 1) if way == 0 else k + 1
        v = piece(fields[a], wrap(step) * 2 + core, *SPAN[h])
        i = ((a * 2 + way) * 4 + k) * 2 + h
        return rcopy(v, v, ag_s.at[i], ag_r.at[i], zdev(1 if way == 0 else -1))

    def ag_send(a, way, k, h):
        step = -k if way == 0 else k
        v = piece(fields[a], wrap(step) * 2 + core, *SPAN[h])
        i = ((a * 2 + way) * 4 + k) * 2 + h
        return rcopy(v, v, ag_s.at[i], ag_r.at[i], zdev(1 if way == 0 else -1))

    def sb_place(j):
        if j == 0:
            return 0, (0, U)
        if j < 7:
            way, k = (j - 1) // 3, (j - 1) % 3
            return (-(k + 1) if way == 0 else k + 1), (0, U)
        return 4, SPAN[j - 7]

    def sb_copy(a, j, mine):
        step, span = sb_place(j)
        v = piece(fields[a], wrap(step) * 2 + (core if mine else 1 - core), *span)
        return rcopy(v, v, sb_s.at[a * 9 + j], sb_r.at[a * 9 + j], sdev)

    def ag_start(a):
        for h in range(2):
            for way in range(2):
                go(ag_send(a, way, 0, h))
        go(sb_copy(a, 0, True))

    def ag_event(a, k, h):
        for way in range(2):
            if k == 3 and h != way:
                continue
            ag_copy(a, way, k, h).wait_recv()
            if k < 2 or (k == 2 and h == way):
                go(ag_send(a, way, k + 1, h))
        if k < 3 and h == 1:
            go(sb_copy(a, 1 + k, True))
            go(sb_copy(a, 4 + k, True))
        if k == 3:
            go(sb_copy(a, 7 + h, True))

    def gathered(a):
        for j in range(9):
            sb_copy(a, j, False).wait_recv()

    def turn():
        def body(n, carry):
            for s in range(SLOTS):
                i = n * SLOTS + s
                wint[n, :, s * BLK:(s + 1) * BLK] = win[i].T
                woutt[i] = wout[i].T
            return carry

        lax.fori_loop(0, ROWS, body, 0)

    def listed(ref, n):
        parts = []
        for s in range(SLOTS):
            i = live_col(n, s) * 2
            parts += [ref[i], ref[i + 1]]
        return cat(parts, 0)

    def tall(ref, n):
        return ref[n * SLOTS:(n + 1) * SLOTS].reshape(SLOTS * BLK, BLK)

    def hidden(lo, hi):
        for n in range(lo, hi):
            pre = dot(wint[n], listed(xg, n))
            sq = pre * pre
            th = jnp.tanh(C0 * pre * (1.0 + C1 * sq))
            half = 0.5 * (1.0 + th)
            dgelu[n] = half + 0.5 * pre * (1.0 - th * th) * (C0 * (1.0 + 3.0 * C1 * sq))
            hid[n] = (pre * half).astype(BF)

    def shares(w, act):
        for n in range(ROWS):
            cbuf[n * SLOTS:(n + 1) * SLOTS] = dot(tall(w, n), act[n]).reshape(SLOTS, BLK, BLK)

    def sib_copy(a, zz):
        i = a * NZ + zz
        src = part.at[a, zz, pl.ds(pl.multiple_of((1 - core) * CH, 64), CH)]
        return rcopy(src, sib.at[a, zz], ss_s.at[i], ss_r.at[i], sdev)

    def place(a):
        def add(r, acc):
            acc = acc * tab[1, r].astype(F32) + cbuf[tab[0, r]]
            run[r] = acc.astype(BF)
            return acc

        lax.fori_loop(0, NB, add, jnp.zeros((BLK, BLK), F32), unroll=4)
        for step in ORDER:
            zz = wrap(step)
            for k in range(7):
                part[a, zz, BLK * k:BLK * (k + 1), :] = run[tab[2, zz * 7 + k]]
            go(sib_copy(a, zz))

    met = set()

    def chip_sum(a, step, h):
        zz = wrap(step)
        if (a, step % NZ) not in met:
            met.add((a, step % NZ))
            sib_copy(a, zz).wait_recv()
        src = part.at[a, zz, pl.ds(pl.multiple_of(core * CH + h * H, 32), H)]
        return src, src[...].astype(F32) + sib[a, zz, h * H:(h + 1) * H].astype(F32)

    def z_copy(src, a, way, r, h):
        i = ((a * 2 + way) * 4 + r) * 2 + h
        dst = zb.at[a, way, r, pl.ds(h * H, H)]
        return rcopy(src, dst, zs.at[i], zr.at[i], zdev(1 if way == 0 else -1))

    def z_first(a):
        for r in (3, 2):
            for way in range(2):
                h = way if r == 3 else 1 - way
                src, total = chip_sum(a, r + 1 if way == 0 else -(r + 1), h)
                src[...] = total.astype(BF)
                go(z_copy(src, a, way, r, h))

    def z_next(a, r, only=None):
        for h2 in range(2):
            for way in range(2):
                h = way if h2 == 0 else 1 - way
                if r == 3 and h2 == 1:
                    continue
                buf = zb.at[a, way, r, pl.ds(h * H, H)]
                z_copy(buf, a, way, r, h).wait_recv()
                src, total = chip_sum(a, r if way == 0 else -r, h)
                buf[...] = (buf[...].astype(F32) + total).astype(BF)
                go(z_copy(buf, a, way, r - 1, h))

    def z_last(a, dst):
        for h in range(2):
            src, total = chip_sum(a, 0, h)
            for way in range(2):
                buf = zb.at[a, way, 0, pl.ds(h * H, H)]
                z_copy(buf, a, way, 0, h).wait_recv()
                total = total + buf[...].astype(F32)
            dst[h * H:(h + 1) * H, :] = total.astype(BF)

    coords = ((yy, xx), (xx, yy))
    devs = ((ydev, xdev), (xdev, ydev))

    def at4(i):
        return (i + 2 * NQ) % NQ

    def lines(p):
        return pl.ds(p * W, W)

    def w_dst(a, ph, p, m):
        return (wp if ph == 0 else w2).at[a, p, m]

    def w_copy(src, a, ph, p, m):
        sign = 1 if p % 2 == 0 else -1
        i = ((a * 2 + ph) * 4 + p) * 3 + m
        return rcopy(
            src, w_dst(a, ph, p, m), xs.at[i], xr.at[i], devs[p // 2][ph](sign if m < 2 else -sign)
        )

    def w_src(a, ph, p, step):
        c = at4(coords[p // 2][ph] + step * (1 if p % 2 == 0 else -1))
        if ph == 0:
            return wgt.at[a, c, :, lines(p)]
        return red.at[a, c, lines(p)]

    def w_start(a, ph, *ps):
        for p in ps:
            go(w_copy(w_src(a, ph, p, 2), a, ph, p, 0))
        for p in ps:
            go(w_copy(w_src(a, ph, p, -1), a, ph, p, 2))

    def w_pass(a, ph, *ps):
        for p in ps:
            buf = w_dst(a, ph, p, 0)
            w_copy(buf, a, ph, p, 0).wait_recv()
            mine = w_src(a, ph, p, 1)
            buf[...] = (buf[...].astype(F32) + mine[...].astype(F32)).astype(BF)
            go(w_copy(buf, a, ph, p, 1))

    def w_done(a, ph, p, dst):
        total = w_src(a, ph, p, 0)[...].astype(F32)
        for m in (2, 1):
            w_copy(w_dst(a, ph, p, m), a, ph, p, m).wait_recv()
            total = total + w_dst(a, ph, p, m)[...].astype(F32)
        if ph == 0:
            red[a, :, lines(p)] = total.astype(BF)
        else:
            dst[lines(p), :] = total

    def w_turn(a, *ps):
        for p in ps:
            w_done(a, 0, p, None)
            w_start(a, 1, p)

    def store(a, row, both):
        both = both.astype(BF).reshape(NQ, NQ, 16, BLK)
        if row < 2 * W:
            wgt[a, :, :, row:row + 16, :] = both
        else:
            for p in range(NQ):
                for q in range(NQ):
                    wgt[a, p, q, row:row + 16, :] = both[q, p]

    def backward_out(lo, hi):
        for n in range(lo, hi):
            picked = listed(gg, n)
            gh = dot(cat([wout[n * SLOTS + s] for s in range(SLOTS)], 1), picked)
            gpre[n] = (gh * dgelu[n]).astype(BF)
            gw = lax.dot_general(hid[n], picked, NT, preferred_element_type=F32)
            for s in range(0, SLOTS, 2):
                one = gw[:, s * BLK:(s + 1) * BLK].reshape(16, 8, BLK)
                two = gw[:, (s + 1) * BLK:(s + 2) * BLK].reshape(16, 8, BLK)
                store(0, (n * SLOTS + s) * 8, cat([one, two], 1))

    def backward_in(lo, hi):
        for n in range(lo, hi):
            gw = lax.dot_general(listed(xg, n), gpre[n], NT, preferred_element_type=F32)
            gw = gw.reshape(SLOTS, 16, 8, BLK)
            for s in range(0, SLOTS, 2):
                store(1, (n * SLOTS + s) * 8, cat([gw[s], gw[s + 1]], 1))

    local[0].wait()
    local[1].wait()
    pl.semaphore_wait(barrier, 7)
    ag_start(0)
    ag_start(1)
    make_table()
    tcopy = pltpu.make_async_copy(tabv, tab, lsem.at[4])
    tcopy.start()
    local[2].wait()
    local[3].wait()
    turn()
    tcopy.wait()
    for k in range(3):
        for a in range(2):
            ag_event(a, k, 0)
            ag_event(a, k, 1)
    ag_event(0, 3, 0)
    ag_event(0, 3, 1)
    gathered(0)
    hidden(0, 4)
    ag_event(1, 3, 0)
    ag_event(1, 3, 1)
    hidden(4, 7)
    gathered(1)
    backward_out(0, 4)
    w_start(0, 0, 0, 1)
    backward_out(4, 7)
    w_start(0, 0, 2, 3)
    shares(woutt, hid)
    place(0)
    backward_in(0, 4)
    w_start(1, 0, 0, 1)
    backward_in(4, 7)
    w_start(1, 0, 2, 3)
    z_first(0)
    w_pass(0, 0, 0, 1)
    shares(win, gpre)
    place(1)
    w_pass(0, 0, 2, 3)
    z_next(0, 3)
    z_first(1)
    w_pass(1, 0, 0, 1)
    z_next(0, 2)
    z_next(1, 3)
    w_pass(1, 0, 2, 3)
    w_turn(0, 0, 1, 2, 3)
    z_next(1, 2)
    z_next(0, 1)
    w_turn(1, 0, 1, 2, 3)
    w_pass(0, 1, 0, 1, 2, 3)
    z_next(1, 1)
    w_pass(1, 1, 0, 1, 2, 3)
    z_last(0, out_ref)
    for p in range(4):
        w_done(0, 1, p, gwout_ref)
    z_last(1, ing_ref)
    for p in range(4):
        w_done(1, 1, p, gwin_ref)
    for c in sends:
        c.wait_send()


def finish(*refs):
    for i in range(4):
        refs[4 + i][...] = refs[i][...]


def on_device(inputs, out_grad, w_in, w_out, columns, counts):
    vm = pl.BlockSpec(memory_space=pltpu.VMEM)
    sm = pl.BlockSpec(memory_space=pltpu.SMEM)
    hbm = pl.BlockSpec(memory_space=pltpu.HBM)
    dma = pltpu.SemaphoreType.DMA
    shapes = (
        jax.ShapeDtypeStruct((CH, BLK), BF),
        jax.ShapeDtypeStruct((CH, BLK), BF),
        jax.ShapeDtypeStruct((CH, BLK), F32),
        jax.ShapeDtypeStruct((CH, BLK), F32),
    )
    res = pl.pallas_call(
        kernel,
        out_shape=shapes,
        in_specs=[sm, sm, hbm, hbm, hbm, hbm],
        out_specs=(vm, vm, vm, vm),
        scratch_shapes=[
            pltpu.VMEM((2 * DB + 2, 64, BLK), BF),
            pltpu.VMEM((2 * DB + 2, 64, BLK), BF),
            pltpu.VMEM((NB, BLK, BLK), BF),
            pltpu.VMEM((NB, BLK, BLK), BF),
            pltpu.VMEM((ROWS, BLK, SLOTS * BLK), BF),
            pltpu.VMEM((NB, BLK, BLK), BF),
            pltpu.VMEM((ROWS, BLK, 128), F32),
            pltpu.VMEM((ROWS, BLK, 128), BF),
            pltpu.VMEM((ROWS, BLK, 128), BF),
            pltpu.VMEM((NB, BLK, 128), F32),
            pltpu.VMEM((NB + 1, BLK, 128), BF),
            pltpu.VMEM((2, NZ, 2 * CH, BLK), BF),
            pltpu.VMEM((2, NZ, CH, BLK), BF),
            pltpu.VMEM((2, 2, 4, CH, BLK), BF),
            pltpu.VMEM((2, NQ, NQ, CH, BLK), BF),
            pltpu.VMEM((2, 4, 3, NQ, W, BLK), BF),
            pltpu.VMEM((2, NQ, CH, BLK), BF),
            pltpu.VMEM((2, 4, 3, W, BLK), BF),
            pltpu.VMEM((8, 128), jnp.int32),
            pltpu.SMEM((8, 128), jnp.int32),
            dma((5,)),
            dma((32,)), dma((32,)),
            dma((18,)), dma((18,)),
            dma((16,)), dma((16,)),
            dma((32,)), dma((32,)),
            dma((48,)), dma((48,)),
        ],
        compiler_params=pltpu.CompilerParams(
            collective_id=0, has_side_effects=True, vmem_limit_bytes=63 * 1024 * 1024
        ),
        cost_estimate=pl.CostEstimate(flops=1_409_286_144, bytes_accessed=8_000_000, transcendentals=114_688),
    )(
        columns, counts,
        inputs.T.reshape(U, 64, BLK), out_grad.T.reshape(U, 64, BLK),
        w_in.reshape(NB, BLK, BLK), w_out.reshape(NB, BLK, BLK),
    )
    out, ing, gwin, gwout = pl.pallas_call(
        finish,
        out_shape=shapes,
        in_specs=[vm] * 4,
        out_specs=(vm,) * 4,
        compiler_params=pltpu.CompilerParams(vmem_limit_bytes=63 * 1024 * 1024),
        cost_estimate=pl.CostEstimate(flops=0, bytes_accessed=1_400_000, transcendentals=0),
    )(*res)
    return (out.T, ing.T, gwin.reshape(ROWS, SLOTS, 8, BLK), gwout.reshape(ROWS, SLOTS, 8, BLK))


def solution(mesh):
    return jax.shard_map(
        on_device,
        mesh=mesh,
        in_specs=(
            P("dp", "tensor"),
            P("dp", "tensor"),
            P("tensor", None, None, None),
            P("tensor", None, None, None),
            P("tensor", None),
            P("tensor"),
        ),
        out_specs=(
            P("dp", "tensor"),
            P("dp", "tensor"),
            P("tensor", None, "dp", None),
            P("tensor", None, "dp", None),
        ),
        check_vma=False,
    )
```

time: 103 us -> 65.3 us (0.63)
  Pallas kernels: 94.8 us -> 63.4 us
  local copies, waits for them, and re-layouts: 5.77 us -> 0 us
    pallas_call x1, Pallas kernels: 22 us -> 2.01 us  [on_device(): pl.pallas_call(finish, out_shape=shapes, in_specs=[vm] * 4, out_specs=(vm...]
    pallas_call x1, Pallas kernels: 72.9 us -> 61.4 us  [on_device(): pl.pallas_call(kernel, out_shape=shapes, in_specs=[sm, sm, hbm, hbm, hbm,...]
    unnamed x16 -> x0, local copies, waits for them, and re-layouts: 5.77 us -> none
where the time goes in v3:
time: 65.3 us; the launch traced here: 64 us
  Pallas kernels  63.4 us (97%)
    pallas_call x1, Pallas kernels, on_device(): pl.pallas_call(kernel, out_shape=shapes, in_specs=[sm, sm, hbm, hbm, hbm,...  61.4 us
    pallas_call x1, Pallas kernels, on_device(): pl.pallas_call(finish, out_shape=shapes, in_specs=[vm] * 4, out_specs=(vm...  2.01 us

profile of v3, /device:TPU:32, one launch (start us, length us, event | category | flops | bytes accessed | tf_op | source)
XLA Modules:
  0.0 64.0 jit_solution(2734318025376903520)
XLA Ops:
  0.6 61.4 %shard_map.93 = (bf16[448,128]{1,0:T(8,128)(2,1)}, bf16[448,128]{1,0:T(8,128)(2,1)}, f32[448,128]{1,0:T(8,128)}, f32[448,128]{1,0:T(8,128)}) custom-call(s32[7,8]{1,0:T(8,128)} %col_ref.1, s32[7]{0:T(128)} %cnt_ref.1, bf16[7,64,128]{2,1,0:T(8,128)(2,1)} %bitcast.16, bf16[7,64,128]{2,1,0:T(8,128)(2,1)} %bitcast.17, bf16[56,128,128]{2,1,0:T(8,128)(2,1)} %bitcast.12, ...), custom_call_target="tpu_custom_call" | custom-call | flops 1409286144 | bytes 8000000 | tf_op jit(solution)/shard_map/pallas_call | solution.py:443
  62.0 2.0 %shard_map.94 = (bf16[448,128]{1,0:T(8,128)(2,1)}, bf16[448,128]{1,0:T(8,128)(2,1)}, f32[448,128]{1,0:T(8,128)}, f32[448,128]{1,0:T(8,128)}) custom-call(bf16[448,128]{1,0:T(8,128)(2,1)} %get-tuple-element.12.refs_0_, bf16[448,128]{1,0:T(8,128)(2,1)} %get-tuple-element.13.refs_1_, f32[448,128]{1,0:T(8,128)} %get-tuple-element.14.refs_2_, ...), custom_call_target="tpu_custom_call" | custom-call | bytes 1400000 | tf_op jit(solution)/shard_map/pallas_call | solution.py:485

commit v4 on v3

--- a/solution.py
+++ b/solution.py
@@ -35,10 +35,10 @@
 
 
 def kernel(
-    col_ref, cnt_ref, x_hbm, g_hbm, win_hbm, wout_hbm,
+    col_hbm, cnt_hbm, x_hbm, g_hbm, win_hbm, wout_hbm,
     out_ref, ing_ref, gwin_ref, gwout_ref,
     xg, gg, win, wout, wint, woutt, dgelu, hid, gpre, cbuf, run, part, sib, zb,
-    wgt, wp, red, w2, tabv, tab,
+    wgt, wp, red, w2, tabv, tab, col_ref, cnt_ref,
     lsem, ag_s, ag_r, sb_s, sb_r, ss_s, ss_r, zs, zr, xs, xr,
 ):
     dp = lax.axis_index("dp")
@@ -80,6 +80,8 @@
         pltpu.make_async_copy(g_hbm, gg.at[own], lsem.at[1]),
         pltpu.make_async_copy(win_hbm, win, lsem.at[2]),
         pltpu.make_async_copy(wout_hbm, wout, lsem.at[3]),
+        pltpu.make_async_copy(col_hbm, col_ref, lsem.at[5]),
+        pltpu.make_async_copy(cnt_hbm, cnt_ref, lsem.at[6]),
     ]
     for c in local:
         c.start()
@@ -163,24 +165,30 @@
         v = piece(fields[a], wrap(step) * 2 + (core if mine else 1 - core), *span)
         return rcopy(v, v, sb_s.at[a * 9 + j], sb_r.at[a * 9 + j], sdev)
 
+    def part_of(way, i):
+        return way if i == 0 else 1 - way
+
     def ag_start(a):
-        for h in range(2):
+        for i in range(2):
             for way in range(2):
-                go(ag_send(a, way, 0, h))
+                go(ag_send(a, way, 0, part_of(way, i)))
         go(sb_copy(a, 0, True))
 
-    def ag_event(a, k, h):
+    def ag_pass(a, k, i):
         for way in range(2):
-            if k == 3 and h != way:
-                continue
+            go(ag_send(a, way, k + 1, part_of(way, i)))
+
+    def ag_take(a, k, i, on=True):
+        for way in range(2):
+            h = part_of(way, i)
             ag_copy(a, way, k, h).wait_recv()
-            if k < 2 or (k == 2 and h == way):
+            if on and (k < 2 or (k == 2 and i == 0)):
                 go(ag_send(a, way, k + 1, h))
-        if k < 3 and h == 1:
+            if k == 3:
+                go(sb_copy(a, 7 + h, True))
+        if k < 3 and i == 1:
             go(sb_copy(a, 1 + k, True))
             go(sb_copy(a, 4 + k, True))
-        if k == 3:
-            go(sb_copy(a, 7 + h, True))
 
     def gathered(a):
         for j in range(9):
@@ -344,12 +352,14 @@
                 for q in range(NQ):
                     wgt[a, p, q, row:row + 16, :] = both[q, p]
 
+    def backward_hidden():
+        for n in range(ROWS):
+            gh = dot(cat([wout[n * SLOTS + s] for s in range(SLOTS)], 1), listed(gg, n))
+            gpre[n] = (gh * dgelu[n]).astype(BF)
+
     def backward_out(lo, hi):
         for n in range(lo, hi):
-            picked = listed(gg, n)
-            gh = dot(cat([wout[n * SLOTS + s] for s in range(SLOTS)], 1), picked)
-            gpre[n] = (gh * dgelu[n]).astype(BF)
-            gw = lax.dot_general(hid[n], picked, NT, preferred_element_type=F32)
+            gw = lax.dot_general(hid[n], listed(gg, n), NT, preferred_element_type=F32)
             for s in range(0, SLOTS, 2):
                 one = gw[:, s * BLK:(s + 1) * BLK].reshape(16, 8, BLK)
                 two = gw[:, (s + 1) * BLK:(s + 2) * BLK].reshape(16, 8, BLK)
@@ -362,11 +372,20 @@
             for s in range(0, SLOTS, 2):
                 store(1, (n * SLOTS + s) * 8, cat([gw[s], gw[s + 1]], 1))
 
+    waited = [0]
+
+    def drain(upto):
+        for c in sends[waited[0]:upto]:
+            c.wait_send()
+        waited[0] = upto
+
     local[0].wait()
     local[1].wait()
     pl.semaphore_wait(barrier, 7)
     ag_start(0)
     ag_start(1)
+    local[4].wait()
+    local[5].wait()
     make_table()
     tcopy = pltpu.make_async_copy(tabv, tab, lsem.at[4])
     tcopy.start()
@@ -374,54 +393,65 @@
     local[3].wait()
     turn()
     tcopy.wait()
-    for k in range(3):
-        for a in range(2):
-            ag_event(a, k, 0)
-            ag_event(a, k, 1)
-    ag_event(0, 3, 0)
-    ag_event(0, 3, 1)
+    for i in range(2):
+        ag_take(0, 0, i)
+    for i in range(2):
+        ag_take(1, 0, i)
+    for i in range(2):
+        ag_take(0, 1, i)
+    ag_take(1, 1, 0)
+    ag_take(1, 1, 1, on=False)
+    ag_take(0, 2, 0)
+    ag_pass(1, 1, 1)
+    ag_take(0, 2, 1)
+    ag_take(1, 2, 0)
+    ag_take(0, 3, 0)
+    ag_take(1, 2, 1)
+    ag_take(1, 3, 0)
+    gather_sends = len(sends)
     gathered(0)
-    hidden(0, 4)
-    ag_event(1, 3, 0)
-    ag_event(1, 3, 1)
-    hidden(4, 7)
+    hidden(0, ROWS)
     gathered(1)
+    backward_hidden()
     backward_out(0, 4)
     w_start(0, 0, 0, 1)
     backward_out(4, 7)
     w_start(0, 0, 2, 3)
     shares(woutt, hid)
     place(0)
+    shares(win, gpre)
+    place(1)
+    z_first(0)
     backward_in(0, 4)
     w_start(1, 0, 0, 1)
+    z_first(1)
     backward_in(4, 7)
     w_start(1, 0, 2, 3)
-    z_first(0)
-    w_pass(0, 0, 0, 1)
-    shares(win, gpre)
-    place(1)
-    w_pass(0, 0, 2, 3)
+    w_pass(0, 0, 0, 1, 2, 3)
+    drain(gather_sends)
     z_next(0, 3)
-    z_first(1)
+    z_next(1, 3)
     w_pass(1, 0, 0, 1)
+    first_sends = len(sends)
     z_next(0, 2)
-    z_next(1, 3)
     w_pass(1, 0, 2, 3)
+    z_next(1, 2)
     w_turn(0, 0, 1, 2, 3)
-    z_next(1, 2)
+    drain(first_sends)
     z_next(0, 1)
+    z_next(1, 1)
     w_turn(1, 0, 1, 2, 3)
     w_pass(0, 1, 0, 1, 2, 3)
-    z_next(1, 1)
+    second_sends = len(sends)
+    z_last(0, out_ref)
     w_pass(1, 1, 0, 1, 2, 3)
-    z_last(0, out_ref)
+    z_last(1, ing_ref)
     for p in range(4):
         w_done(0, 1, p, gwout_ref)
-    z_last(1, ing_ref)
+    drain(second_sends)
     for p in range(4):
         w_done(1, 1, p, gwin_ref)
-    for c in sends:
-        c.wait_send()
+    drain(len(sends))
 
 
 def finish(*refs):
@@ -431,7 +461,6 @@
 
 def on_device(inputs, out_grad, w_in, w_out, columns, counts):
     vm = pl.BlockSpec(memory_space=pltpu.VMEM)
-    sm = pl.BlockSpec(memory_space=pltpu.SMEM)
     hbm = pl.BlockSpec(memory_space=pltpu.HBM)
     dma = pltpu.SemaphoreType.DMA
     shapes = (
@@ -443,7 +472,7 @@
     res = pl.pallas_call(
         kernel,
         out_shape=shapes,
-        in_specs=[sm, sm, hbm, hbm, hbm, hbm],
+        in_specs=[hbm] * 6,
         out_specs=(vm, vm, vm, vm),
         scratch_shapes=[
             pltpu.VMEM((2 * DB + 2, 64, BLK), BF),
@@ -466,7 +495,9 @@
             pltpu.VMEM((2, 4, 3, W, BLK), BF),
             pltpu.VMEM((8, 128), jnp.int32),
             pltpu.SMEM((8, 128), jnp.int32),
-            dma((5,)),
+            pltpu.SMEM((ROWS, SLOTS), jnp.int32),
+            pltpu.SMEM((ROWS,), jnp.int32),
+            dma((7,)),
             dma((32,)), dma((32,)),
             dma((18,)), dma((18,)),
             dma((16,)), dma((16,)),

time: 65.3 us -> 62.9 us (0.963); the launches traced: 64 us -> 62.8 us
  Pallas kernels: 63.4 us -> 62.2 us
    pallas_call x1, Pallas kernels: 61.4 us -> 60.2 us  [on_device(): pl.pallas_call(kernel, out_shape=shapes, in_specs=[hbm] * 6, out_specs=(v...]
where the time goes in v4:
time: 62.9 us; the launch traced here: 62.8 us
  Pallas kernels  62.2 us (99%)
  between operations  0.64 us (1%)
    pallas_call x1, Pallas kernels, on_device(): pl.pallas_call(kernel, out_shape=shapes, in_specs=[hbm] * 6, out_specs=(v...  60.2 us
    pallas_call x1, Pallas kernels, on_device(): pl.pallas_call(finish, out_shape=shapes, in_specs=[vm] * 4, out_specs=(vm...  2.01 us

profile of v4, /device:TPU:32, one launch (start us, length us, event | category | flops | bytes accessed | tf_op | source)
XLA Modules:
  0.0 62.8 jit_solution(10396636135396744384)
XLA Ops:
  0.6 60.2 %shard_map.93 = (bf16[448,128]{1,0:T(8,128)(2,1)}, bf16[448,128]{1,0:T(8,128)(2,1)}, f32[448,128]{1,0:T(8,128)}, f32[448,128]{1,0:T(8,128)}) custom-call(s32[7,8]{1,0:T(8,128)} %col_hbm.1, s32[7]{0:T(128)} %cnt_hbm.1, bf16[7,64,128]{2,1,0:T(8,128)(2,1)} %bitcast.16, bf16[7,64,128]{2,1,0:T(8,128)(2,1)} %bitcast.17, bf16[56,128,128]{2,1,0:T(8,128)(2,1)} %bitcast.12, ...), custom_call_target="tpu_custom_call" | custom-call | flops 1409286144 | bytes 8000000 | tf_op jit(solution)/shard_map/pallas_call | solution.py:472
  60.8 2.0 %shard_map.94 = (bf16[448,128]{1,0:T(8,128)(2,1)}, bf16[448,128]{1,0:T(8,128)(2,1)}, f32[448,128]{1,0:T(8,128)}, f32[448,128]{1,0:T(8,128)}) custom-call(bf16[448,128]{1,0:T(8,128)(2,1)} %get-tuple-element.12.refs_0_, bf16[448,128]{1,0:T(8,128)(2,1)} %get-tuple-element.13.refs_1_, f32[448,128]{1,0:T(8,128)} %get-tuple-element.14.refs_2_, ...), custom_call_target="tpu_custom_call" | custom-call | bytes 1400000 | tf_op jit(solution)/shard_map/pallas_call | solution.py:516

commit v5 on v4

--- a/solution.py
+++ b/solution.py
@@ -17,6 +17,7 @@
 SPAN = ((0, 4), (4, 3))
 H = 224
 W = 112
+GROUPS = ((0, 4), (4, 7))
 BF = jnp.bfloat16
 F32 = jnp.float32
 MESH = pl.DeviceIdType.MESH
@@ -24,6 +25,25 @@
 C1 = 0.044715
 ORDER = (4, 3, -3, 2, -2, 1, -1, 0)
 NT = (((1,), (1,)), ((), ()))
+PLAN = (
+    ("ag0", 0, 0), ("own", 0), ("ag0", 0, 1), ("ag0", 1, 0), ("own", 1), ("agw", 0, 0, 0), ("agf", 0, 0, 0),
+    ("agw", 0, 0, 1), ("agf", 0, 0, 1), ("agw", 1, 0, 0), ("ag0", 1, 1), ("tabl",), ("agf", 1, 0, 0),
+    ("agw", 0, 1, 0), ("agf", 0, 1, 0), ("turn",), ("agw", 0, 1, 1), ("agf", 0, 1, 1), ("ags", 0, 0),
+    ("agw", 1, 0, 1), ("ags", 1, 0), ("ags", 0, 1), ("agf", 1, 0, 1), ("agw", 0, 2, 0), ("agf", 0, 2, 0),
+    ("agw", 1, 1, 0), ("agw", 0, 2, 1), ("agf", 1, 1, 0), ("agw", 1, 1, 1), ("ags", 1, 1), ("ags", 0, 2),
+    ("agf", 1, 1, 1), ("agw", 0, 3, 0), ("ags", 0, 3), ("agw", 1, 2, 0), ("agf", 1, 2, 0), ("gath", 0), ("H", 0, 4),
+    ("agw", 1, 2, 1), ("ags", 1, 2), ("H", 4, 7), ("agw", 1, 3, 0), ("ags", 1, 3), ("S", 0), ("tab",), ("P", 0),
+    ("gath", 1), ("GO", 0), ("wm", 0, 0, 0, 0), ("GO", 1), ("wm", 0, 0, 1, 0), ("zf", 0, 3), ("wm", 0, 0, 0, 2),
+    ("GH",), ("zf", 0, 2), ("GI", 0), ("wm", 1, 0, 0, 2), ("S", 1), ("wm", 1, 0, 0, 0), ("zn", 0, 3, 0), ("P", 1),
+    ("zn", 0, 2, 1), ("wm", 0, 0, 1, 2), ("GI", 1), ("wm", 1, 0, 1, 0), ("zf", 1, 3), ("zn", 0, 2, 0), ("zf", 1, 2),
+    ("wp", 0, 0, 1), ("wp", 1, 0, 0), ("wp", 0, 0, 0), ("wm", 1, 0, 1, 2), ("zn", 1, 3, 0), ("zn", 0, 1, 0),
+    ("wp", 1, 0, 1), ("zn", 1, 2, 1), ("wd", 1, 0, 0), ("wm", 1, 1, 0, 0), ("zn", 1, 2, 0), ("zn", 0, 1, 1),
+    ("wd", 0, 0, 0), ("wm", 0, 1, 0, 0), ("wd", 0, 0, 1), ("wm", 0, 1, 1, 0), ("wd", 1, 0, 1), ("wm", 1, 1, 1, 0),
+    ("zn", 1, 1, 1), ("wm", 1, 1, 0, 2), ("drain", ("GI", 1)), ("wp", 1, 1, 0), ("wm", 0, 1, 0, 2),
+    ("wm", 0, 1, 1, 2), ("zn", 1, 1, 0), ("wp", 0, 1, 0), ("wp", 0, 1, 1), ("wm", 1, 1, 1, 2), ("wp", 1, 1, 1),
+    ("drain", ("wd", 1, 0, 0)), ("zl", 0), ("wd", 0, 1, 0), ("drain", ("wp", 1, 1, 0)), ("wd", 1, 1, 0),
+    ("wd", 0, 1, 1), ("zl", 1), ("wd", 1, 1, 1),
+)
 
 
 def cat(parts, axis):
@@ -168,27 +188,24 @@
     def part_of(way, i):
         return way if i == 0 else 1 - way
 
-    def ag_start(a):
-        for i in range(2):
-            for way in range(2):
-                go(ag_send(a, way, 0, part_of(way, i)))
-        go(sb_copy(a, 0, True))
+    def ag_first(a, i):
+        for way in range(2):
+            go(ag_send(a, way, 0, part_of(way, i)))
+
+    def ag_wait(a, k, i):
+        for way in range(2):
+            ag_copy(a, way, k, part_of(way, i)).wait_recv()
 
     def ag_pass(a, k, i):
         for way in range(2):
             go(ag_send(a, way, k + 1, part_of(way, i)))
 
-    def ag_take(a, k, i, on=True):
+    def ag_own(a):
+        go(sb_copy(a, 0, True))
+
+    def ag_sib(a, k):
         for way in range(2):
-            h = part_of(way, i)
-            ag_copy(a, way, k, h).wait_recv()
-            if on and (k < 2 or (k == 2 and i == 0)):
-                go(ag_send(a, way, k + 1, h))
-            if k == 3:
-                go(sb_copy(a, 7 + h, True))
-        if k < 3 and i == 1:
-            go(sb_copy(a, 1 + k, True))
-            go(sb_copy(a, 4 + k, True))
+            go(sb_copy(a, 7 + way if k == 3 else 1 + 3 * way + k, True))
 
     def gathered(a):
         for j in range(9):
@@ -223,7 +240,8 @@
             dgelu[n] = half + 0.5 * pre * (1.0 - th * th) * (C0 * (1.0 + 3.0 * C1 * sq))
             hid[n] = (pre * half).astype(BF)
 
-    def shares(w, act):
+    def shares(a):
+        w, act = ((woutt, hid), (win, gpre))[a]
         for n in range(ROWS):
             cbuf[n * SLOTS:(n + 1) * SLOTS] = dot(tall(w, n), act[n]).reshape(SLOTS, BLK, BLK)
 
@@ -260,27 +278,24 @@
         dst = zb.at[a, way, r, pl.ds(h * H, H)]
         return rcopy(src, dst, zs.at[i], zr.at[i], zdev(1 if way == 0 else -1))
 
-    def z_first(a):
-        for r in (3, 2):
-            for way in range(2):
-                h = way if r == 3 else 1 - way
-                src, total = chip_sum(a, r + 1 if way == 0 else -(r + 1), h)
-                src[...] = total.astype(BF)
-                go(z_copy(src, a, way, r, h))
-
-    def z_next(a, r, only=None):
-        for h2 in range(2):
-            for way in range(2):
-                h = way if h2 == 0 else 1 - way
-                if r == 3 and h2 == 1:
-                    continue
-                buf = zb.at[a, way, r, pl.ds(h * H, H)]
-                z_copy(buf, a, way, r, h).wait_recv()
-                src, total = chip_sum(a, r if way == 0 else -r, h)
-                buf[...] = (buf[...].astype(F32) + total).astype(BF)
-                go(z_copy(buf, a, way, r - 1, h))
-
-    def z_last(a, dst):
+    def z_first(a, r):
+        for way in range(2):
+            h = way if r == 3 else 1 - way
+            src, total = chip_sum(a, r + 1 if way == 0 else -(r + 1), h)
+            src[...] = total.astype(BF)
+            go(z_copy(src, a, way, r, h))
+
+    def z_next(a, r, i):
+        for way in range(2):
+            h = way if i == 0 else 1 - way
+            buf = zb.at[a, way, r, pl.ds(h * H, H)]
+            z_copy(buf, a, way, r, h).wait_recv()
+            src, total = chip_sum(a, r if way == 0 else -r, h)
+            buf[...] = (buf[...].astype(F32) + total).astype(BF)
+            go(z_copy(buf, a, way, r - 1, h))
+
+    def z_last(a):
+        dst = (out_ref, ing_ref)[a]
         for h in range(2):
             src, total = chip_sum(a, 0, h)
             for way in range(2):
@@ -295,162 +310,117 @@
     def at4(i):
         return (i + 2 * NQ) % NQ
 
-    def lines(p):
-        return pl.ds(p * W, W)
-
-    def w_dst(a, ph, p, m):
-        return (wp if ph == 0 else w2).at[a, p, m]
-
-    def w_copy(src, a, ph, p, m):
+    def lines(p, g):
+        lo, hi = GROUPS[g]
+        return pl.ds(p * W + lo * 16, (hi - lo) * 16)
+
+    def w_dst(a, ph, p, g, m):
+        return wp.at[a, m, :, lines(p, g)] if ph == 0 else w2.at[a, m, lines(p, g)]
+
+    def w_copy(src, a, ph, p, g, m):
         sign = 1 if p % 2 == 0 else -1
-        i = ((a * 2 + ph) * 4 + p) * 3 + m
+        i = (((a * 2 + ph) * 2 + g) * 4 + p) * 3 + m
         return rcopy(
-            src, w_dst(a, ph, p, m), xs.at[i], xr.at[i], devs[p // 2][ph](sign if m < 2 else -sign)
+            src, w_dst(a, ph, p, g, m), xs.at[i], xr.at[i], devs[p // 2][ph](sign if m < 2 else -sign)
         )
 
-    def w_src(a, ph, p, step):
+    def w_src(a, ph, p, g, step):
         c = at4(coords[p // 2][ph] + step * (1 if p % 2 == 0 else -1))
         if ph == 0:
-            return wgt.at[a, c, :, lines(p)]
-        return red.at[a, c, lines(p)]
-
-    def w_start(a, ph, *ps):
-        for p in ps:
-            go(w_copy(w_src(a, ph, p, 2), a, ph, p, 0))
-        for p in ps:
-            go(w_copy(w_src(a, ph, p, -1), a, ph, p, 2))
-
-    def w_pass(a, ph, *ps):
-        for p in ps:
-            buf = w_dst(a, ph, p, 0)
-            w_copy(buf, a, ph, p, 0).wait_recv()
-            mine = w_src(a, ph, p, 1)
+            return wgt.at[a, c, :, lines(p, g)]
+        return red.at[a, c, lines(p, g)]
+
+    def w_send(a, ph, g, m):
+        for p in range(4):
+            go(w_copy(w_src(a, ph, p, g, 2 if m == 0 else -1), a, ph, p, g, m))
+
+    def w_pass(a, ph, g):
+        for p in range(4):
+            buf = w_dst(a, ph, p, g, 0)
+            w_copy(buf, a, ph, p, g, 0).wait_recv()
+            mine = w_src(a, ph, p, g, 1)
             buf[...] = (buf[...].astype(F32) + mine[...].astype(F32)).astype(BF)
-            go(w_copy(buf, a, ph, p, 1))
-
-    def w_done(a, ph, p, dst):
-        total = w_src(a, ph, p, 0)[...].astype(F32)
-        for m in (2, 1):
-            w_copy(w_dst(a, ph, p, m), a, ph, p, m).wait_recv()
-            total = total + w_dst(a, ph, p, m)[...].astype(F32)
-        if ph == 0:
-            red[a, :, lines(p)] = total.astype(BF)
-        else:
-            dst[lines(p), :] = total
-
-    def w_turn(a, *ps):
-        for p in ps:
-            w_done(a, 0, p, None)
-            w_start(a, 1, p)
-
-    def store(a, row, both):
+            go(w_copy(buf, a, ph, p, g, 1))
+
+    def w_done(a, ph, g):
+        dst = (gwout_ref, gwin_ref)[a]
+        lo, hi = GROUPS[g]
+        for p in range(4):
+            total = w_src(a, ph, p, g, 0)[...].astype(F32)
+            for m in (2, 1):
+                buf = w_dst(a, ph, p, g, m)
+                w_copy(buf, a, ph, p, g, m).wait_recv()
+                total = total + buf[...].astype(F32)
+            if ph == 0:
+                red[a, :, lines(p, g)] = total.astype(BF)
+            else:
+                for n in range(lo, hi):
+                    dst[n * 64 + p * 16:n * 64 + p * 16 + 16, :] = total[(n - lo) * 16:(n - lo) * 16 + 16]
+
+    def store(a, n, p, both):
         both = both.astype(BF).reshape(NQ, NQ, 16, BLK)
-        if row < 2 * W:
+        row = p * W + n * 16
+        if p < 2:
             wgt[a, :, :, row:row + 16, :] = both
         else:
-            for p in range(NQ):
-                for q in range(NQ):
-                    wgt[a, p, q, row:row + 16, :] = both[q, p]
+            for i in range(NQ):
+                for j in range(NQ):
+                    wgt[a, i, j, row:row + 16, :] = both[j, i]
 
     def backward_hidden():
         for n in range(ROWS):
             gh = dot(cat([wout[n * SLOTS + s] for s in range(SLOTS)], 1), listed(gg, n))
             gpre[n] = (gh * dgelu[n]).astype(BF)
 
-    def backward_out(lo, hi):
-        for n in range(lo, hi):
+    def backward_out(g):
+        for n in range(*GROUPS[g]):
             gw = lax.dot_general(hid[n], listed(gg, n), NT, preferred_element_type=F32)
-            for s in range(0, SLOTS, 2):
-                one = gw[:, s * BLK:(s + 1) * BLK].reshape(16, 8, BLK)
-                two = gw[:, (s + 1) * BLK:(s + 2) * BLK].reshape(16, 8, BLK)
-                store(0, (n * SLOTS + s) * 8, cat([one, two], 1))
-
-    def backward_in(lo, hi):
-        for n in range(lo, hi):
+            for p in range(4):
+                one = gw[:, 2 * p * BLK:(2 * p + 1) * BLK].reshape(16, 8, BLK)
+                two = gw[:, (2 * p + 1) * BLK:(2 * p + 2) * BLK].reshape(16, 8, BLK)
+                store(0, n, p, cat([one, two], 1))
+
+    def backward_in(g):
+        for n in range(*GROUPS[g]):
             gw = lax.dot_general(listed(xg, n), gpre[n], NT, preferred_element_type=F32)
             gw = gw.reshape(SLOTS, 16, 8, BLK)
-            for s in range(0, SLOTS, 2):
-                store(1, (n * SLOTS + s) * 8, cat([gw[s], gw[s + 1]], 1))
+            for p in range(4):
+                store(1, n, p, cat([gw[2 * p], gw[2 * p + 1]], 1))
 
     waited = [0]
 
     def drain(upto):
+        if isinstance(upto, tuple):
+            upto = marks[PLAN.index(upto)]
         for c in sends[waited[0]:upto]:
             c.wait_send()
         waited[0] = upto
 
+    def make():
+        local[4].wait()
+        local[5].wait()
+        make_table()
+        tcopy.start()
+
+    def turned():
+        local[2].wait()
+        local[3].wait()
+        turn()
+
+    tcopy = pltpu.make_async_copy(tabv, tab, lsem.at[4])
+    tasks = {
+        "ag0": ag_first, "agw": ag_wait, "agf": ag_pass, "own": ag_own, "ags": ag_sib, "gath": gathered,
+        "tabl": make, "turn": turned, "H": hidden, "GH": backward_hidden, "GO": backward_out,
+        "GI": backward_in, "S": shares, "P": place, "zf": z_first, "zn": z_next, "zl": z_last,
+        "wm": w_send, "wp": w_pass, "wd": w_done, "tab": tcopy.wait, "drain": drain,
+    }
+    marks = []
     local[0].wait()
     local[1].wait()
     pl.semaphore_wait(barrier, 7)
-    ag_start(0)
-    ag_start(1)
-    local[4].wait()
-    local[5].wait()
-    make_table()
-    tcopy = pltpu.make_async_copy(tabv, tab, lsem.at[4])
-    tcopy.start()
-    local[2].wait()
-    local[3].wait()
-    turn()
-    tcopy.wait()
-    for i in range(2):
-        ag_take(0, 0, i)
-    for i in range(2):
-        ag_take(1, 0, i)
-    for i in range(2):
-        ag_take(0, 1, i)
-    ag_take(1, 1, 0)
-    ag_take(1, 1, 1, on=False)
-    ag_take(0, 2, 0)
-    ag_pass(1, 1, 1)
-    ag_take(0, 2, 1)
-    ag_take(1, 2, 0)
-    ag_take(0, 3, 0)
-    ag_take(1, 2, 1)
-    ag_take(1, 3, 0)
-    gather_sends = len(sends)
-    gathered(0)
-    hidden(0, ROWS)
-    gathered(1)
-    backward_hidden()
-    backward_out(0, 4)
-    w_start(0, 0, 0, 1)
-    backward_out(4, 7)
-    w_start(0, 0, 2, 3)
-    shares(woutt, hid)
-    place(0)
-    shares(win, gpre)
-    place(1)
-    z_first(0)
-    backward_in(0, 4)
-    w_start(1, 0, 0, 1)
-    z_first(1)
-    backward_in(4, 7)
-    w_start(1, 0, 2, 3)
-    w_pass(0, 0, 0, 1, 2, 3)
-    drain(gather_sends)
-    z_next(0, 3)
-    z_next(1, 3)
-    w_pass(1, 0, 0, 1)
-    first_sends = len(sends)
-    z_next(0, 2)
-    w_pass(1, 0, 2, 3)
-    z_next(1, 2)
-    w_turn(0, 0, 1, 2, 3)
-    drain(first_sends)
-    z_next(0, 1)
-    z_next(1, 1)
-    w_turn(1, 0, 1, 2, 3)
-    w_pass(0, 1, 0, 1, 2, 3)
-    second_sends = len(sends)
-    z_last(0, out_ref)
-    w_pass(1, 1, 0, 1, 2, 3)
-    z_last(1, ing_ref)
-    for p in range(4):
-        w_done(0, 1, p, gwout_ref)
-    drain(second_sends)
-    for p in range(4):
-        w_done(1, 1, p, gwin_ref)
+    for name, *args in PLAN:
+        marks.append(len(sends))
+        tasks[name](*args)
     drain(len(sends))
 
 
@@ -490,9 +460,9 @@
             pltpu.VMEM((2, NZ, CH, BLK), BF),
             pltpu.VMEM((2, 2, 4, CH, BLK), BF),
             pltpu.VMEM((2, NQ, NQ, CH, BLK), BF),
-            pltpu.VMEM((2, 4, 3, NQ, W, BLK), BF),
+            pltpu.VMEM((2, 3, NQ, CH, BLK), BF),
             pltpu.VMEM((2, NQ, CH, BLK), BF),
-            pltpu.VMEM((2, 4, 3, W, BLK), BF),
+            pltpu.VMEM((2, 3, CH, BLK), BF),
             pltpu.VMEM((8, 128), jnp.int32),
             pltpu.SMEM((8, 128), jnp.int32),
             pltpu.SMEM((ROWS, SLOTS), jnp.int32),
@@ -502,7 +472,7 @@
             dma((18,)), dma((18,)),
             dma((16,)), dma((16,)),
             dma((32,)), dma((32,)),
-            dma((48,)), dma((48,)),
+            dma((96,)), dma((96,)),
         ],
         compiler_params=pltpu.CompilerParams(
             collective_id=0, has_side_effects=True, vmem_limit_bytes=63 * 1024 * 1024

time: 62.9 us -> 63.4 us (level)
  no operation moved by 1% of the time
where the time goes in v5:
time: 63.4 us; the launch traced here: 63.3 us
  Pallas kernels  62.6 us (99%)
  between operations  0.64 us (1%)
    pallas_call x1, Pallas kernels, on_device(): pl.pallas_call(kernel, out_shape=shapes, in_specs=[hbm] * 6, out_specs=(v...  60.6 us
    pallas_call x1, Pallas kernels, on_device(): pl.pallas_call(finish, out_shape=shapes, in_specs=[vm] * 4, out_specs=(vm...  2.01 us

profile of v5, /device:TPU:32, one launch (start us, length us, event | category | flops | bytes accessed | tf_op | source)
XLA Modules:
  0.0 63.3 jit_solution(15246059552801432326)
XLA Ops:
  0.6 60.6 %shard_map.93 = (bf16[448,128]{1,0:T(8,128)(2,1)}, bf16[448,128]{1,0:T(8,128)(2,1)}, f32[448,128]{1,0:T(8,128)}, f32[448,128]{1,0:T(8,128)}) custom-call(s32[7,8]{1,0:T(8,128)} %col_hbm.1, s32[7]{0:T(128)} %cnt_hbm.1, bf16[7,64,128]{2,1,0:T(8,128)(2,1)} %bitcast.16, bf16[7,64,128]{2,1,0:T(8,128)(2,1)} %bitcast.17, bf16[56,128,128]{2,1,0:T(8,128)(2,1)} %bitcast.12, ...), custom_call_target="tpu_custom_call" | custom-call | flops 1409286144 | bytes 8000000 | tf_op jit(solution)/shard_map/pallas_call | solution.py:442
  61.3 2.0 %shard_map.94 = (bf16[448,128]{1,0:T(8,128)(2,1)}, bf16[448,128]{1,0:T(8,128)(2,1)}, f32[448,128]{1,0:T(8,128)}, f32[448,128]{1,0:T(8,128)}) custom-call(bf16[448,128]{1,0:T(8,128)(2,1)} %get-tuple-element.12.refs_0_, bf16[448,128]{1,0:T(8,128)(2,1)} %get-tuple-element.13.refs_1_, f32[448,128]{1,0:T(8,128)} %get-tuple-element.14.refs_2_, ...), custom_call_target="tpu_custom_call" | custom-call | bytes 1400000 | tf_op jit(solution)/shard_map/pallas_call | solution.py:486

commit v6 on v5

--- a/solution.py
+++ b/solution.py
@@ -66,16 +66,18 @@
     yy, xx = dp // NQ, dp % NQ
     z, core = tn // 2, tn % 2
 
-    def zdev(step):
-        return {"dp": dp, "tensor": ((z + step + NZ) % NZ) * 2 + core}
-
-    sdev = {"dp": dp, "tensor": z * 2 + (1 - core)}
-
-    def ydev(step):
-        return {"dp": ((yy + step + NQ) % NQ) * NQ + xx, "tensor": tn}
-
-    def xdev(step):
-        return {"dp": yy * NQ + (xx + step + NQ) % NQ, "tensor": tn}
+    zat = [z] + [(z + i) % NZ for i in range(1, NZ)]
+    yat = [yy] + [(yy + i) % NQ for i in range(1, NQ)]
+    xat = [xx] + [(xx + i) % NQ for i in range(1, NQ)]
+    other = 1 - core
+    chunk = [[zat[i] * 2 + core for i in range(NZ)], [zat[i] * 2 + other for i in range(NZ)]]
+    first = [[t * U for t in half] for half in chunk]
+    zdevs = {i: {"dp": dp, "tensor": chunk[0][i % NZ]} for i in (1, -1)}
+    sdev = {"dp": dp, "tensor": chunk[1][0]}
+    ydevs = {i: {"dp": yat[i % NQ] * NQ + xx, "tensor": tn} for i in (1, -1)}
+    xdevs = {i: {"dp": yy * NQ + xat[i % NQ], "tensor": tn} for i in (1, -1)}
+    zdev, ydev, xdev = zdevs.get, ydevs.get, xdevs.get
+    own_row, sib_row = core * CH, other * CH
 
     sends = []
 
@@ -94,7 +96,7 @@
         pl.semaphore_signal(barrier, inc=1, device_id=dev, device_id_type=MESH)
 
     fields = (xg, gg)
-    own = pl.ds(tn * U, U)
+    own = pl.ds(first[0][0], U)
     local = [
         pltpu.make_async_copy(x_hbm, xg.at[own], lsem.at[0]),
         pltpu.make_async_copy(g_hbm, gg.at[own], lsem.at[1]),
@@ -154,21 +156,21 @@
         ref[2 * DB + 1] = jnp.zeros((64, BLK), BF)
     run[NB] = jnp.zeros((BLK, BLK), BF)
 
-    def piece(ref, t, lo=0, n=U):
-        return ref.at[pl.ds(t * U + lo, n)]
+    def piece(ref, side, step, lo=0, n=U):
+        return ref.at[pl.ds(first[side][step % NZ] + lo, n)]
 
     def wrap(step):
-        return (z + step + 2 * NZ) % NZ
+        return zat[step % NZ]
 
     def ag_copy(a, way, k, h):
         step = -(k + 1) if way == 0 else k + 1
-        v = piece(fields[a], wrap(step) * 2 + core, *SPAN[h])
+        v = piece(fields[a], 0, step, *SPAN[h])
         i = ((a * 2 + way) * 4 + k) * 2 + h
         return rcopy(v, v, ag_s.at[i], ag_r.at[i], zdev(1 if way == 0 else -1))
 
     def ag_send(a, way, k, h):
         step = -k if way == 0 else k
-        v = piece(fields[a], wrap(step) * 2 + core, *SPAN[h])
+        v = piece(fields[a], 0, step, *SPAN[h])
         i = ((a * 2 + way) * 4 + k) * 2 + h
         return rcopy(v, v, ag_s.at[i], ag_r.at[i], zdev(1 if way == 0 else -1))
 
@@ -182,7 +184,7 @@
 
     def sb_copy(a, j, mine):
         step, span = sb_place(j)
-        v = piece(fields[a], wrap(step) * 2 + (core if mine else 1 - core), *span)
+        v = piece(fields[a], 0 if mine else 1, step, *span)
         return rcopy(v, v, sb_s.at[a * 9 + j], sb_r.at[a * 9 + j], sdev)
 
     def part_of(way, i):
@@ -247,7 +249,7 @@
 
     def sib_copy(a, zz):
         i = a * NZ + zz
-        src = part.at[a, zz, pl.ds(pl.multiple_of((1 - core) * CH, 64), CH)]
+        src = part.at[a, zz, pl.ds(pl.multiple_of(sib_row, 64), CH)]
         return rcopy(src, sib.at[a, zz], ss_s.at[i], ss_r.at[i], sdev)
 
     def place(a):
@@ -270,7 +272,7 @@
         if (a, step % NZ) not in met:
             met.add((a, step % NZ))
             sib_copy(a, zz).wait_recv()
-        src = part.at[a, zz, pl.ds(pl.multiple_of(core * CH + h * H, 32), H)]
+        src = part.at[a, zz, pl.ds(pl.multiple_of(own_row + h * H, 32), H)]
         return src, src[...].astype(F32) + sib[a, zz, h * H:(h + 1) * H].astype(F32)
 
     def z_copy(src, a, way, r, h):
@@ -304,11 +306,8 @@
                 total = total + buf[...].astype(F32)
             dst[h * H:(h + 1) * H, :] = total.astype(BF)
 
-    coords = ((yy, xx), (xx, yy))
+    coords = ((yat, xat), (xat, yat))
     devs = ((ydev, xdev), (xdev, ydev))
-
-    def at4(i):
-        return (i + 2 * NQ) % NQ
 
     def lines(p, g):
         lo, hi = GROUPS[g]
@@ -325,7 +324,7 @@
         )
 
     def w_src(a, ph, p, g, step):
-        c = at4(coords[p // 2][ph] + step * (1 if p % 2 == 0 else -1))
+        c = coords[p // 2][ph][(step if p % 2 == 0 else -step) % NQ]
         if ph == 0:
             return wgt.at[a, c, :, lines(p, g)]
         return red.at[a, c, lines(p, g)]

time: 63.4 us -> 63.4 us (level)
  no operation moved by 1% of the time
where the time goes in v6:
time: 63.4 us; the launch traced here: 63.3 us
  Pallas kernels  62.7 us (99%)
  between operations  0.64 us (1%)
    pallas_call x1, Pallas kernels, on_device(): pl.pallas_call(kernel, out_shape=shapes, in_specs=[hbm] * 6, out_specs=(v...  60.6 us
    pallas_call x1, Pallas kernels, on_device(): pl.pallas_call(finish, out_shape=shapes, in_specs=[vm] * 4, out_specs=(vm...  2.01 us

profile of v6, /device:TPU:32, one launch (start us, length us, event | category | flops | bytes accessed | tf_op | source)
XLA Modules:
  0.0 63.3 jit_solution(9810956149811956687)
XLA Ops:
  0.6 60.6 %shard_map.93 = (bf16[448,128]{1,0:T(8,128)(2,1)}, bf16[448,128]{1,0:T(8,128)(2,1)}, f32[448,128]{1,0:T(8,128)}, f32[448,128]{1,0:T(8,128)}) custom-call(s32[7,8]{1,0:T(8,128)} %col_hbm.1, s32[7]{0:T(128)} %cnt_hbm.1, bf16[7,64,128]{2,1,0:T(8,128)(2,1)} %bitcast.16, bf16[7,64,128]{2,1,0:T(8,128)(2,1)} %bitcast.17, bf16[56,128,128]{2,1,0:T(8,128)(2,1)} %bitcast.12, ...), custom_call_target="tpu_custom_call" | custom-call | flops 1409286144 | bytes 8000000 | tf_op jit(solution)/shard_map/pallas_call | solution.py:441
  61.3 2.0 %shard_map.94 = (bf16[448,128]{1,0:T(8,128)(2,1)}, bf16[448,128]{1,0:T(8,128)(2,1)}, f32[448,128]{1,0:T(8,128)}, f32[448,128]{1,0:T(8,128)}) custom-call(bf16[448,128]{1,0:T(8,128)(2,1)} %get-tuple-element.12.refs_0_, bf16[448,128]{1,0:T(8,128)(2,1)} %get-tuple-element.13.refs_1_, f32[448,128]{1,0:T(8,128)} %get-tuple-element.14.refs_2_, ...), custom_call_target="tpu_custom_call" | custom-call | bytes 1400000 | tf_op jit(solution)/shard_map/pallas_call | solution.py:485

commit v7 on v6

--- a/solution.py
+++ b/solution.py
@@ -17,32 +17,29 @@
 SPAN = ((0, 4), (4, 3))
 H = 224
 W = 112
-GROUPS = ((0, 4), (4, 7))
+GROUPS = ((0, 7),)
 BF = jnp.bfloat16
 F32 = jnp.float32
 MESH = pl.DeviceIdType.MESH
 C0 = 0.7978845608028654
 C1 = 0.044715
 ORDER = (4, 3, -3, 2, -2, 1, -1, 0)
+FIRST = 3
 NT = (((1,), (1,)), ((), ()))
 PLAN = (
-    ("ag0", 0, 0), ("own", 0), ("ag0", 0, 1), ("ag0", 1, 0), ("own", 1), ("agw", 0, 0, 0), ("agf", 0, 0, 0),
-    ("agw", 0, 0, 1), ("agf", 0, 0, 1), ("agw", 1, 0, 0), ("ag0", 1, 1), ("tabl",), ("agf", 1, 0, 0),
-    ("agw", 0, 1, 0), ("agf", 0, 1, 0), ("turn",), ("agw", 0, 1, 1), ("agf", 0, 1, 1), ("ags", 0, 0),
-    ("agw", 1, 0, 1), ("ags", 1, 0), ("ags", 0, 1), ("agf", 1, 0, 1), ("agw", 0, 2, 0), ("agf", 0, 2, 0),
-    ("agw", 1, 1, 0), ("agw", 0, 2, 1), ("agf", 1, 1, 0), ("agw", 1, 1, 1), ("ags", 1, 1), ("ags", 0, 2),
-    ("agf", 1, 1, 1), ("agw", 0, 3, 0), ("ags", 0, 3), ("agw", 1, 2, 0), ("agf", 1, 2, 0), ("gath", 0), ("H", 0, 4),
-    ("agw", 1, 2, 1), ("ags", 1, 2), ("H", 4, 7), ("agw", 1, 3, 0), ("ags", 1, 3), ("S", 0), ("tab",), ("P", 0),
-    ("gath", 1), ("GO", 0), ("wm", 0, 0, 0, 0), ("GO", 1), ("wm", 0, 0, 1, 0), ("zf", 0, 3), ("wm", 0, 0, 0, 2),
-    ("GH",), ("zf", 0, 2), ("GI", 0), ("wm", 1, 0, 0, 2), ("S", 1), ("wm", 1, 0, 0, 0), ("zn", 0, 3, 0), ("P", 1),
-    ("zn", 0, 2, 1), ("wm", 0, 0, 1, 2), ("GI", 1), ("wm", 1, 0, 1, 0), ("zf", 1, 3), ("zn", 0, 2, 0), ("zf", 1, 2),
-    ("wp", 0, 0, 1), ("wp", 1, 0, 0), ("wp", 0, 0, 0), ("wm", 1, 0, 1, 2), ("zn", 1, 3, 0), ("zn", 0, 1, 0),
-    ("wp", 1, 0, 1), ("zn", 1, 2, 1), ("wd", 1, 0, 0), ("wm", 1, 1, 0, 0), ("zn", 1, 2, 0), ("zn", 0, 1, 1),
-    ("wd", 0, 0, 0), ("wm", 0, 1, 0, 0), ("wd", 0, 0, 1), ("wm", 0, 1, 1, 0), ("wd", 1, 0, 1), ("wm", 1, 1, 1, 0),
-    ("zn", 1, 1, 1), ("wm", 1, 1, 0, 2), ("drain", ("GI", 1)), ("wp", 1, 1, 0), ("wm", 0, 1, 0, 2),
-    ("wm", 0, 1, 1, 2), ("zn", 1, 1, 0), ("wp", 0, 1, 0), ("wp", 0, 1, 1), ("wm", 1, 1, 1, 2), ("wp", 1, 1, 1),
-    ("drain", ("wd", 1, 0, 0)), ("zl", 0), ("wd", 0, 1, 0), ("drain", ("wp", 1, 1, 0)), ("wd", 1, 1, 0),
-    ("wd", 0, 1, 1), ("zl", 1), ("wd", 1, 1, 1),
+    ("ag0", 0, 0), ("ag0", 0, 1), ("turn",), ("ag0", 1, 0), ("ag0", 1, 1), ("agw", 0, 0, 0), ("agf", 0, 0, 0),
+    ("agw", 0, 0, 1), ("agw", 1, 0, 0), ("agf", 1, 0, 0), ("agf", 0, 0, 1), ("agw", 0, 1, 0), ("agf", 0, 1, 0),
+    ("agw", 1, 0, 1), ("agf", 1, 0, 1), ("own", 0), ("agw", 1, 1, 0), ("agf", 1, 1, 0), ("tabl",), ("ags", 1, 0),
+    ("agw", 0, 1, 1), ("own", 1), ("ags", 0, 0), ("agf", 0, 1, 1), ("agw", 0, 2, 0), ("agf", 0, 2, 0),
+    ("agw", 1, 1, 1), ("ags", 0, 1), ("agf", 1, 1, 1), ("agw", 1, 2, 0), ("agf", 1, 2, 0), ("agw", 0, 2, 1),
+    ("ags", 0, 2), ("ags", 1, 1), ("agw", 0, 3, 0), ("ags", 0, 3), ("agw", 1, 2, 1), ("ags", 1, 2), ("agw", 1, 3, 0),
+    ("ags", 1, 3), ("gath", 0), ("H", 0, 4), ("H", 4, 7), ("S", 0), ("tab",), ("P", 0), ("gath", 1), ("GH",),
+    ("GO", 0), ("wm", 0, 0, 0, 0), ("S", 1), ("P", 1), ("zf", 0), ("wm", 0, 0, 0, 2), ("GI", 0), ("zf", 1),
+    ("wm", 1, 0, 0, 0), ("wm", 1, 0, 0, 2), ("zn", 0, 3), ("zn", 1, 3), ("wp", 0, 0, 0), ("wp", 1, 0, 0),
+    ("zn", 0, 2), ("zn", 1, 2), ("wd", 0, 0, 0), ("wm", 0, 1, 0, 0), ("wm", 0, 1, 0, 2), ("zn", 0, 1),
+    ("wd", 1, 0, 0), ("wm", 1, 1, 0, 0), ("zn", 1, 1), ("wp", 0, 1, 0), ("wm", 1, 1, 0, 2), ("wp", 1, 1, 0),
+    ("ag_sent",), ("w_sent", 0, 0), ("w_sent", 1, 0), ("wd", 0, 1, 0), ("zl", 0), ("zl", 1), ("wd", 1, 1, 0),
+    ("z_sent", 0), ("z_sent", 1), ("w_sent", 0, 1), ("w_sent", 1, 1),
 )
 
 
@@ -79,7 +76,11 @@
     zdev, ydev, xdev = zdevs.get, ydevs.get, xdevs.get
     own_row, sib_row = core * CH, other * CH
 
-    sends = []
+    def landed(view, rsem):
+        rcopy(view, view, lsem.at[0], rsem, sdev).wait_recv()
+
+    def sent(view, ssem):
+        rcopy(view, view, ssem, lsem.at[0], sdev).wait_send()
 
     def rcopy(src, dst, ssem, rsem, dev):
         return pltpu.make_async_remote_copy(
@@ -89,7 +90,6 @@
 
     def go(copy):
         copy.start()
-        sends.append(copy)
 
     barrier = pltpu.get_barrier_semaphore()
     for dev in (sdev, zdev(1), zdev(-1), xdev(1), xdev(-1), ydev(1), ydev(-1)):
@@ -166,13 +166,13 @@
         step = -(k + 1) if way == 0 else k + 1
         v = piece(fields[a], 0, step, *SPAN[h])
         i = ((a * 2 + way) * 4 + k) * 2 + h
-        return rcopy(v, v, ag_s.at[i], ag_r.at[i], zdev(1 if way == 0 else -1))
+        return rcopy(v, v, ag_s.at[a], ag_r.at[i], zdev(1 if way == 0 else -1))
 
     def ag_send(a, way, k, h):
         step = -k if way == 0 else k
         v = piece(fields[a], 0, step, *SPAN[h])
         i = ((a * 2 + way) * 4 + k) * 2 + h
-        return rcopy(v, v, ag_s.at[i], ag_r.at[i], zdev(1 if way == 0 else -1))
+        return rcopy(v, v, ag_s.at[a], ag_r.at[i], zdev(1 if way == 0 else -1))
 
     def sb_place(j):
         if j == 0:
@@ -185,7 +185,7 @@
     def sb_copy(a, j, mine):
         step, span = sb_place(j)
         v = piece(fields[a], 0 if mine else 1, step, *span)
-        return rcopy(v, v, sb_s.at[a * 9 + j], sb_r.at[a * 9 + j], sdev)
+        return rcopy(v, v, sb_s.at[a], sb_r.at[a], sdev)
 
     def part_of(way, i):
         return way if i == 0 else 1 - way
@@ -210,8 +210,7 @@
             go(sb_copy(a, 7 + way if k == 3 else 1 + 3 * way + k, True))
 
     def gathered(a):
-        for j in range(9):
-            sb_copy(a, j, False).wait_recv()
+        landed(fields[a].at[pl.ds(0, NZ * U)], sb_r.at[a])
 
     def turn():
         def body(n, carry):
@@ -247,10 +246,10 @@
         for n in range(ROWS):
             cbuf[n * SLOTS:(n + 1) * SLOTS] = dot(tall(w, n), act[n]).reshape(SLOTS, BLK, BLK)
 
-    def sib_copy(a, zz):
-        i = a * NZ + zz
-        src = part.at[a, zz, pl.ds(pl.multiple_of(sib_row, 64), CH)]
-        return rcopy(src, sib.at[a, zz], ss_s.at[i], ss_r.at[i], sdev)
+    def sib_copy(a, g):
+        span = pl.ds(0, FIRST) if g == 0 else pl.ds(FIRST, NZ - FIRST)
+        src = part.at[a, span, pl.ds(pl.multiple_of(sib_row, 64), CH)]
+        return rcopy(src, sib.at[a, span], ss_s.at[a], ss_r.at[a * 2 + g], sdev)
 
     def place(a):
         def add(r, acc):
@@ -259,51 +258,58 @@
             return acc
 
         lax.fori_loop(0, NB, add, jnp.zeros((BLK, BLK), F32), unroll=4)
-        for step in ORDER:
+        for j, step in enumerate(ORDER):
             zz = wrap(step)
             for k in range(7):
-                part[a, zz, BLK * k:BLK * (k + 1), :] = run[tab[2, zz * 7 + k]]
-            go(sib_copy(a, zz))
+                part[a, j, BLK * k:BLK * (k + 1), :] = run[tab[2, zz * 7 + k]]
+            if j == FIRST - 1:
+                go(sib_copy(a, 0))
+        go(sib_copy(a, 1))
 
     met = set()
 
     def chip_sum(a, step, h):
-        zz = wrap(step)
-        if (a, step % NZ) not in met:
-            met.add((a, step % NZ))
-            sib_copy(a, zz).wait_recv()
-        src = part.at[a, zz, pl.ds(pl.multiple_of(own_row + h * H, 32), H)]
-        return src, src[...].astype(F32) + sib[a, zz, h * H:(h + 1) * H].astype(F32)
-
-    def z_copy(src, a, way, r, h):
-        i = ((a * 2 + way) * 4 + r) * 2 + h
-        dst = zb.at[a, way, r, pl.ds(h * H, H)]
-        return rcopy(src, dst, zs.at[i], zr.at[i], zdev(1 if way == 0 else -1))
-
-    def z_first(a, r):
+        j = ORDER.index(step if step in ORDER else step + NZ)
+        g = 0 if j < FIRST else 1
+        if (a, g) not in met:
+            met.add((a, g))
+            sib_copy(a, g).wait_recv()
+        src = part.at[a, j, pl.ds(pl.multiple_of(own_row + h * H, 32), H)]
+        return src, src[...].astype(F32) + sib[a, j, h * H:(h + 1) * H].astype(F32)
+
+    def z_copy(src, a, way, r):
+        dst = zb.at[a, way, r]
+        if r == 3:
+            dst = dst.at[pl.ds(way * H, H)]
+        return rcopy(src, dst, zs.at[a], zr.at[a * 4 + r], zdev(1 if way == 0 else -1))
+
+    def z_first(a):
         for way in range(2):
-            h = way if r == 3 else 1 - way
-            src, total = chip_sum(a, r + 1 if way == 0 else -(r + 1), h)
+            src, total = chip_sum(a, 4 if way == 0 else -4, way)
             src[...] = total.astype(BF)
-            go(z_copy(src, a, way, r, h))
-
-    def z_next(a, r, i):
+            go(z_copy(src, a, way, 3))
+
+    def z_next(a, r):
+        if r == 3:
+            landed(zb.at[a, :, r, pl.ds(0, H)], zr.at[a * 4 + r])
+        else:
+            landed(zb.at[a, :, r], zr.at[a * 4 + r])
         for way in range(2):
-            h = way if i == 0 else 1 - way
-            buf = zb.at[a, way, r, pl.ds(h * H, H)]
-            z_copy(buf, a, way, r, h).wait_recv()
-            src, total = chip_sum(a, r if way == 0 else -r, h)
-            buf[...] = (buf[...].astype(F32) + total).astype(BF)
-            go(z_copy(buf, a, way, r - 1, h))
+            for h in range(2):
+                src, total = chip_sum(a, r if way == 0 else -r, h)
+                buf = zb.at[a, way, r, pl.ds(h * H, H)]
+                if r < 3 or h == way:
+                    total = total + buf[...].astype(F32)
+                buf[...] = total.astype(BF)
+            go(z_copy(zb.at[a, way, r], a, way, r - 1))
 
     def z_last(a):
         dst = (out_ref, ing_ref)[a]
+        landed(zb.at[a, :, 0], zr.at[a * 4])
         for h in range(2):
             src, total = chip_sum(a, 0, h)
             for way in range(2):
-                buf = zb.at[a, way, 0, pl.ds(h * H, H)]
-                z_copy(buf, a, way, 0, h).wait_recv()
-                total = total + buf[...].astype(F32)
+                total = total + zb[a, way, 0, h * H:(h + 1) * H].astype(F32)
             dst[h * H:(h + 1) * H, :] = total.astype(BF)
 
     coords = ((yat, xat), (xat, yat))
@@ -318,10 +324,20 @@
 
     def w_copy(src, a, ph, p, g, m):
         sign = 1 if p % 2 == 0 else -1
-        i = (((a * 2 + ph) * 2 + g) * 4 + p) * 3 + m
+        i = ((a * 2 + ph) * len(GROUPS) + g) * 2 + (0 if m == 0 else 1)
         return rcopy(
-            src, w_dst(a, ph, p, g, m), xs.at[i], xr.at[i], devs[p // 2][ph](sign if m < 2 else -sign)
+            src, w_dst(a, ph, p, g, m), xs.at[a * 2 + ph], xr.at[i], devs[p // 2][ph](sign if m < 2 else -sign)
         )
+
+    def w_landed(a, ph, g, m):
+        i = ((a * 2 + ph) * len(GROUPS) + g) * 2 + (0 if m == 0 else 1)
+        lo, hi = GROUPS[g]
+        span = pl.ds(0, (hi - lo) * 64)
+        if m == 0:
+            view = wp.at[a, 0, :, span] if ph == 0 else w2.at[a, 0, span]
+        else:
+            view = wp.at[a, pl.ds(1, 2), :, span] if ph == 0 else w2.at[a, pl.ds(1, 2), span]
+        landed(view, xr.at[i])
 
     def w_src(a, ph, p, g, step):
         c = coords[p // 2][ph][(step if p % 2 == 0 else -step) % NQ]
@@ -334,9 +350,9 @@
             go(w_copy(w_src(a, ph, p, g, 2 if m == 0 else -1), a, ph, p, g, m))
 
     def w_pass(a, ph, g):
+        w_landed(a, ph, g, 0)
         for p in range(4):
             buf = w_dst(a, ph, p, g, 0)
-            w_copy(buf, a, ph, p, g, 0).wait_recv()
             mine = w_src(a, ph, p, g, 1)
             buf[...] = (buf[...].astype(F32) + mine[...].astype(F32)).astype(BF)
             go(w_copy(buf, a, ph, p, g, 1))
@@ -344,11 +360,11 @@
     def w_done(a, ph, g):
         dst = (gwout_ref, gwin_ref)[a]
         lo, hi = GROUPS[g]
+        w_landed(a, ph, g, 1)
         for p in range(4):
             total = w_src(a, ph, p, g, 0)[...].astype(F32)
             for m in (2, 1):
                 buf = w_dst(a, ph, p, g, m)
-                w_copy(buf, a, ph, p, g, m).wait_recv()
                 total = total + buf[...].astype(F32)
             if ph == 0:
                 red[a, :, lines(p, g)] = total.astype(BF)
@@ -386,14 +402,17 @@
             for p in range(4):
                 store(1, n, p, cat([gw[2 * p], gw[2 * p + 1]], 1))
 
-    waited = [0]
-
-    def drain(upto):
-        if isinstance(upto, tuple):
-            upto = marks[PLAN.index(upto)]
-        for c in sends[waited[0]:upto]:
-            c.wait_send()
-        waited[0] = upto
+    def ag_sent():
+        for a in range(2):
+            sent(fields[a].at[pl.ds(0, 7 * U)], ag_s.at[a])
+            sent(fields[a].at[pl.ds(0, NZ * U)], sb_s.at[a])
+
+    def z_sent(a):
+        sent(sib.at[a], ss_s.at[a])
+        sent(sib.at[a, pl.ds(0, 7)], zs.at[a])
+
+    def w_sent(a, ph):
+        sent(wp.at[a] if ph == 0 else w2.at[a], xs.at[a * 2 + ph])
 
     def make():
         local[4].wait()
@@ -411,16 +430,13 @@
         "ag0": ag_first, "agw": ag_wait, "agf": ag_pass, "own": ag_own, "ags": ag_sib, "gath": gathered,
         "tabl": make, "turn": turned, "H": hidden, "GH": backward_hidden, "GO": backward_out,
         "GI": backward_in, "S": shares, "P": place, "zf": z_first, "zn": z_next, "zl": z_last,
-        "wm": w_send, "wp": w_pass, "wd": w_done, "tab": tcopy.wait, "drain": drain,
+        "wm": w_send, "wp": w_pass, "wd": w_done, "tab": tcopy.wait, "ag_sent": ag_sent, "z_sent": z_sent, "w_sent": w_sent,
     }
-    marks = []
     local[0].wait()
     local[1].wait()
     pl.semaphore_wait(barrier, 7)
     for name, *args in PLAN:
-        marks.append(len(sends))
         tasks[name](*args)
-    drain(len(sends))
 
 
 def finish(*refs):
@@ -467,11 +483,11 @@
             pltpu.SMEM((ROWS, SLOTS), jnp.int32),
             pltpu.SMEM((ROWS,), jnp.int32),
             dma((7,)),
-            dma((32,)), dma((32,)),
-            dma((18,)), dma((18,)),
-            dma((16,)), dma((16,)),
-            dma((32,)), dma((32,)),
-            dma((96,)), dma((96,)),
+            dma((2,)), dma((32,)),
+            dma((2,)), dma((2,)),
+            dma((2,)), dma((4,)),
+            dma((2,)), dma((8,)),
+            dma((4,)), dma((8,)),
         ],
         compiler_params=pltpu.CompilerParams(
             collective_id=0, has_side_effects=True, vmem_limit_bytes=63 * 1024 * 1024

time: 63.4 us -> 59.6 us (0.940)
  Pallas kernels: 62.7 us -> 58.7 us
    pallas_call x1, Pallas kernels: 60.6 us -> 56.7 us  [on_device(): pl.pallas_call(kernel, out_shape=shapes, in_specs=[hbm] * 6, out_specs=(v...]
where the time goes in v7:
time: 59.6 us; the launch traced here: 59.4 us
  Pallas kernels  58.7 us (98%)
  between operations  0.64 us (1%)
    pallas_call x1, Pallas kernels, on_device(): pl.pallas_call(kernel, out_shape=shapes, in_specs=[hbm] * 6, out_specs=(v...  56.7 us
    pallas_call x1, Pallas kernels, on_device(): pl.pallas_call(finish, out_shape=shapes, in_specs=[vm] * 4, out_specs=(vm...  2.01 us

profile of v7, /device:TPU:32, one launch (start us, length us, event | category | flops | bytes accessed | tf_op | source)
XLA Modules:
  0.0 59.4 jit_solution(11723428812383292925)
XLA Ops:
  0.6 56.7 %shard_map.93 = (bf16[448,128]{1,0:T(8,128)(2,1)}, bf16[448,128]{1,0:T(8,128)(2,1)}, f32[448,128]{1,0:T(8,128)}, f32[448,128]{1,0:T(8,128)}) custom-call(s32[7,8]{1,0:T(8,128)} %col_hbm.1, s32[7]{0:T(128)} %cnt_hbm.1, bf16[7,64,128]{2,1,0:T(8,128)(2,1)} %bitcast.16, bf16[7,64,128]{2,1,0:T(8,128)(2,1)} %bitcast.17, bf16[56,128,128]{2,1,0:T(8,128)(2,1)} %bitcast.12, ...), custom_call_target="tpu_custom_call" | custom-call | flops 1409286144 | bytes 8000000 | tf_op jit(solution)/shard_map/pallas_call | solution.py:457
  57.3 2.0 %shard_map.94 = (bf16[448,128]{1,0:T(8,128)(2,1)}, bf16[448,128]{1,0:T(8,128)(2,1)}, f32[448,128]{1,0:T(8,128)}, f32[448,128]{1,0:T(8,128)}) custom-call(bf16[448,128]{1,0:T(8,128)(2,1)} %get-tuple-element.12.refs_0_, bf16[448,128]{1,0:T(8,128)(2,1)} %get-tuple-element.13.refs_1_, f32[448,128]{1,0:T(8,128)} %get-tuple-element.14.refs_2_, ...), custom_call_target="tpu_custom_call" | custom-call | bytes 1400000 | tf_op jit(solution)/shard_map/pallas_call | solution.py:501

commit v8 on v7

--- a/solution.py
+++ b/solution.py
@@ -16,30 +16,34 @@
 U = 7
 SPAN = ((0, 4), (4, 3))
 H = 224
-W = 112
-GROUPS = ((0, 7),)
+GROUPS = ((0, 4), (4, 7))
 BF = jnp.bfloat16
 F32 = jnp.float32
 MESH = pl.DeviceIdType.MESH
 C0 = 0.7978845608028654
 C1 = 0.044715
 ORDER = (4, 3, -3, 2, -2, 1, -1, 0)
+HALVES = (True, True)
 FIRST = 3
 NT = (((1,), (1,)), ((), ()))
 PLAN = (
-    ("ag0", 0, 0), ("ag0", 0, 1), ("turn",), ("ag0", 1, 0), ("ag0", 1, 1), ("agw", 0, 0, 0), ("agf", 0, 0, 0),
-    ("agw", 0, 0, 1), ("agw", 1, 0, 0), ("agf", 1, 0, 0), ("agf", 0, 0, 1), ("agw", 0, 1, 0), ("agf", 0, 1, 0),
-    ("agw", 1, 0, 1), ("agf", 1, 0, 1), ("own", 0), ("agw", 1, 1, 0), ("agf", 1, 1, 0), ("tabl",), ("ags", 1, 0),
-    ("agw", 0, 1, 1), ("own", 1), ("ags", 0, 0), ("agf", 0, 1, 1), ("agw", 0, 2, 0), ("agf", 0, 2, 0),
-    ("agw", 1, 1, 1), ("ags", 0, 1), ("agf", 1, 1, 1), ("agw", 1, 2, 0), ("agf", 1, 2, 0), ("agw", 0, 2, 1),
-    ("ags", 0, 2), ("ags", 1, 1), ("agw", 0, 3, 0), ("ags", 0, 3), ("agw", 1, 2, 1), ("ags", 1, 2), ("agw", 1, 3, 0),
-    ("ags", 1, 3), ("gath", 0), ("H", 0, 4), ("H", 4, 7), ("S", 0), ("tab",), ("P", 0), ("gath", 1), ("GH",),
-    ("GO", 0), ("wm", 0, 0, 0, 0), ("S", 1), ("P", 1), ("zf", 0), ("wm", 0, 0, 0, 2), ("GI", 0), ("zf", 1),
-    ("wm", 1, 0, 0, 0), ("wm", 1, 0, 0, 2), ("zn", 0, 3), ("zn", 1, 3), ("wp", 0, 0, 0), ("wp", 1, 0, 0),
-    ("zn", 0, 2), ("zn", 1, 2), ("wd", 0, 0, 0), ("wm", 0, 1, 0, 0), ("wm", 0, 1, 0, 2), ("zn", 0, 1),
-    ("wd", 1, 0, 0), ("wm", 1, 1, 0, 0), ("zn", 1, 1), ("wp", 0, 1, 0), ("wm", 1, 1, 0, 2), ("wp", 1, 1, 0),
-    ("ag_sent",), ("w_sent", 0, 0), ("w_sent", 1, 0), ("wd", 0, 1, 0), ("zl", 0), ("zl", 1), ("wd", 1, 1, 0),
-    ("z_sent", 0), ("z_sent", 1), ("w_sent", 0, 1), ("w_sent", 1, 1),
+    ("ag0", 0, 0), ("ag0", 1, 0), ("ag0", 0, 1), ("turn",), ("ag0", 1, 1), ("agw", 0, 0, 0), ("agf", 0, 0, 0),
+    ("own", 1), ("agw", 1, 0, 0), ("agf", 1, 0, 0), ("own", 0), ("agw", 1, 0, 1), ("agw", 0, 0, 1), ("agf", 0, 0, 1),
+    ("agw", 0, 1, 0), ("agf", 0, 1, 0), ("tabl",), ("agf", 1, 0, 1), ("agw", 1, 1, 0), ("agf", 1, 1, 0),
+    ("agw", 0, 1, 1), ("agf", 0, 1, 1), ("agw", 0, 2, 0), ("agf", 0, 2, 0), ("agw", 1, 1, 1), ("agf", 1, 1, 1),
+    ("ags", 0, 0), ("agw", 1, 2, 0), ("agf", 1, 2, 0), ("ags", 1, 1), ("agw", 0, 2, 1), ("ags", 1, 0), ("ags", 0, 2),
+    ("ags", 0, 1), ("agw", 0, 3, 0), ("ags", 0, 3), ("agw", 1, 2, 1), ("ags", 1, 2), ("agw", 1, 3, 0), ("ags", 1, 3),
+    ("gath", 0), ("H", 0, 4), ("H", 4, 7), ("S", 0), ("tab",), ("P", 0), ("gath", 1), ("GH",), ("GI", 0),
+    ("wm", 1, 0, 0, 2), ("GO", 0), ("zf", 0), ("wm", 0, 0, 0, 2), ("S", 1), ("wm", 0, 0, 0, 0), ("P", 1), ("zg", 0),
+    ("wm", 1, 0, 0, 0), ("GO", 1), ("wm", 0, 0, 1, 0), ("zn", 0, 3, 0), ("GI", 1), ("zf", 1), ("wm", 1, 0, 1, 0),
+    ("zg", 1), ("wp", 0, 0, 0), ("zn", 0, 2, 1), ("wp", 1, 0, 0), ("zn", 0, 2, 0), ("wm", 0, 0, 1, 2),
+    ("wp", 0, 0, 1), ("zn", 1, 3, 0), ("wm", 1, 0, 1, 2), ("zn", 1, 2, 1), ("wp", 1, 0, 1), ("wd", 0, 0, 0),
+    ("wm", 0, 1, 0, 0), ("wd", 1, 0, 0), ("wm", 1, 1, 0, 0), ("zn", 0, 1, 1), ("wm", 1, 1, 0, 2), ("zn", 1, 2, 0),
+    ("wd", 0, 0, 1), ("wm", 0, 1, 0, 2), ("wm", 0, 1, 1, 0), ("zn", 0, 1, 0), ("zn", 1, 1, 1), ("wd", 1, 0, 1),
+    ("wm", 1, 1, 1, 0), ("wp", 0, 1, 0), ("wm", 1, 1, 1, 2), ("wm", 0, 1, 1, 2), ("zn", 1, 1, 0), ("wp", 0, 1, 1),
+    ("wp", 1, 1, 0), ("wp", 1, 1, 1), ("ag_sent",), ("w_sent", 0, 0), ("w_sent", 1, 0), ("wd", 0, 1, 0), ("zl", 0),
+    ("wd", 0, 1, 1), ("zl", 1), ("wd", 1, 1, 0), ("wd", 1, 1, 1), ("z_sent", 0), ("z_sent", 1), ("w_sent", 0, 1),
+    ("w_sent", 1, 1),
 )
 
 
@@ -55,7 +59,7 @@
     col_hbm, cnt_hbm, x_hbm, g_hbm, win_hbm, wout_hbm,
     out_ref, ing_ref, gwin_ref, gwout_ref,
     xg, gg, win, wout, wint, woutt, dgelu, hid, gpre, cbuf, run, part, sib, zb,
-    wgt, wp, red, w2, tabv, tab, col_ref, cnt_ref,
+    wgts, wps, reds, w2s, tabv, tab, col_ref, cnt_ref,
     lsem, ag_s, ag_r, sb_s, sb_r, ss_s, ss_r, zs, zr, xs, xr,
 ):
     dp = lax.axis_index("dp")
@@ -172,7 +176,8 @@
         step = -k if way == 0 else k
         v = piece(fields[a], 0, step, *SPAN[h])
         i = ((a * 2 + way) * 4 + k) * 2 + h
-        return rcopy(v, v, ag_s.at[a], ag_r.at[i], zdev(1 if way == 0 else -1))
+        src = (x_hbm, g_hbm)[a].at[pl.ds(*SPAN[h])] if k == 0 else v
+        return rcopy(src, v, ag_s.at[a], ag_r.at[i], zdev(1 if way == 0 else -1))
 
     def sb_place(j):
         if j == 0:
@@ -185,7 +190,8 @@
     def sb_copy(a, j, mine):
         step, span = sb_place(j)
         v = piece(fields[a], 0 if mine else 1, step, *span)
-        return rcopy(v, v, sb_s.at[a], sb_r.at[a], sdev)
+        src = (x_hbm, g_hbm)[a] if j == 0 else v
+        return rcopy(src, v, sb_s.at[a], sb_r.at[a], sdev)
 
     def part_of(way, i):
         return way if i == 0 else 1 - way
@@ -210,6 +216,7 @@
             go(sb_copy(a, 7 + way if k == 3 else 1 + 3 * way + k, True))
 
     def gathered(a):
+        local[a].wait()
         landed(fields[a].at[pl.ds(0, NZ * U)], sb_r.at[a])
 
     def turn():
@@ -277,35 +284,51 @@
         src = part.at[a, j, pl.ds(pl.multiple_of(own_row + h * H, 32), H)]
         return src, src[...].astype(F32) + sib[a, j, h * H:(h + 1) * H].astype(F32)
 
-    def z_copy(src, a, way, r):
-        dst = zb.at[a, way, r]
-        if r == 3:
-            dst = dst.at[pl.ds(way * H, H)]
-        return rcopy(src, dst, zs.at[a], zr.at[a * 4 + r], zdev(1 if way == 0 else -1))
+    def z_half(ref, way, i):
+        if i is None:
+            return ref
+        return ref.at[pl.ds((way if i == 0 else 1 - way) * H, H)]
+
+    def z_sem(a, r, i):
+        return zr.at[(a * 4 + r) * 2 + (i or 0)]
+
+    def z_copy(src, a, way, r, i):
+        dst = z_half(zb.at[a, way, r], way, i)
+        return rcopy(src, dst, zs.at[a], z_sem(a, r, i), zdev(1 if way == 0 else -1))
+
+    def z_wait(a, r, i):
+        view = zb.at[a, :, r] if i is None else zb.at[a, :, r, pl.ds(0, H)]
+        landed(view, z_sem(a, r, i))
+
+    def z_start(a, r):
+        for way in range(2):
+            src, total = chip_sum(a, r + 1 if way == 0 else -(r + 1), way if r == 3 else 1 - way)
+            src[...] = total.astype(BF)
+            go(z_copy(src, a, way, r, 3 - r))
 
     def z_first(a):
-        for way in range(2):
-            src, total = chip_sum(a, 4 if way == 0 else -4, way)
-            src[...] = total.astype(BF)
-            go(z_copy(src, a, way, 3))
-
-    def z_next(a, r):
-        if r == 3:
-            landed(zb.at[a, :, r, pl.ds(0, H)], zr.at[a * 4 + r])
-        else:
-            landed(zb.at[a, :, r], zr.at[a * 4 + r])
+        z_start(a, 3)
+
+    def z_near(a):
+        z_start(a, 2)
+
+    def z_next(a, r, i=None):
+        z_wait(a, r, 0 if r == 3 else i)
         for way in range(2):
             for h in range(2):
+                if i is not None and h != (way if i == 0 else 1 - way):
+                    continue
                 src, total = chip_sum(a, r if way == 0 else -r, h)
                 buf = zb.at[a, way, r, pl.ds(h * H, H)]
                 if r < 3 or h == way:
                     total = total + buf[...].astype(F32)
                 buf[...] = total.astype(BF)
-            go(z_copy(zb.at[a, way, r], a, way, r - 1))
+            go(z_copy(z_half(zb.at[a, way, r], way, i), a, way, r - 1, i))
 
     def z_last(a):
         dst = (out_ref, ing_ref)[a]
-        landed(zb.at[a, :, 0], zr.at[a * 4])
+        for i in (0, 1) if HALVES[a] else (None,):
+            z_wait(a, 0, i)
         for h in range(2):
             src, total = chip_sum(a, 0, h)
             for way in range(2):
@@ -315,35 +338,26 @@
     coords = ((yat, xat), (xat, yat))
     devs = ((ydev, xdev), (xdev, ydev))
 
-    def lines(p, g):
-        lo, hi = GROUPS[g]
-        return pl.ds(p * W + lo * 16, (hi - lo) * 16)
-
     def w_dst(a, ph, p, g, m):
-        return wp.at[a, m, :, lines(p, g)] if ph == 0 else w2.at[a, m, lines(p, g)]
+        return wps[g].at[a, m, p] if ph == 0 else w2s[g].at[a, m, p]
+
+    def w_sem(a, ph, g, m):
+        return xr.at[((a * 2 + ph) * len(GROUPS) + g) * 2 + (0 if m == 0 else 1)]
 
     def w_copy(src, a, ph, p, g, m):
         sign = 1 if p % 2 == 0 else -1
-        i = ((a * 2 + ph) * len(GROUPS) + g) * 2 + (0 if m == 0 else 1)
         return rcopy(
-            src, w_dst(a, ph, p, g, m), xs.at[a * 2 + ph], xr.at[i], devs[p // 2][ph](sign if m < 2 else -sign)
+            src, w_dst(a, ph, p, g, m), xs.at[(a * 2 + ph) * len(GROUPS) + g], w_sem(a, ph, g, m),
+            devs[p // 2][ph](sign if m < 2 else -sign)
         )
 
     def w_landed(a, ph, g, m):
-        i = ((a * 2 + ph) * len(GROUPS) + g) * 2 + (0 if m == 0 else 1)
-        lo, hi = GROUPS[g]
-        span = pl.ds(0, (hi - lo) * 64)
-        if m == 0:
-            view = wp.at[a, 0, :, span] if ph == 0 else w2.at[a, 0, span]
-        else:
-            view = wp.at[a, pl.ds(1, 2), :, span] if ph == 0 else w2.at[a, pl.ds(1, 2), span]
-        landed(view, xr.at[i])
+        ref = (wps if ph == 0 else w2s)[g]
+        landed(ref.at[a, 0] if m == 0 else ref.at[a, pl.ds(1, 2)], w_sem(a, ph, g, m))
 
     def w_src(a, ph, p, g, step):
         c = coords[p // 2][ph][(step if p % 2 == 0 else -step) % NQ]
-        if ph == 0:
-            return wgt.at[a, c, :, lines(p, g)]
-        return red.at[a, c, lines(p, g)]
+        return (wgts if ph == 0 else reds)[g].at[a, p, c]
 
     def w_send(a, ph, g, m):
         for p in range(4):
@@ -367,20 +381,21 @@
                 buf = w_dst(a, ph, p, g, m)
                 total = total + buf[...].astype(F32)
             if ph == 0:
-                red[a, :, lines(p, g)] = total.astype(BF)
+                reds[g][a, p] = total.astype(BF)
             else:
                 for n in range(lo, hi):
                     dst[n * 64 + p * 16:n * 64 + p * 16 + 16, :] = total[(n - lo) * 16:(n - lo) * 16 + 16]
 
     def store(a, n, p, both):
         both = both.astype(BF).reshape(NQ, NQ, 16, BLK)
-        row = p * W + n * 16
+        g = [lo <= n < hi for lo, hi in GROUPS].index(True)
+        row = (n - GROUPS[g][0]) * 16
         if p < 2:
-            wgt[a, :, :, row:row + 16, :] = both
+            wgts[g][a, p, :, :, row:row + 16, :] = both
         else:
             for i in range(NQ):
                 for j in range(NQ):
-                    wgt[a, i, j, row:row + 16, :] = both[j, i]
+                    wgts[g][a, p, i, j, row:row + 16, :] = both[j, i]
 
     def backward_hidden():
         for n in range(ROWS):
@@ -412,7 +427,8 @@
         sent(sib.at[a, pl.ds(0, 7)], zs.at[a])
 
     def w_sent(a, ph):
-        sent(wp.at[a] if ph == 0 else w2.at[a], xs.at[a * 2 + ph])
+        for g in range(len(GROUPS)):
+            sent((wps if ph == 0 else w2s)[g].at[a], xs.at[(a * 2 + ph) * len(GROUPS) + g])
 
     def make():
         local[4].wait()
@@ -429,11 +445,9 @@
     tasks = {
         "ag0": ag_first, "agw": ag_wait, "agf": ag_pass, "own": ag_own, "ags": ag_sib, "gath": gathered,
         "tabl": make, "turn": turned, "H": hidden, "GH": backward_hidden, "GO": backward_out,
-        "GI": backward_in, "S": shares, "P": place, "zf": z_first, "zn": z_next, "zl": z_last,
+        "GI": backward_in, "S": shares, "P": place, "zf": z_first, "zg": z_near, "zn": z_next, "zl": z_last,
         "wm": w_send, "wp": w_pass, "wd": w_done, "tab": tcopy.wait, "ag_sent": ag_sent, "z_sent": z_sent, "w_sent": w_sent,
     }
-    local[0].wait()
-    local[1].wait()
     pl.semaphore_wait(barrier, 7)
     for name, *args in PLAN:
         tasks[name](*args)
@@ -448,6 +462,7 @@
     vm = pl.BlockSpec(memory_space=pltpu.VMEM)
     hbm = pl.BlockSpec(memory_space=pltpu.HBM)
     dma = pltpu.SemaphoreType.DMA
+    heights = [(hi - lo) * 16 for lo, hi in GROUPS]
     shapes = (
         jax.ShapeDtypeStruct((CH, BLK), BF),
         jax.ShapeDtypeStruct((CH, BLK), BF),
@@ -474,10 +489,10 @@
             pltpu.VMEM((2, NZ, 2 * CH, BLK), BF),
             pltpu.VMEM((2, NZ, CH, BLK), BF),
             pltpu.VMEM((2, 2, 4, CH, BLK), BF),
-            pltpu.VMEM((2, NQ, NQ, CH, BLK), BF),
-            pltpu.VMEM((2, 3, NQ, CH, BLK), BF),
-            pltpu.VMEM((2, NQ, CH, BLK), BF),
-            pltpu.VMEM((2, 3, CH, BLK), BF),
+            [pltpu.VMEM((2, 4, NQ, NQ, r, BLK), BF) for r in heights],
+            [pltpu.VMEM((2, 3, 4, NQ, r, BLK), BF) for r in heights],
+            [pltpu.VMEM((2, 4, NQ, r, BLK), BF) for r in heights],
+            [pltpu.VMEM((2, 3, 4, r, BLK), BF) for r in heights],
             pltpu.VMEM((8, 128), jnp.int32),
             pltpu.SMEM((8, 128), jnp.int32),
             pltpu.SMEM((ROWS, SLOTS), jnp.int32),
@@ -486,8 +501,8 @@
             dma((2,)), dma((32,)),
             dma((2,)), dma((2,)),
             dma((2,)), dma((4,)),
-            dma((2,)), dma((8,)),
-            dma((4,)), dma((8,)),
+            dma((2,)), dma((16,)),
+            dma((8,)), dma((16,)),
         ],
         compiler_params=pltpu.CompilerParams(
             collective_id=0, has_side_effects=True, vmem_limit_bytes=63 * 1024 * 1024

time: 59.6 us -> 59.5 us (level)
  no operation moved by 1% of the time
where the time goes in v8:
time: 59.5 us; the launch traced here: 59 us
  Pallas kernels  58.3 us (98%)
  between operations  0.64 us (1%)
    pallas_call x1, Pallas kernels, on_device(): pl.pallas_call(kernel, out_shape=shapes, in_specs=[hbm] * 6, out_specs=(v...  56.3 us
    pallas_call x1, Pallas kernels, on_device(): pl.pallas_call(finish, out_shape=shapes, in_specs=[vm] * 4, out_specs=(vm...  2.01 us

profile of v8, /device:TPU:32, one launch (start us, length us, event | category | flops | bytes accessed | tf_op | source)
XLA Modules:
  0.0 59.0 jit_solution(1545936784029109548)
XLA Ops:
  0.6 56.3 %shard_map.93 = (bf16[448,128]{1,0:T(8,128)(2,1)}, bf16[448,128]{1,0:T(8,128)(2,1)}, f32[448,128]{1,0:T(8,128)}, f32[448,128]{1,0:T(8,128)}) custom-call(s32[7,8]{1,0:T(8,128)} %col_hbm.1, s32[7]{0:T(128)} %cnt_hbm.1, bf16[7,64,128]{2,1,0:T(8,128)(2,1)} %bitcast.16, bf16[7,64,128]{2,1,0:T(8,128)(2,1)} %bitcast.17, bf16[56,128,128]{2,1,0:T(8,128)(2,1)} %bitcast.12, ...), custom_call_target="tpu_custom_call" | custom-call | flops 1409286144 | bytes 8000000 | tf_op jit(solution)/shard_map/pallas_call | solution.py:472
  57.0 2.0 %shard_map.94 = (bf16[448,128]{1,0:T(8,128)(2,1)}, bf16[448,128]{1,0:T(8,128)(2,1)}, f32[448,128]{1,0:T(8,128)}, f32[448,128]{1,0:T(8,128)}) custom-call(bf16[448,128]{1,0:T(8,128)(2,1)} %get-tuple-element.12.refs_0_, bf16[448,128]{1,0:T(8,128)(2,1)} %get-tuple-element.13.refs_1_, f32[448,128]{1,0:T(8,128)} %get-tuple-element.14.refs_2_, ...), custom_call_target="tpu_custom_call" | custom-call | bytes 1400000 | tf_op jit(solution)/shard_map/pallas_call | solution.py:516

commit v9 on v8

--- a/solution.py
+++ b/solution.py
@@ -16,34 +16,30 @@
 U = 7
 SPAN = ((0, 4), (4, 3))
 H = 224
-GROUPS = ((0, 4), (4, 7))
+GROUPS = ((0, 7),)
 BF = jnp.bfloat16
 F32 = jnp.float32
 MESH = pl.DeviceIdType.MESH
 C0 = 0.7978845608028654
 C1 = 0.044715
 ORDER = (4, 3, -3, 2, -2, 1, -1, 0)
-HALVES = (True, True)
+HALVES = (False, False)
 FIRST = 3
 NT = (((1,), (1,)), ((), ()))
 PLAN = (
-    ("ag0", 0, 0), ("ag0", 1, 0), ("ag0", 0, 1), ("turn",), ("ag0", 1, 1), ("agw", 0, 0, 0), ("agf", 0, 0, 0),
-    ("own", 1), ("agw", 1, 0, 0), ("agf", 1, 0, 0), ("own", 0), ("agw", 1, 0, 1), ("agw", 0, 0, 1), ("agf", 0, 0, 1),
-    ("agw", 0, 1, 0), ("agf", 0, 1, 0), ("tabl",), ("agf", 1, 0, 1), ("agw", 1, 1, 0), ("agf", 1, 1, 0),
-    ("agw", 0, 1, 1), ("agf", 0, 1, 1), ("agw", 0, 2, 0), ("agf", 0, 2, 0), ("agw", 1, 1, 1), ("agf", 1, 1, 1),
-    ("ags", 0, 0), ("agw", 1, 2, 0), ("agf", 1, 2, 0), ("ags", 1, 1), ("agw", 0, 2, 1), ("ags", 1, 0), ("ags", 0, 2),
-    ("ags", 0, 1), ("agw", 0, 3, 0), ("ags", 0, 3), ("agw", 1, 2, 1), ("ags", 1, 2), ("agw", 1, 3, 0), ("ags", 1, 3),
-    ("gath", 0), ("H", 0, 4), ("H", 4, 7), ("S", 0), ("tab",), ("P", 0), ("gath", 1), ("GH",), ("GI", 0),
-    ("wm", 1, 0, 0, 2), ("GO", 0), ("zf", 0), ("wm", 0, 0, 0, 2), ("S", 1), ("wm", 0, 0, 0, 0), ("P", 1), ("zg", 0),
-    ("wm", 1, 0, 0, 0), ("GO", 1), ("wm", 0, 0, 1, 0), ("zn", 0, 3, 0), ("GI", 1), ("zf", 1), ("wm", 1, 0, 1, 0),
-    ("zg", 1), ("wp", 0, 0, 0), ("zn", 0, 2, 1), ("wp", 1, 0, 0), ("zn", 0, 2, 0), ("wm", 0, 0, 1, 2),
-    ("wp", 0, 0, 1), ("zn", 1, 3, 0), ("wm", 1, 0, 1, 2), ("zn", 1, 2, 1), ("wp", 1, 0, 1), ("wd", 0, 0, 0),
-    ("wm", 0, 1, 0, 0), ("wd", 1, 0, 0), ("wm", 1, 1, 0, 0), ("zn", 0, 1, 1), ("wm", 1, 1, 0, 2), ("zn", 1, 2, 0),
-    ("wd", 0, 0, 1), ("wm", 0, 1, 0, 2), ("wm", 0, 1, 1, 0), ("zn", 0, 1, 0), ("zn", 1, 1, 1), ("wd", 1, 0, 1),
-    ("wm", 1, 1, 1, 0), ("wp", 0, 1, 0), ("wm", 1, 1, 1, 2), ("wm", 0, 1, 1, 2), ("zn", 1, 1, 0), ("wp", 0, 1, 1),
-    ("wp", 1, 1, 0), ("wp", 1, 1, 1), ("ag_sent",), ("w_sent", 0, 0), ("w_sent", 1, 0), ("wd", 0, 1, 0), ("zl", 0),
-    ("wd", 0, 1, 1), ("zl", 1), ("wd", 1, 1, 0), ("wd", 1, 1, 1), ("z_sent", 0), ("z_sent", 1), ("w_sent", 0, 1),
-    ("w_sent", 1, 1),
+    ("ag0", 0, 0), ("ag0", 0, 1), ("turn",), ("ag0", 1, 0), ("ag0", 1, 1), ("agw", 0, 0, 0), ("agf", 0, 0, 0),
+    ("agw", 0, 0, 1), ("agw", 1, 0, 0), ("agf", 1, 0, 0), ("agf", 0, 0, 1), ("agw", 0, 1, 0), ("agf", 0, 1, 0),
+    ("agw", 1, 0, 1), ("agf", 1, 0, 1), ("own", 0), ("agw", 1, 1, 0), ("agf", 1, 1, 0), ("tabl",), ("ags", 1, 0),
+    ("agw", 0, 1, 1), ("own", 1), ("ags", 0, 0), ("agf", 0, 1, 1), ("agw", 0, 2, 0), ("agf", 0, 2, 0),
+    ("agw", 1, 1, 1), ("ags", 0, 1), ("agf", 1, 1, 1), ("agw", 1, 2, 0), ("agf", 1, 2, 0), ("agw", 0, 2, 1),
+    ("ags", 0, 2), ("ags", 1, 1), ("agw", 0, 3, 0), ("ags", 0, 3), ("agw", 1, 2, 1), ("ags", 1, 2), ("agw", 1, 3, 0),
+    ("ags", 1, 3), ("gath", 0), ("H", 0, 4), ("H", 4, 7), ("S", 0), ("tab",), ("P", 0), ("gath", 1), ("GH",),
+    ("GO", 0), ("wm", 0, 0, 0, 0), ("S", 1), ("P", 1), ("zf", 0), ("wm", 0, 0, 0, 2), ("GI", 0), ("zf", 1),
+    ("wm", 1, 0, 0, 0), ("wm", 1, 0, 0, 2), ("zn", 0, 3), ("zn", 1, 3), ("wp", 0, 0, 0), ("wp", 1, 0, 0),
+    ("zn", 0, 2), ("zn", 1, 2), ("wd", 0, 0, 0), ("wm", 0, 1, 0, 0), ("wm", 0, 1, 0, 2), ("zn", 0, 1),
+    ("wd", 1, 0, 0), ("wm", 1, 1, 0, 0), ("zn", 1, 1), ("wp", 0, 1, 0), ("wm", 1, 1, 0, 2), ("wp", 1, 1, 0),
+    ("ag_sent",), ("w_sent", 0, 0), ("w_sent", 1, 0), ("wd", 0, 1, 0), ("zl", 0), ("zl", 1), ("wd", 1, 1, 0),
+    ("z_sent", 0), ("z_sent", 1), ("w_sent", 0, 1), ("w_sent", 1, 1),
 )
 
 
@@ -57,7 +53,7 @@
 
 def kernel(
     col_hbm, cnt_hbm, x_hbm, g_hbm, win_hbm, wout_hbm,
-    out_ref, ing_ref, gwin_ref, gwout_ref,
+    act_ref, grad_ref,
     xg, gg, win, wout, wint, woutt, dgelu, hid, gpre, cbuf, run, part, sib, zb,
     wgts, wps, reds, w2s, tabv, tab, col_ref, cnt_ref,
     lsem, ag_s, ag_r, sb_s, sb_r, ss_s, ss_r, zs, zr, xs, xr,
@@ -166,17 +162,10 @@
     def wrap(step):
         return zat[step % NZ]
 
-    def ag_copy(a, way, k, h):
-        step = -(k + 1) if way == 0 else k + 1
-        v = piece(fields[a], 0, step, *SPAN[h])
-        i = ((a * 2 + way) * 4 + k) * 2 + h
-        return rcopy(v, v, ag_s.at[a], ag_r.at[i], zdev(1 if way == 0 else -1))
-
     def ag_send(a, way, k, h):
-        step = -k if way == 0 else k
-        v = piece(fields[a], 0, step, *SPAN[h])
-        i = ((a * 2 + way) * 4 + k) * 2 + h
+        v = piece(fields[a], 0, -k if way == 0 else k, *SPAN[h])
         src = (x_hbm, g_hbm)[a].at[pl.ds(*SPAN[h])] if k == 0 else v
+        i = (a * 4 + k) * 2 + (0 if h == way else 1)
         return rcopy(src, v, ag_s.at[a], ag_r.at[i], zdev(1 if way == 0 else -1))
 
     def sb_place(j):
@@ -201,8 +190,7 @@
             go(ag_send(a, way, 0, part_of(way, i)))
 
     def ag_wait(a, k, i):
-        for way in range(2):
-            ag_copy(a, way, k, part_of(way, i)).wait_recv()
+        landed(fields[a].at[pl.ds(0, U)], ag_r.at[(a * 4 + k) * 2 + i])
 
     def ag_pass(a, k, i):
         for way in range(2):
@@ -301,10 +289,13 @@
         landed(view, z_sem(a, r, i))
 
     def z_start(a, r):
+        copies = []
         for way in range(2):
             src, total = chip_sum(a, r + 1 if way == 0 else -(r + 1), way if r == 3 else 1 - way)
             src[...] = total.astype(BF)
-            go(z_copy(src, a, way, r, 3 - r))
+            copies.append(z_copy(src, a, way, r, 3 - r))
+        for c in copies:
+            go(c)
 
     def z_first(a):
         z_start(a, 3)
@@ -323,10 +314,11 @@
                 if r < 3 or h == way:
                     total = total + buf[...].astype(F32)
                 buf[...] = total.astype(BF)
+        for way in range(2):
             go(z_copy(z_half(zb.at[a, way, r], way, i), a, way, r - 1, i))
 
     def z_last(a):
-        dst = (out_ref, ing_ref)[a]
+        dst = act_ref.at[a]
         for i in (0, 1) if HALVES[a] else (None,):
             z_wait(a, 0, i)
         for h in range(2):
@@ -369,10 +361,11 @@
             buf = w_dst(a, ph, p, g, 0)
             mine = w_src(a, ph, p, g, 1)
             buf[...] = (buf[...].astype(F32) + mine[...].astype(F32)).astype(BF)
-            go(w_copy(buf, a, ph, p, g, 1))
+        for p in range(4):
+            go(w_copy(w_dst(a, ph, p, g, 0), a, ph, p, g, 1))
 
     def w_done(a, ph, g):
-        dst = (gwout_ref, gwin_ref)[a]
+        dst = grad_ref.at[a]
         lo, hi = GROUPS[g]
         w_landed(a, ph, g, 1)
         for p in range(4):
@@ -453,27 +446,17 @@
         tasks[name](*args)
 
 
-def finish(*refs):
-    for i in range(4):
-        refs[4 + i][...] = refs[i][...]
-
-
 def on_device(inputs, out_grad, w_in, w_out, columns, counts):
     vm = pl.BlockSpec(memory_space=pltpu.VMEM)
     hbm = pl.BlockSpec(memory_space=pltpu.HBM)
     dma = pltpu.SemaphoreType.DMA
     heights = [(hi - lo) * 16 for lo, hi in GROUPS]
-    shapes = (
-        jax.ShapeDtypeStruct((CH, BLK), BF),
-        jax.ShapeDtypeStruct((CH, BLK), BF),
-        jax.ShapeDtypeStruct((CH, BLK), F32),
-        jax.ShapeDtypeStruct((CH, BLK), F32),
-    )
-    res = pl.pallas_call(
+    shapes = (jax.ShapeDtypeStruct((2, CH, BLK), BF), jax.ShapeDtypeStruct((2, CH, BLK), F32))
+    act, grad = pl.pallas_call(
         kernel,
         out_shape=shapes,
         in_specs=[hbm] * 6,
-        out_specs=(vm, vm, vm, vm),
+        out_specs=(vm, vm),
         scratch_shapes=[
             pltpu.VMEM((2 * DB + 2, 64, BLK), BF),
             pltpu.VMEM((2 * DB + 2, 64, BLK), BF),
@@ -498,11 +481,11 @@
             pltpu.SMEM((ROWS, SLOTS), jnp.int32),
             pltpu.SMEM((ROWS,), jnp.int32),
             dma((7,)),
-            dma((2,)), dma((32,)),
+            dma((2,)), dma((16,)),
             dma((2,)), dma((2,)),
             dma((2,)), dma((4,)),
             dma((2,)), dma((16,)),
-            dma((8,)), dma((16,)),
+            dma((4,)), dma((8,)),
         ],
         compiler_params=pltpu.CompilerParams(
             collective_id=0, has_side_effects=True, vmem_limit_bytes=63 * 1024 * 1024
@@ -513,15 +496,8 @@
         inputs.T.reshape(U, 64, BLK), out_grad.T.reshape(U, 64, BLK),
         w_in.reshape(NB, BLK, BLK), w_out.reshape(NB, BLK, BLK),
     )
-    out, ing, gwin, gwout = pl.pallas_call(
-        finish,
-        out_shape=shapes,
-        in_specs=[vm] * 4,
-        out_specs=(vm,) * 4,
-        compiler_params=pltpu.CompilerParams(vmem_limit_bytes=63 * 1024 * 1024),
-        cost_estimate=pl.CostEstimate(flops=0, bytes_accessed=1_400_000, transcendentals=0),
-    )(*res)
-    return (out.T, ing.T, gwin.reshape(ROWS, SLOTS, 8, BLK), gwout.reshape(ROWS, SLOTS, 8, BLK))
+    shape = (ROWS, SLOTS, 8, BLK)
+    return act[0].T, act[1].T, grad[1].reshape(shape), grad[0].reshape(shape)
 
 
 def solution(mesh):

time: 59.5 us -> 61.2 us (1.029)
  local copies, waits for them, and re-layouts: 0 us -> 3.5 us
  Pallas kernels: 58.3 us -> 56.9 us
    pallas_call x1 -> x0, Pallas kernels: 2.01 us -> none  [on_device(): pl.pallas_call(finish, out_shape=shapes, in_specs=[vm] * 4, out_specs=(vm...]
    slice x0 -> x1, local copies, waits for them, and re-layouts: none -> 1.84 us  [on_device(): return (act[0].T, act[1].T, grad[1].reshape(shape), grad[0].reshape(shape))]
    transpose x0 -> x1, local copies, waits for them, and re-layouts: none -> 1.65 us  [on_device(): return (act[0].T, act[1].T, grad[1].reshape(shape), grad[0].reshape(shape))]
where the time goes in v9:
time: 61.2 us; the launch traced here: 61 us
  Pallas kernels  56.9 us (93%)
  local copies, waits for them, and re-layouts  3.5 us (6%)
  between operations  0.64 us (1%)
    pallas_call x1, Pallas kernels, on_device(): pl.pallas_call(kernel, out_shape=shapes, in_specs=[hbm] * 6, out_specs=(v...  56.9 us
    slice x1, local copies, waits for them, and re-layouts, on_device(): return (act[0].T, act[1].T, grad[1].reshape(shape), grad[0].reshape(shape))  1.84 us
    transpose x1, local copies, waits for them, and re-layouts, on_device(): return (act[0].T, act[1].T, grad[1].reshape(shape), grad[0].reshape(shape))  1.65 us

profile of v9, /device:TPU:32, one launch (start us, length us, event | category | flops | bytes accessed | tf_op | source)
XLA Modules:
  0.0 61.0 jit_solution(3779949914131198358)
XLA Ops:
  0.6 56.9 %shard_map.93 = (bf16[2,448,128]{2,1,0:T(8,128)(2,1)}, f32[2,448,128]{2,1,0:T(8,128)}) custom-call(s32[7,8]{1,0:T(8,128)} %col_hbm.1, s32[7]{0:T(128)} %cnt_hbm.1, bf16[7,64,128]{2,1,0:T(8,128)(2,1)} %bitcast.22, bf16[7,64,128]{2,1,0:T(8,128)(2,1)} %bitcast.23, bf16[56,128,128]{2,1,0:T(8,128)(2,1)} %bitcast.20, bf16[56,128,128]{2,1,0:T(8,128)(2,1)} %bitcast.21), custom_call_target="tpu_custom_call" | custom-call | flops 1409286144 | bytes 8000000 | tf_op jit(solution)/shard_map/pallas_call | solution.py:455
  57.5 1.7 %slice_bitcast_fusion = (bf16[128,448]{0,1:T(8,128)(2,1)}, bf16[128,448]{0,1:T(8,128)(2,1)}) fusion(bf16[2,448,128]{2,1,0:T(8,128)(2,1)} %get-tuple-element.6), kind=kLoop, calls=%fused_computation | loop fusion | bytes 458752 | tf_op jit(solution)/shard_map/transpose | solution.py:500
  59.1 1.8 %fusion = (f32[1,448,128]{2,1,0:T(8,128)}, f32[1,448,128]{2,1,0:T(8,128)}) fusion(f32[2,448,128]{2,1,0:T(8,128)} %get-tuple-element.7), kind=kLoop, calls=%fused_computation.2 | loop fusion | bytes 917504 | tf_op jit(solution)/shard_map/slice | solution.py:500

commit v10 on v7

--- a/solution.py
+++ b/solution.py
@@ -28,18 +28,18 @@
 NT = (((1,), (1,)), ((), ()))
 PLAN = (
     ("ag0", 0, 0), ("ag0", 0, 1), ("turn",), ("ag0", 1, 0), ("ag0", 1, 1), ("agw", 0, 0, 0), ("agf", 0, 0, 0),
-    ("agw", 0, 0, 1), ("agw", 1, 0, 0), ("agf", 1, 0, 0), ("agf", 0, 0, 1), ("agw", 0, 1, 0), ("agf", 0, 1, 0),
-    ("agw", 1, 0, 1), ("agf", 1, 0, 1), ("own", 0), ("agw", 1, 1, 0), ("agf", 1, 1, 0), ("tabl",), ("ags", 1, 0),
-    ("agw", 0, 1, 1), ("own", 1), ("ags", 0, 0), ("agf", 0, 1, 1), ("agw", 0, 2, 0), ("agf", 0, 2, 0),
-    ("agw", 1, 1, 1), ("ags", 0, 1), ("agf", 1, 1, 1), ("agw", 1, 2, 0), ("agf", 1, 2, 0), ("agw", 0, 2, 1),
-    ("ags", 0, 2), ("ags", 1, 1), ("agw", 0, 3, 0), ("ags", 0, 3), ("agw", 1, 2, 1), ("ags", 1, 2), ("agw", 1, 3, 0),
-    ("ags", 1, 3), ("gath", 0), ("H", 0, 4), ("H", 4, 7), ("S", 0), ("tab",), ("P", 0), ("gath", 1), ("GH",),
-    ("GO", 0), ("wm", 0, 0, 0, 0), ("S", 1), ("P", 1), ("zf", 0), ("wm", 0, 0, 0, 2), ("GI", 0), ("zf", 1),
-    ("wm", 1, 0, 0, 0), ("wm", 1, 0, 0, 2), ("zn", 0, 3), ("zn", 1, 3), ("wp", 0, 0, 0), ("wp", 1, 0, 0),
-    ("zn", 0, 2), ("zn", 1, 2), ("wd", 0, 0, 0), ("wm", 0, 1, 0, 0), ("wm", 0, 1, 0, 2), ("zn", 0, 1),
-    ("wd", 1, 0, 0), ("wm", 1, 1, 0, 0), ("zn", 1, 1), ("wp", 0, 1, 0), ("wm", 1, 1, 0, 2), ("wp", 1, 1, 0),
-    ("ag_sent",), ("w_sent", 0, 0), ("w_sent", 1, 0), ("wd", 0, 1, 0), ("zl", 0), ("zl", 1), ("wd", 1, 1, 0),
-    ("z_sent", 0), ("z_sent", 1), ("w_sent", 0, 1), ("w_sent", 1, 1),
+    ("agw", 0, 0, 1), ("ags", 0, 0), ("tabl",), ("agf", 0, 0, 1), ("agw", 1, 0, 0), ("agf", 1, 0, 0),
+    ("agw", 0, 1, 0), ("agf", 0, 1, 0), ("agw", 1, 0, 1), ("agf", 1, 0, 1), ("agw", 0, 1, 1), ("ags", 0, 1),
+    ("own", 1), ("own", 0), ("agf", 0, 1, 1), ("agw", 1, 1, 0), ("agf", 1, 1, 0), ("ags", 1, 0), ("agw", 0, 2, 0),
+    ("agf", 0, 2, 0), ("agw", 1, 1, 1), ("agw", 0, 2, 1), ("agf", 1, 1, 1), ("ags", 1, 1), ("ags", 0, 2),
+    ("agw", 1, 2, 0), ("agf", 1, 2, 0), ("agw", 0, 3, 0), ("ags", 0, 3), ("gath", 0), ("H", 0, 4), ("agw", 1, 2, 1),
+    ("ags", 1, 2), ("agw", 1, 3, 0), ("ags", 1, 3), ("H", 4, 7), ("S", 0), ("tab",), ("P", 0), ("gath", 1), ("GO", 0),
+    ("wm", 0, 0, 0, 0), ("GH",), ("zf", 0), ("wm", 0, 0, 0, 2), ("S", 1), ("P", 1), ("GI", 0), ("wm", 1, 0, 0, 0),
+    ("zf", 1), ("wp", 0, 0, 0), ("zn", 0, 3), ("zn", 1, 3), ("wm", 1, 0, 0, 2), ("wp", 1, 0, 0), ("zn", 0, 2),
+    ("zn", 1, 2), ("wd", 0, 0, 0), ("wm", 0, 1, 0, 0), ("zn", 0, 1), ("wd", 1, 0, 0), ("wm", 1, 1, 0, 0),
+    ("wm", 1, 1, 0, 2), ("zn", 1, 1), ("wm", 0, 1, 0, 2), ("wp", 0, 1, 0), ("wp", 1, 1, 0), ("ag_sent",),
+    ("w_sent", 0, 0), ("w_sent", 1, 0), ("wd", 0, 1, 0), ("zl", 0), ("wd", 1, 1, 0), ("zl", 1), ("z_sent", 0),
+    ("z_sent", 1), ("w_sent", 0, 1), ("w_sent", 1, 1),
 )
 
 

time: 59.6 us -> 59.1 us (level)
  no operation moved by 1% of the time
where the time goes in v10:
time: 59.1 us; the launch traced here: 58.9 us
  Pallas kernels  58.3 us (99%)
  between operations  0.64 us (1%)
    pallas_call x1, Pallas kernels, on_device(): pl.pallas_call(kernel, out_shape=shapes, in_specs=[hbm] * 6, out_specs=(v...  56.3 us
    pallas_call x1, Pallas kernels, on_device(): pl.pallas_call(finish, out_shape=shapes, in_specs=[vm] * 4, out_specs=(vm...  2.01 us

profile of v10, /device:TPU:32, one launch (start us, length us, event | category | flops | bytes accessed | tf_op | source)
XLA Modules:
  0.0 58.9 jit_solution(5636223513790975742)
XLA Ops:
  0.6 56.3 %shard_map.93 = (bf16[448,128]{1,0:T(8,128)(2,1)}, bf16[448,128]{1,0:T(8,128)(2,1)}, f32[448,128]{1,0:T(8,128)}, f32[448,128]{1,0:T(8,128)}) custom-call(s32[7,8]{1,0:T(8,128)} %col_hbm.1, s32[7]{0:T(128)} %cnt_hbm.1, bf16[7,64,128]{2,1,0:T(8,128)(2,1)} %bitcast.16, bf16[7,64,128]{2,1,0:T(8,128)(2,1)} %bitcast.17, bf16[56,128,128]{2,1,0:T(8,128)(2,1)} %bitcast.12, ...), custom_call_target="tpu_custom_call" | custom-call | flops 1409286144 | bytes 8000000 | tf_op jit(solution)/shard_map/pallas_call | solution.py:457
  56.9 2.0 %shard_map.94 = (bf16[448,128]{1,0:T(8,128)(2,1)}, bf16[448,128]{1,0:T(8,128)(2,1)}, f32[448,128]{1,0:T(8,128)}, f32[448,128]{1,0:T(8,128)}) custom-call(bf16[448,128]{1,0:T(8,128)(2,1)} %get-tuple-element.12.refs_0_, bf16[448,128]{1,0:T(8,128)(2,1)} %get-tuple-element.13.refs_1_, f32[448,128]{1,0:T(8,128)} %get-tuple-element.14.refs_2_, ...), custom_call_target="tpu_custom_call" | custom-call | bytes 1400000 | tf_op jit(solution)/shard_map/pallas_call | solution.py:501

commit v11 on v8

--- a/solution.py
+++ b/solution.py
@@ -16,7 +16,7 @@
 U = 7
 SPAN = ((0, 4), (4, 3))
 H = 224
-GROUPS = ((0, 4), (4, 7))
+GROUPS = ((0, 7),)
 BF = jnp.bfloat16
 F32 = jnp.float32
 MESH = pl.DeviceIdType.MESH
@@ -27,23 +27,20 @@
 FIRST = 3
 NT = (((1,), (1,)), ((), ()))
 PLAN = (
-    ("ag0", 0, 0), ("ag0", 1, 0), ("ag0", 0, 1), ("turn",), ("ag0", 1, 1), ("agw", 0, 0, 0), ("agf", 0, 0, 0),
-    ("own", 1), ("agw", 1, 0, 0), ("agf", 1, 0, 0), ("own", 0), ("agw", 1, 0, 1), ("agw", 0, 0, 1), ("agf", 0, 0, 1),
-    ("agw", 0, 1, 0), ("agf", 0, 1, 0), ("tabl",), ("agf", 1, 0, 1), ("agw", 1, 1, 0), ("agf", 1, 1, 0),
-    ("agw", 0, 1, 1), ("agf", 0, 1, 1), ("agw", 0, 2, 0), ("agf", 0, 2, 0), ("agw", 1, 1, 1), ("agf", 1, 1, 1),
-    ("ags", 0, 0), ("agw", 1, 2, 0), ("agf", 1, 2, 0), ("ags", 1, 1), ("agw", 0, 2, 1), ("ags", 1, 0), ("ags", 0, 2),
-    ("ags", 0, 1), ("agw", 0, 3, 0), ("ags", 0, 3), ("agw", 1, 2, 1), ("ags", 1, 2), ("agw", 1, 3, 0), ("ags", 1, 3),
-    ("gath", 0), ("H", 0, 4), ("H", 4, 7), ("S", 0), ("tab",), ("P", 0), ("gath", 1), ("GH",), ("GI", 0),
-    ("wm", 1, 0, 0, 2), ("GO", 0), ("zf", 0), ("wm", 0, 0, 0, 2), ("S", 1), ("wm", 0, 0, 0, 0), ("P", 1), ("zg", 0),
-    ("wm", 1, 0, 0, 0), ("GO", 1), ("wm", 0, 0, 1, 0), ("zn", 0, 3, 0), ("GI", 1), ("zf", 1), ("wm", 1, 0, 1, 0),
-    ("zg", 1), ("wp", 0, 0, 0), ("zn", 0, 2, 1), ("wp", 1, 0, 0), ("zn", 0, 2, 0), ("wm", 0, 0, 1, 2),
-    ("wp", 0, 0, 1), ("zn", 1, 3, 0), ("wm", 1, 0, 1, 2), ("zn", 1, 2, 1), ("wp", 1, 0, 1), ("wd", 0, 0, 0),
-    ("wm", 0, 1, 0, 0), ("wd", 1, 0, 0), ("wm", 1, 1, 0, 0), ("zn", 0, 1, 1), ("wm", 1, 1, 0, 2), ("zn", 1, 2, 0),
-    ("wd", 0, 0, 1), ("wm", 0, 1, 0, 2), ("wm", 0, 1, 1, 0), ("zn", 0, 1, 0), ("zn", 1, 1, 1), ("wd", 1, 0, 1),
-    ("wm", 1, 1, 1, 0), ("wp", 0, 1, 0), ("wm", 1, 1, 1, 2), ("wm", 0, 1, 1, 2), ("zn", 1, 1, 0), ("wp", 0, 1, 1),
-    ("wp", 1, 1, 0), ("wp", 1, 1, 1), ("ag_sent",), ("w_sent", 0, 0), ("w_sent", 1, 0), ("wd", 0, 1, 0), ("zl", 0),
-    ("wd", 0, 1, 1), ("zl", 1), ("wd", 1, 1, 0), ("wd", 1, 1, 1), ("z_sent", 0), ("z_sent", 1), ("w_sent", 0, 1),
-    ("w_sent", 1, 1),
+    ("ag0", 0, 0), ("ag0", 0, 1), ("turn",), ("own", 1), ("ag0", 1, 0), ("ag0", 1, 1), ("agw", 0, 0, 0),
+    ("agf", 0, 0, 0), ("agw", 0, 0, 1), ("agf", 0, 0, 1), ("agw", 1, 0, 0), ("agf", 1, 0, 0), ("agw", 1, 0, 1),
+    ("own", 0), ("agw", 0, 1, 0), ("agf", 0, 1, 0), ("tabl",), ("agf", 1, 0, 1), ("agw", 1, 1, 0), ("agf", 1, 1, 0),
+    ("ags", 1, 0), ("ags", 0, 0), ("agw", 0, 1, 1), ("agf", 0, 1, 1), ("agw", 0, 2, 0), ("agf", 0, 2, 0),
+    ("agw", 1, 1, 1), ("agf", 1, 1, 1), ("agw", 1, 2, 0), ("agf", 1, 2, 0), ("ags", 1, 1), ("agw", 0, 2, 1),
+    ("ags", 0, 2), ("ags", 0, 1), ("agw", 0, 3, 0), ("ags", 0, 3), ("agw", 1, 2, 1), ("ags", 1, 2), ("agw", 1, 3, 0),
+    ("ags", 1, 3), ("gath", 0), ("H", 0, 4), ("H", 4, 7), ("S", 0), ("tab",), ("P", 0), ("gath", 1), ("GO", 0),
+    ("wm", 0, 0, 0, 0), ("GH",), ("wm", 0, 0, 0, 2), ("zf", 0), ("GI", 0), ("wm", 1, 0, 0, 0), ("S", 1), ("P", 1),
+    ("zg", 0), ("zn", 0, 3, 0), ("wp", 0, 0, 0), ("zf", 1), ("wm", 1, 0, 0, 2), ("zg", 1), ("zn", 0, 2, 1),
+    ("wp", 1, 0, 0), ("zn", 0, 2, 0), ("zn", 1, 3, 0), ("zn", 1, 2, 1), ("wd", 0, 0, 0), ("wm", 0, 1, 0, 0),
+    ("zn", 0, 1, 1), ("zn", 1, 2, 0), ("wd", 1, 0, 0), ("wm", 1, 1, 0, 0), ("zn", 1, 1, 1), ("zn", 0, 1, 0),
+    ("wm", 1, 1, 0, 2), ("wp", 0, 1, 0), ("wm", 0, 1, 0, 2), ("zn", 1, 1, 0), ("wp", 1, 1, 0), ("ag_sent",),
+    ("w_sent", 0, 0), ("w_sent", 1, 0), ("wd", 0, 1, 0), ("zl", 0), ("zl", 1), ("wd", 1, 1, 0), ("z_sent", 0),
+    ("z_sent", 1), ("w_sent", 0, 1), ("w_sent", 1, 1),
 )
 
 
@@ -166,17 +163,10 @@
     def wrap(step):
         return zat[step % NZ]
 
-    def ag_copy(a, way, k, h):
-        step = -(k + 1) if way == 0 else k + 1
-        v = piece(fields[a], 0, step, *SPAN[h])
-        i = ((a * 2 + way) * 4 + k) * 2 + h
-        return rcopy(v, v, ag_s.at[a], ag_r.at[i], zdev(1 if way == 0 else -1))
-
     def ag_send(a, way, k, h):
-        step = -k if way == 0 else k
-        v = piece(fields[a], 0, step, *SPAN[h])
-        i = ((a * 2 + way) * 4 + k) * 2 + h
+        v = piece(fields[a], 0, -k if way == 0 else k, *SPAN[h])
         src = (x_hbm, g_hbm)[a].at[pl.ds(*SPAN[h])] if k == 0 else v
+        i = (a * 4 + k) * 2 + (0 if h == way else 1)
         return rcopy(src, v, ag_s.at[a], ag_r.at[i], zdev(1 if way == 0 else -1))
 
     def sb_place(j):
@@ -201,8 +191,7 @@
             go(ag_send(a, way, 0, part_of(way, i)))
 
     def ag_wait(a, k, i):
-        for way in range(2):
-            ag_copy(a, way, k, part_of(way, i)).wait_recv()
+        landed(fields[a].at[pl.ds(0, U)], ag_r.at[(a * 4 + k) * 2 + i])
 
     def ag_pass(a, k, i):
         for way in range(2):
@@ -498,11 +487,11 @@
             pltpu.SMEM((ROWS, SLOTS), jnp.int32),
             pltpu.SMEM((ROWS,), jnp.int32),
             dma((7,)),
-            dma((2,)), dma((32,)),
+            dma((2,)), dma((16,)),
             dma((2,)), dma((2,)),
             dma((2,)), dma((4,)),
             dma((2,)), dma((16,)),
-            dma((8,)), dma((16,)),
+            dma((4,)), dma((8,)),
         ],
         compiler_params=pltpu.CompilerParams(
             collective_id=0, has_side_effects=True, vmem_limit_bytes=63 * 1024 * 1024

time: 59.5 us -> 59.2 us (level)
  no operation moved by 1% of the time
where the time goes in v11:
time: 59.2 us; the launch traced here: 58.8 us
  Pallas kernels  58.2 us (98%)
  between operations  0.64 us (1%)
    pallas_call x1, Pallas kernels, on_device(): pl.pallas_call(kernel, out_shape=shapes, in_specs=[hbm] * 6, out_specs=(v...  56.2 us
    pallas_call x1, Pallas kernels, on_device(): pl.pallas_call(finish, out_shape=shapes, in_specs=[vm] * 4, out_specs=(vm...  2.01 us

profile of v11, /device:TPU:32, one launch (start us, length us, event | category | flops | bytes accessed | tf_op | source)
XLA Modules:
  0.0 58.8 jit_solution(2819672894512523959)
XLA Ops:
  0.6 56.2 %shard_map.93 = (bf16[448,128]{1,0:T(8,128)(2,1)}, bf16[448,128]{1,0:T(8,128)(2,1)}, f32[448,128]{1,0:T(8,128)}, f32[448,128]{1,0:T(8,128)}) custom-call(s32[7,8]{1,0:T(8,128)} %col_hbm.1, s32[7]{0:T(128)} %cnt_hbm.1, bf16[7,64,128]{2,1,0:T(8,128)(2,1)} %bitcast.16, bf16[7,64,128]{2,1,0:T(8,128)(2,1)} %bitcast.17, bf16[56,128,128]{2,1,0:T(8,128)(2,1)} %bitcast.12, ...), custom_call_target="tpu_custom_call" | custom-call | flops 1409286144 | bytes 8000000 | tf_op jit(solution)/shard_map/pallas_call | solution.py:461
  56.8 2.0 %shard_map.94 = (bf16[448,128]{1,0:T(8,128)(2,1)}, bf16[448,128]{1,0:T(8,128)(2,1)}, f32[448,128]{1,0:T(8,128)}, f32[448,128]{1,0:T(8,128)}) custom-call(bf16[448,128]{1,0:T(8,128)(2,1)} %get-tuple-element.12.refs_0_, bf16[448,128]{1,0:T(8,128)(2,1)} %get-tuple-element.13.refs_1_, f32[448,128]{1,0:T(8,128)} %get-tuple-element.14.refs_2_, ...), custom_call_target="tpu_custom_call" | custom-call | bytes 1400000 | tf_op jit(solution)/shard_map/pallas_call | solution.py:505

commit v12 on v11

--- a/solution.py
+++ b/solution.py
@@ -33,7 +33,7 @@
     ("ags", 1, 0), ("ags", 0, 0), ("agw", 0, 1, 1), ("agf", 0, 1, 1), ("agw", 0, 2, 0), ("agf", 0, 2, 0),
     ("agw", 1, 1, 1), ("agf", 1, 1, 1), ("agw", 1, 2, 0), ("agf", 1, 2, 0), ("ags", 1, 1), ("agw", 0, 2, 1),
     ("ags", 0, 2), ("ags", 0, 1), ("agw", 0, 3, 0), ("ags", 0, 3), ("agw", 1, 2, 1), ("ags", 1, 2), ("agw", 1, 3, 0),
-    ("ags", 1, 3), ("gath", 0), ("H", 0, 4), ("H", 4, 7), ("S", 0), ("tab",), ("P", 0), ("gath", 1), ("GO", 0),
+    ("ags", 1, 3), ("gath", 0), ("H", 0, 7), ("S", 0), ("tab",), ("P", 0), ("gath", 1), ("GO", 0),
     ("wm", 0, 0, 0, 0), ("GH",), ("wm", 0, 0, 0, 2), ("zf", 0), ("GI", 0), ("wm", 1, 0, 0, 0), ("S", 1), ("P", 1),
     ("zg", 0), ("zn", 0, 3, 0), ("wp", 0, 0, 0), ("zf", 1), ("wm", 1, 0, 0, 2), ("zg", 1), ("zn", 0, 2, 1),
     ("wp", 1, 0, 0), ("zn", 0, 2, 0), ("zn", 1, 3, 0), ("zn", 1, 2, 1), ("wd", 0, 0, 0), ("wm", 0, 1, 0, 0),
@@ -253,7 +253,7 @@
             run[r] = acc.astype(BF)
             return acc
 
-        lax.fori_loop(0, NB, add, jnp.zeros((BLK, BLK), F32), unroll=4)
+        lax.fori_loop(0, NB, add, jnp.zeros((BLK, BLK), F32), unroll=14)
         for j, step in enumerate(ORDER):
             zz = wrap(step)
             for k in range(7):

time: 59.2 us -> 59.1 us (level)
  no operation moved by 1% of the time
where the time goes in v12:
time: 59.1 us; the launch traced here: 58.7 us
  Pallas kernels  58.1 us (98%)
  between operations  0.64 us (1%)
    pallas_call x1, Pallas kernels, on_device(): pl.pallas_call(kernel, out_shape=shapes, in_specs=[hbm] * 6, out_specs=(v...  56.1 us
    pallas_call x1, Pallas kernels, on_device(): pl.pallas_call(finish, out_shape=shapes, in_specs=[vm] * 4, out_specs=(vm...  2.01 us

profile of v12, /device:TPU:32, one launch (start us, length us, event | category | flops | bytes accessed | tf_op | source)
XLA Modules:
  0.0 58.7 jit_solution(11535840411042825966)
XLA Ops:
  0.6 56.1 %shard_map.93 = (bf16[448,128]{1,0:T(8,128)(2,1)}, bf16[448,128]{1,0:T(8,128)(2,1)}, f32[448,128]{1,0:T(8,128)}, f32[448,128]{1,0:T(8,128)}) custom-call(s32[7,8]{1,0:T(8,128)} %col_hbm.1, s32[7]{0:T(128)} %cnt_hbm.1, bf16[7,64,128]{2,1,0:T(8,128)(2,1)} %bitcast.16, bf16[7,64,128]{2,1,0:T(8,128)(2,1)} %bitcast.17, bf16[56,128,128]{2,1,0:T(8,128)(2,1)} %bitcast.12, ...), custom_call_target="tpu_custom_call" | custom-call | flops 1409286144 | bytes 8000000 | tf_op jit(solution)/shard_map/pallas_call | solution.py:461
  56.7 2.0 %shard_map.94 = (bf16[448,128]{1,0:T(8,128)(2,1)}, bf16[448,128]{1,0:T(8,128)(2,1)}, f32[448,128]{1,0:T(8,128)}, f32[448,128]{1,0:T(8,128)}) custom-call(bf16[448,128]{1,0:T(8,128)(2,1)} %get-tuple-element.12.refs_0_, bf16[448,128]{1,0:T(8,128)(2,1)} %get-tuple-element.13.refs_1_, f32[448,128]{1,0:T(8,128)} %get-tuple-element.14.refs_2_, ...), custom_call_target="tpu_custom_call" | custom-call | bytes 1400000 | tf_op jit(solution)/shard_map/pallas_call | solution.py:505
